TPU v7x, 32 devices: a whole 2x2x4 slice. The times are simulated.
32 devices in a mesh: dp: 8 (over y, x, core), tensor: 4 (over z).
Axes of the slice: x: 2, y: 2, z: 4, core: 2. Of those that a mesh axis runs over, the one named last changes fastest.
Arguments:
- tokens: bfloat16 [24576, 1024], P(('dp', 'tensor')), may hold values from -6 to 6
- cotangent: bfloat16 [24576, 1024], P(('dp', 'tensor')), may hold values from -6 to 6
- item_len: int32 [8, 2], P('dp'), may hold values from 0 to 3072, as said below
- bucket_table: int32 [3072], replicated, may hold values from 0 to 31, as said below
- w_qkv: float32 [3, 1024, 1024], P(None, 'dp', 'tensor'), may hold values from -0.1875 to 0.1875
- w_proj: float32 [1024, 1024], P('tensor', 'dp'), may hold values from -2 to 2
- w_up: float32 [1024, 4096], P('dp', 'tensor'), may hold values from -0.1875 to 0.1875
- w_down: float32 [4096, 1024], P('tensor', 'dp'), may hold values from -0.09375 to 0.09375
- rel_bias: float32 [512], P(('dp', 'tensor')), may hold values from -4 to 4
- ln_gain: float32 [2, 1024], P(None, ('dp', 'tensor')), may hold values from 0.25 to 1.75
- ln_shift: float32 [2, 1024], P(None, ('dp', 'tensor')), may hold values from -2 to 2
- mean_qkv: float32 [3, 1024, 1024], P(None, 'dp', 'tensor'), may hold values from -0.002 to 0.002
- mean_proj: float32 [1024, 1024], P('tensor', 'dp'), may hold values from -0.002 to 0.002
- mean_up: float32 [1024, 4096], P('dp', 'tensor'), may hold values from -0.002 to 0.002
- mean_down: float32 [4096, 1024], P('tensor', 'dp'), may hold values from -0.002 to 0.002
- mean_bias: float32 [512], P(('dp', 'tensor')), may hold values from -0.002 to 0.002
- mean_gain: float32 [2, 1024], P(None, ('dp', 'tensor')), may hold values from -0.002 to 0.002
- mean_shift: float32 [2, 1024], P(None, ('dp', 'tensor')), may hold values from -0.002 to 0.002
- square_qkv: float32 [3, 1024, 1024], P(None, 'dp', 'tensor'), may hold values from 1e-08 to 1e-06
- square_proj: float32 [1024, 1024], P('tensor', 'dp'), may hold values from 5e-10 to 5e-08
- square_up: float32 [1024, 4096], P('dp', 'tensor'), may hold values from 5e-10 to 5e-08
- square_down: float32 [4096, 1024], P('tensor', 'dp'), may hold values from 1e-08 to 1e-06
- square_bias: float32 [512], P(('dp', 'tensor')), may hold values from 1e-08 to 1e-06
- square_gain: float32 [2, 1024], P(None, ('dp', 'tensor')), may hold values from 1e-08 to 1e-06
- square_shift: float32 [2, 1024], P(None, ('dp', 'tensor')), may hold values from 1e-08 to 1e-06
Outputs:
- block_out: bfloat16 [24576, 1024], P(('dp', 'tensor'))
- grad_tokens: bfloat16 [24576, 1024], P(('dp', 'tensor'))
- grad_norm: float32 [], replicated
- param_norms: float32 [2, 11], replicated
- new_w_qkv: float32 [3, 1024, 1024], P(None, 'dp', 'tensor')
- new_w_proj: float32 [1024, 1024], P('tensor', 'dp')
- new_w_up: float32 [1024, 4096], P('dp', 'tensor')
- new_w_down: float32 [4096, 1024], P('tensor', 'dp')
- new_rel_bias: float32 [512], P(('dp', 'tensor'))
- new_ln_gain: float32 [2, 1024], P(None, ('dp', 'tensor'))
- new_ln_shift: float32 [2, 1024], P(None, ('dp', 'tensor'))
- new_mean_qkv: float32 [3, 1024, 1024], P(None, 'dp', 'tensor')
- new_mean_proj: float32 [1024, 1024], P('tensor', 'dp')
- new_mean_up: float32 [1024, 4096], P('dp', 'tensor')
- new_mean_down: float32 [4096, 1024], P('tensor', 'dp')
- new_mean_bias: float32 [512], P(('dp', 'tensor'))
- new_mean_gain: float32 [2, 1024], P(None, ('dp', 'tensor'))
- new_mean_shift: float32 [2, 1024], P(None, ('dp', 'tensor'))
- new_square_qkv: float32 [3, 1024, 1024], P(None, 'dp', 'tensor')
- new_square_proj: float32 [1024, 1024], P('tensor', 'dp')
- new_square_up: float32 [1024, 4096], P('dp', 'tensor')
- new_square_down: float32 [4096, 1024], P('tensor', 'dp')
- new_square_bias: float32 [512], P(('dp', 'tensor'))
- new_square_gain: float32 [2, 1024], P(None, ('dp', 'tensor'))
- new_square_shift: float32 [2, 1024], P(None, ('dp', 'tensor'))
Inputs may be any that keep to these rules, and one draw needn't show every extreme that they name: `item_len`: row g holds the lengths of the items packed in group g: either one item of 3072 tokens and an empty second, or two items of 1536 tokens; every draw has groups of both kinds. `bucket_table`: entry d is the bucket of distance d: d itself for d < 16, non-decreasing in d, reaching 31.
All inputs are finite; a program needn't handle non-finite values.
Results may differ from a plain program's by a relative error of at most 0.018.
Values may be sent and summed in bfloat16 or wider, within the bound.
A program may use at most 512 MiB of HBM per device.

v0:
```python
import jax
import jax.numpy as jnp
import numpy as np
from jax import lax
from jax.sharding import PartitionSpec as P

H = 16
DH = 64
BUCKETS = 32


HIGHEST = lax.Precision.HIGHEST


def layer_norm(values, gain, shift):
    center = values - jnp.mean(values, axis=-1, keepdims=True)
    spread = jnp.mean(center * center, axis=-1, keepdims=True)
    return center * lax.rsqrt(spread + 1e-05) * gain + shift


def gelu_exact(values):
    return jax.nn.gelu(values, approximate=False)


def contract_rows(left, right):
    return lax.dot_general(
        left, right, (((0,), (0,)), ((), ())), preferred_element_type=jnp.float32
    )


def contract_cols(left, right):
    return lax.dot_general(
        left, right, (((1,), (1,)), ((), ())), preferred_element_type=jnp.float32
    )


def toeplitz_bias(dist_bias, start, rows, width):
    heads_here, limit = dist_bias.shape
    period = rows + width
    offsets = np.arange(period)
    offsets = np.where(offsets < width, offsets, offsets - period)
    lookup = np.clip(start - offsets, 0, limit - 1).astype(np.int32)
    pattern = dist_bias[:, lookup]
    tiled = jnp.tile(pattern, (1, rows))[:, : rows * (period - 1)]
    return tiled.reshape(heads_here, rows, period - 1)[:, :, :width]


def block_scores(queries, keys, dist_bias, start, split):
    rows = queries.shape[0]
    width = keys.shape[0]
    head_dim = queries.shape[2]
    product = jnp.einsum(
        "rhd,khd->hrk", queries, keys, preferred_element_type=jnp.float32
    ) * head_dim ** (-0.5)
    query_pos = start + jnp.arange(rows)
    key_pos = jnp.arange(width)
    distance = query_pos[:, None] - key_pos[None, :]
    position_bias = toeplitz_bias(dist_bias, start, rows, width)
    same_item = (query_pos[:, None] >= split) == (key_pos[None, :] >= split)
    return jnp.where((distance >= 0) & same_item, product + position_bias, -jnp.inf)


def diagonal_sums(block):
    heads_here, rows, width = block.shape
    flipped = block[:, :, ::-1]
    padded = jnp.pad(flipped, ((0, 0), (0, 0), (0, rows)))
    full_width = width + rows
    flat = padded.reshape(heads_here, rows * full_width)[:, : rows * (full_width - 1)]
    skewed = flat.reshape(heads_here, rows, full_width - 1)
    totals = jnp.sum(skewed, axis=1)
    return totals[:, rows - 1 : rows - 1 + width]


def attend(queries, keys, values, dist_bias, split):
    tokens_here = queries.shape[0]
    rows = min(512, tokens_here)
    outputs = []
    maxima = []
    totals = []
    for block in range(tokens_here // rows):
        start = block * rows
        stop = start + rows
        scores = block_scores(queries[start:stop], keys[:stop], dist_bias, start, split)
        row_max = jnp.max(scores, axis=-1, keepdims=True)
        weights = jnp.exp(scores - row_max)
        row_total = jnp.sum(weights, axis=-1, keepdims=True)
        shares = (weights / row_total).astype(jnp.bfloat16)
        outputs.append(
            jnp.einsum("hrk,khd->rhd", shares, values[:stop], preferred_element_type=jnp.float32)
        )
        maxima.append(row_max)
        totals.append(row_total)
    return (jnp.concatenate(outputs, axis=0), maxima, totals)


def attend_back(queries, keys, values, grad_out, dist_bias, split, maxima, totals):
    tokens_here, heads_here, head_dim = queries.shape
    rows = min(512, tokens_here)
    scale = head_dim ** (-0.5)
    grad_query_list = []
    grad_keys = jnp.zeros(keys.shape, jnp.float32)
    grad_values = jnp.zeros(values.shape, jnp.float32)
    grad_dist = jnp.zeros((heads_here, tokens_here), jnp.float32)
    for block in range(tokens_here // rows):
        start = block * rows
        stop = start + rows
        scores = block_scores(queries[start:stop], keys[:stop], dist_bias, start, split)
        shares = jnp.exp(scores - maxima[block]) / totals[block]
        grad_shares = jnp.einsum(
            "rhd,khd->hrk", grad_out[start:stop], values[:stop], preferred_element_type=jnp.float32
        )
        inner_sum = jnp.sum(shares * grad_shares, axis=-1, keepdims=True)
        grad_scores = (shares * (grad_shares - inner_sum)).astype(jnp.bfloat16)
        grad_query_list.append(
            jnp.einsum("hrk,khd->rhd", grad_scores, keys[:stop], preferred_element_type=jnp.float32)
            * scale
        )
        grad_keys = grad_keys.at[:stop].add(
            jnp.einsum(
                "hrk,rhd->khd", grad_scores, queries[start:stop], preferred_element_type=jnp.float32
            )
            * scale
        )
        grad_values = grad_values.at[:stop].add(
            jnp.einsum(
                "hrk,rhd->khd",
                shares.astype(jnp.bfloat16),
                grad_out[start:stop],
                preferred_element_type=jnp.float32,
            )
        )
        grad_dist = grad_dist.at[:, :stop].add(diagonal_sums(grad_scores.astype(jnp.float32)))
    return (jnp.concatenate(grad_query_list, axis=0), grad_keys, grad_values, grad_dist)


def param_squares(arrays):
    qkv, proj, up, down, table, gain, shift = arrays
    parts = [
        jnp.sum(qkv * qkv, axis=(1, 2)),
        jnp.stack(
            [jnp.sum(proj * proj), jnp.sum(up * up), jnp.sum(down * down), jnp.sum(table * table)]
        ),
        jnp.sum(gain * gain, axis=1),
        jnp.sum(shift * shift, axis=1),
    ]
    return jnp.concatenate(parts)


def expand(values):
    return (
        values[0:3][:, None, None],
        values[3],
        values[4],
        values[5],
        values[6],
        values[7:9][:, None],
        values[9:11][:, None],
    )


def global_sums(values):
    return lax.psum(values, ("dp", "tensor"))


def per_device(
    tokens,
    cotangent,
    item_len,
    bucket_table,
    w_qkv,
    w_proj,
    w_up,
    w_down,
    rel_bias,
    ln_gain,
    ln_shift,
    mean_qkv,
    mean_proj,
    mean_up,
    mean_down,
    mean_bias,
    mean_gain,
    mean_shift,
    square_qkv,
    square_proj,
    square_up,
    square_down,
    square_bias,
    square_gain,
    square_shift,
):
    heads_local = w_qkv.shape[2] // DH
    head_start = lax.axis_index("tensor") * heads_local
    table_flat, gains, shifts = (
        lax.all_gather(rel_bias, ("dp", "tensor"), axis=0, tiled=True),
        lax.all_gather(ln_gain, ("dp", "tensor"), axis=1, tiled=True),
        lax.all_gather(ln_shift, ("dp", "tensor"), axis=1, tiled=True),
    )
    qkv_full, proj_full, up_full, down_full = (
        lax.all_gather(w_qkv.astype(jnp.bfloat16), "dp", axis=1, tiled=True),
        lax.all_gather(w_proj.astype(jnp.bfloat16), "dp", axis=1, tiled=True),
        lax.all_gather(w_up.astype(jnp.bfloat16), "dp", axis=0, tiled=True),
        lax.all_gather(w_down.astype(jnp.bfloat16), "dp", axis=1, tiled=True),
    )
    x_rows = tokens.astype(jnp.float32)
    first_norm = layer_norm(x_rows, gains[0], shifts[0])
    a_first, grad_all = (
        lax.all_gather(first_norm.astype(jnp.bfloat16), "tensor", axis=0, tiled=True),
        lax.all_gather(cotangent, "tensor", axis=0, tiled=True),
    )
    tok = a_first.shape[0]
    qkv = jnp.einsum("td,cde->cte", a_first, qkv_full, preferred_element_type=jnp.float32).astype(
        jnp.bfloat16
    )
    queries = qkv[0].reshape(tok, heads_local, DH)
    keys = qkv[1].reshape(tok, heads_local, DH)
    values = qkv[2].reshape(tok, heads_local, DH)
    whole_table = table_flat.reshape(BUCKETS, H)
    local_table = lax.dynamic_slice_in_dim(whole_table, head_start, heads_local, 1)
    one_hot = (bucket_table[:, None] == jnp.arange(BUCKETS)[None, :]).astype(jnp.float32)
    dist_bias = jnp.dot(
        one_hot, local_table, precision=HIGHEST, preferred_element_type=jnp.float32
    ).T
    split = item_len[0, 0]
    attended, maxima, totals = attend(queries, keys, values, dist_bias, split)
    attn_out = attended.reshape(tok, heads_local * DH).astype(jnp.bfloat16)
    attn_rows = lax.psum_scatter(
        jnp.dot(attn_out, proj_full, preferred_element_type=jnp.float32),
        "tensor",
        scatter_dimension=0,
        tiled=True,
    )
    middle = x_rows + attn_rows
    second_norm = layer_norm(middle, gains[1], shifts[1])
    a_second = lax.all_gather(second_norm.astype(jnp.bfloat16), "tensor", axis=0, tiled=True)
    hidden_pre = jnp.dot(a_second, up_full, preferred_element_type=jnp.float32)
    hidden = gelu_exact(hidden_pre).astype(jnp.bfloat16)
    ffn_rows = lax.psum_scatter(
        jnp.dot(hidden, down_full, preferred_element_type=jnp.float32).astype(jnp.bfloat16),
        "tensor",
        scatter_dimension=0,
        tiled=True,
    ).astype(jnp.float32)
    block_out = (middle + ffn_rows).astype(jnp.bfloat16)
    _, gelu_back = jax.vjp(gelu_exact, hidden_pre)
    grad_down = contract_rows(hidden, grad_all)
    grad_hidden = contract_cols(grad_all, down_full)
    grad_pre = gelu_back(grad_hidden)[0].astype(jnp.bfloat16)
    grad_up = contract_rows(a_second, grad_pre)
    grad_second = lax.psum_scatter(
        contract_cols(grad_pre, up_full), "tensor", scatter_dimension=0, tiled=True
    )
    _, second_back = jax.vjp(layer_norm, middle, gains[1], shifts[1])
    middle_part, gain_two, shift_two = second_back(grad_second)
    grad_middle = cotangent.astype(jnp.float32) + middle_part
    grad_mid_all = lax.all_gather(grad_middle.astype(jnp.bfloat16), "tensor", axis=0, tiled=True)
    grad_proj = contract_rows(attn_out, grad_mid_all)
    grad_attn = (
        contract_cols(grad_mid_all, proj_full).astype(jnp.bfloat16).reshape(tok, heads_local, DH)
    )
    grad_queries, grad_keys, grad_values, grad_dist = attend_back(
        queries, keys, values, grad_attn, dist_bias, split, maxima, totals
    )
    grad_qkv_low = jnp.stack(
        [grad_queries.reshape(tok, -1), grad_keys.reshape(tok, -1), grad_values.reshape(tok, -1)]
    ).astype(jnp.bfloat16)
    grad_qkv = jnp.einsum("td,cte->cde", a_first, grad_qkv_low, preferred_element_type=jnp.float32)
    grad_first = lax.psum_scatter(
        jnp.einsum(
            "cte,cde->td", grad_qkv_low, qkv_full, preferred_element_type=jnp.float32
        ).astype(jnp.bfloat16),
        "tensor",
        scatter_dimension=0,
        tiled=True,
    ).astype(jnp.float32)
    _, first_back = jax.vjp(layer_norm, x_rows, gains[0], shifts[0])
    input_part, gain_one, shift_one = first_back(grad_first)
    grad_tokens = (grad_middle + input_part).astype(jnp.bfloat16)
    local_bias_grad = jnp.dot(
        one_hot.T, grad_dist.T, precision=HIGHEST, preferred_element_type=jnp.float32
    )
    table_grad = lax.dynamic_update_slice(
        jnp.zeros((BUCKETS, H), jnp.float32), local_bias_grad, (0, head_start)
    ).reshape(-1)
    sum_table, sum_gain, sum_shift = (
        lax.psum_scatter(table_grad, ("dp", "tensor"), scatter_dimension=0, tiled=True),
        lax.psum_scatter(
            jnp.stack([gain_one, gain_two]), ("dp", "tensor"), scatter_dimension=1, tiled=True
        ),
        lax.psum_scatter(
            jnp.stack([shift_one, shift_two]), ("dp", "tensor"), scatter_dimension=1, tiled=True
        ),
    )
    sum_qkv, sum_proj, sum_up, sum_down = (
        lax.psum_scatter(
            grad_qkv.astype(jnp.bfloat16), "dp", scatter_dimension=1, tiled=True
        ).astype(jnp.float32),
        lax.psum_scatter(
            grad_proj.astype(jnp.bfloat16), "dp", scatter_dimension=1, tiled=True
        ).astype(jnp.float32),
        lax.psum_scatter(
            grad_up.astype(jnp.bfloat16), "dp", scatter_dimension=0, tiled=True
        ).astype(jnp.float32),
        lax.psum_scatter(
            grad_down.astype(jnp.bfloat16), "dp", scatter_dimension=1, tiled=True
        ).astype(jnp.float32),
    )
    params = (w_qkv, w_proj, w_up, w_down, rel_bias, ln_gain, ln_shift)
    grads = (sum_qkv, sum_proj, sum_up, sum_down, sum_table, sum_gain, sum_shift)
    means = (mean_qkv, mean_proj, mean_up, mean_down, mean_bias, mean_gain, mean_shift)
    squares = (
        square_qkv,
        square_proj,
        square_up,
        square_down,
        square_bias,
        square_gain,
        square_shift,
    )
    first_sums = global_sums(jnp.concatenate([param_squares(grads), param_squares(params)]))
    sq_grad = first_sums[:11]
    sq_weight = first_sums[11:]
    grad_norm = jnp.sqrt(jnp.sum(sq_grad))
    clip = jnp.minimum(1.0, 1.0 / grad_norm)
    new_means = [0.5 * m + 0.5 * (clip * g) for m, g in zip(means, grads)]
    new_squares = [0.5 * s + 0.5 * (clip * g) * (clip * g) for s, g in zip(squares, grads)]
    updates = [
        nm / (jnp.sqrt(ns) + 1e-06) + 0.01 * w for nm, ns, w in zip(new_means, new_squares, params)
    ]
    sq_update = global_sums(param_squares(updates))
    trust = jnp.sqrt(sq_weight) / jnp.sqrt(sq_update)
    factors = expand(trust)
    new_weights = [w - 0.3 * f * u for w, f, u in zip(params, factors, updates)]
    param_norms = jnp.stack([jnp.sqrt(sq_weight), jnp.sqrt(sq_update)])
    return (
        block_out,
        grad_tokens,
        grad_norm,
        param_norms,
        new_weights[0],
        new_weights[1],
        new_weights[2],
        new_weights[3],
        new_weights[4],
        new_weights[5],
        new_weights[6],
        new_means[0],
        new_means[1],
        new_means[2],
        new_means[3],
        new_means[4],
        new_means[5],
        new_means[6],
        new_squares[0],
        new_squares[1],
        new_squares[2],
        new_squares[3],
        new_squares[4],
        new_squares[5],
        new_squares[6],
    )


def solution(mesh):
    placed = (
        P(("dp", "tensor"), None),
        P(("dp", "tensor"), None),
        P("dp", None),
        P(),
        P(None, "dp", "tensor"),
        P("tensor", "dp"),
        P("dp", "tensor"),
        P("tensor", "dp"),
        P(("dp", "tensor")),
        P(None, ("dp", "tensor")),
        P(None, ("dp", "tensor")),
        P(None, "dp", "tensor"),
        P("tensor", "dp"),
        P("dp", "tensor"),
        P("tensor", "dp"),
        P(("dp", "tensor")),
        P(None, ("dp", "tensor")),
        P(None, ("dp", "tensor")),
        P(None, "dp", "tensor"),
        P("tensor", "dp"),
        P("dp", "tensor"),
        P("tensor", "dp"),
        P(("dp", "tensor")),
        P(None, ("dp", "tensor")),
        P(None, ("dp", "tensor")),
    )
    return jax.shard_map(
        per_device,
        mesh=mesh,
        in_specs=placed,
        out_specs=(
            P(("dp", "tensor"), None),
            P(("dp", "tensor"), None),
            P(),
            P(),
            P(None, "dp", "tensor"),
            P("tensor", "dp"),
            P("dp", "tensor"),
            P("tensor", "dp"),
            P(("dp", "tensor")),
            P(None, ("dp", "tensor")),
            P(None, ("dp", "tensor")),
            P(None, "dp", "tensor"),
            P("tensor", "dp"),
            P("dp", "tensor"),
            P("tensor", "dp"),
            P(("dp", "tensor")),
            P(None, ("dp", "tensor")),
            P(None, ("dp", "tensor")),
            P(None, "dp", "tensor"),
            P("tensor", "dp"),
            P("dp", "tensor"),
            P("tensor", "dp"),
            P(("dp", "tensor")),
            P(None, ("dp", "tensor")),
            P(None, ("dp", "tensor")),
        ),
        check_vma=False,
    )
```

profile of v0, /device:TPU:8, one launch (start us, length us, event | category | flops | bytes accessed | tf_op | source)
XLA Modules:
  0.0 4431.5 jit_solution(1531905288498183312)
XLA Ops:
  9.3 64.2 %all-gather.1 = f32[32,32,2]{1,2,0:T(2,128)S(1)} all-gather(f32[1,32,2]{1,2,0:T(2,128)} %bitcast.461), channel_id=1, replica_groups=mesh['dp'=8,'tensor'=4] {'dp','tensor'}, dimensions={0}, use_global_device_ids=true | all-gather | bytes 8448 | tf_op jit(solution)/shard_map/all_gather | solution.py:197
  73.6 68.8 %all-gather = f32[32,32,2]{1,2,0:T(2,128)S(1)} all-gather(f32[1,32,2]{1,2,0:T(2,128)} %bitcast.462), channel_id=1, replica_groups=mesh['dp'=8,'tensor'=4] {'dp','tensor'}, dimensions={0}, use_global_device_ids=true | all-gather | bytes 8448 | tf_op jit(solution)/shard_map/all_gather | solution.py:196
  151.7 43.8 all-reduce.10
  374.1 47.1 %reshape.964 = f32[4192256]{0:T(1024)} reshape(f32[4,1048064]{1,0:T(4,128)} %slice.853) | data formatting | bytes 33538048
  421.2 24.6 reshape.869
  455.4 23.4 copy.228
  487.1 58.6 %reshape.966 = f32[5240832]{0:T(1024)} reshape(f32[4,1310208]{1,0:T(4,128)} %slice.858) | data formatting | bytes 41926656
  545.7 29.7 reshape.870
  587.0 27.8 copy.229
  624.5 70.6 %reshape.968 = f32[6289408]{0:T(1024)} reshape(f32[4,1572352]{1,0:T(4,128)} %slice.863) | data formatting | bytes 50315264
  695.1 34.5 reshape.871
  742.9 33.6 copy.230
  797.0 82.3 %reshape.970 = f32[7337984]{0:T(1024)} reshape(f32[4,1834496]{1,0:T(4,128)} %slice.868) | data formatting | bytes 58703872
  879.3 39.5 reshape.872
  1053.8 23.7 fusion.250
  1093.6 27.9 fusion.251
  1206.9 210.0 %reduce-scatter.21.cloned.1.call-done = f32[768,1024]{1,0:T(8,128)} async-done(((f32[3072,1024]{1,0:T(8,128)}), f32[768,1024]{1,0:T(8,128)}) %reduce-scatter.21.cloned.1.call-update) | async-done | bytes 3145744 | tf_op jit(solution)/shard_map/reduce_scatter | solution.py:227
  1424.9 23.2 all-gather.16.cloned.1.call-done
  1448.2 114.4 %all-gather.14.cloned.1.call-done = bf16[3072,1024]{1,0:T(8,128)(2,1)} async-done(((bf16[768,1024]{1,0:T(8,128)(2,1)}), bf16[3072,1024]{1,0:T(8,128)(2,1)}) %all-gather.14.cloned.1.call-update) | async-done | bytes 6291472 | tf_op jit(solution)/shard_map/all_gather | solution.py:235
  1594.3 114.0 %all-gather.20.cloned.1.call-done = bf16[3072,1024]{1,0:T(8,128)(2,1)} async-done(((bf16[768,1024]{1,0:T(8,128)(2,1)}), bf16[3072,1024]{1,0:T(8,128)(2,1)}) %all-gather.20.cloned.1.call-update) | async-done | bytes 6291472 | tf_op jit(solution)/shard_map/all_gather | solution.py:209
  1708.3 38.7 add_convert_fusion
  1781.2 190.9 %reduce-scatter.25.cloned.1.call-done = f32[768,1024]{1,0:T(8,128)} async-done(((f32[3072,1024]{1,0:T(8,128)}), f32[768,1024]{1,0:T(8,128)}) %reduce-scatter.25.cloned.1.call-update) | async-done | bytes 3145744 | tf_op jit(solution)/shard_map/reduce_scatter | solution.py:250
  1975.6 110.6 %reduce-scatter.23.cloned.1.call-done = bf16[768,1024]{1,0:T(8,128)(2,1)} async-done(((bf16[3072,1024]{1,0:T(8,128)(2,1)}), bf16[768,1024]{1,0:T(8,128)(2,1)}) %reduce-scatter.23.cloned.1.call-update) | async-done | bytes 1572880 | tf_op jit(solution)/shard_map/reduce_scatter | solution.py:238
  2119.4 87.4 %all-gather.22.cloned.1.call-done = bf16[3072,1024]{1,0:T(8,128)(2,1)} async-done(((bf16[768,1024]{1,0:T(8,128)(2,1)}), bf16[3072,1024]{1,0:T(8,128)(2,1)}) %all-gather.22.cloned.1.call-update) | async-done | bytes 6291472 | tf_op jit(solution)/shard_map/all_gather | solution.py:256
  2328.9 22.4 fusion.66
  2521.0 21.0 rev.18
  2542.0 63.9 %rev.19 = f32[4,512,1024]{2,1,0:T(8,128)} reverse(bf16[4,512,1024]{2,1,0:T(8,128)(2,1)} %copy-done.4), dimensions={2} | reverse | bytes 12582912 | tf_op jit(solution)/shard_map/rev | solution.py:65
  2605.9 95.4 %rev.20 = f32[4,512,1536]{2,1,0:T(8,128)} reverse(bf16[4,512,1536]{2,1,0:T(8,128)(2,1)} %copy-done.3), dimensions={2} | reverse | bytes 18874368 | tf_op jit(solution)/shard_map/rev | solution.py:65
  2701.2 126.8 %rev.21 = f32[4,512,2048]{2,1,0:T(8,128)} reverse(bf16[4,512,2048]{2,1,0:T(8,128)(2,1)} %copy-done.2), dimensions={2} | reverse | bytes 25165824 | tf_op jit(solution)/shard_map/rev | solution.py:65
  2828.0 158.3 %rev.22 = f32[4,512,2560]{2,1,0:T(8,128)} reverse(bf16[4,512,2560]{2,1,0:T(8,128)(2,1)} %copy-done.1), dimensions={2} | reverse | bytes 31457280 | tf_op jit(solution)/shard_map/rev | solution.py:65
  2986.3 189.8 %rev.23 = f32[4,512,3072]{2,1,0:T(8,128)} reverse(bf16[4,512,3072]{2,1,0:T(8,128)(2,1)} %copy-done), dimensions={2} | reverse | bytes 37748736 | tf_op jit(solution)/shard_map/rev | solution.py:65
  3337.3 46.8 %reshape.974 = f32[4192256]{0:T(1024)} reshape(f32[4,1048064]{1,0:T(4,128)} %slice.889) | data formatting | bytes 33538048
  3384.1 24.6 reshape.884
  3423.7 34.0 copy.235
  3474.9 58.9 %reshape.976 = f32[5240832]{0:T(1024)} reshape(f32[4,1310208]{1,0:T(4,128)} %slice.892) | data formatting | bytes 41926656
  3533.8 29.6 reshape.886
  3581.2 37.5 copy.236
  3618.7 20.6 slice.895
  3639.3 70.8 %reshape.978 = f32[6289408]{0:T(1024)} reshape(f32[4,1572352]{1,0:T(4,128)} %slice.895) | data formatting | bytes 50315264
  3710.1 34.5 reshape.888
  3772.9 33.7 copy.237
  3826.8 82.5 %reshape.980 = f32[7337984]{0:T(1024)} reshape(f32[4,1834496]{1,0:T(4,128)} %slice.897) | data formatting | bytes 58703872
  3909.3 39.5 reshape.890
  3964.1 42.5 all-reduce.11
  4023.8 126.2 %reduce-scatter.37.cloned.1.call-done = f32[32,2]{1,0:T(8,128)} async-done(((f32[1024,2]{1,0:T(8,128)}), f32[32,2]{1,0:T(8,128)}) %reduce-scatter.37.cloned.1.call-update) | async-done | bytes 272
  4152.7 130.8 %reduce-scatter.39.cloned.1.call-done = f32[32,2]{1,0:T(8,128)} async-done(((f32[1024,2]{1,0:T(8,128)}), f32[32,2]{1,0:T(8,128)}) %reduce-scatter.39.cloned.1.call-update) | async-done | bytes 272
  4294.0 42.7 psum.14
  4364.7 39.3 psum.15
  (586 shorter events, 1249.6 us)
Async XLA Ops:
  7.2 144.1 %copy-start.121 = (s32[1024]{0:T(1024)S(1)}, s32[1024]{0:T(1024)}, u32[]{:S(2)}) copy-start(s32[1024]{0:T(1024)} %constant.643) | copy-start | bytes 12292
  7.2 188.2 %copy-start.109 = (s32[3584]{0:T(1024)S(1)}, s32[3584]{0:T(1024)}, u32[]{:S(2)}) copy-start(s32[3584]{0:T(1024)} %constant.648) | copy-start | bytes 43012
  7.2 193.9 %copy-start.119 = (s32[2048]{0:T(1024)S(1)}, s32[2048]{0:T(1024)}, u32[]{:S(2)}) copy-start(s32[2048]{0:T(1024)} %constant.645) | copy-start | bytes 24580
  7.2 193.9 %copy-start.120 = (s32[1536]{0:T(1024)S(1)}, s32[1536]{0:T(1024)}, u32[]{:S(2)}) copy-start(s32[1536]{0:T(1024)} %constant.644) | copy-start | bytes 18436
  7.3 144.1 %copy-start.123 = (f32[16]{0:T(128)S(1)}, f32[16]{0:T(128)}, u32[]{:S(2)}) copy-start(f32[16]{0:T(128)} %param.99) | copy-start | bytes 196
  7.3 188.8 %copy-start.110 = (s32[3072]{0:T(1024)S(1)}, s32[3072]{0:T(1024)}, u32[]{:S(2)}) copy-start(s32[3072]{0:T(1024)} %param.94) | copy-start | bytes 36868
  7.3 937.0 %all-gather.12.cloned.1.call-start = ((), (), s32[]{:S(2)}) async-start(), calls=%async_computation.11 | async-start | bytes 1769472 | tf_op jit(solution)/shard_map/all_gather | solution.py:200
  8.5 187.6 %copy-start.24 = (f32[3,128,256]{1,2,0:T(8,128)}, f32[3,128,256]{1,2,0:T(8,128)S(1)}, u32[]{:S(2)}) copy-start(f32[3,128,256]{1,2,0:T(8,128)S(1)} %copy.173) | copy-start | bytes 1179652
  9.3 935.0 %all-gather.10.cloned.1.call-start = ((), (), s32[]{:S(2)}) async-start(), calls=%async_computation.10 | async-start | bytes 7864320 | tf_op jit(solution)/shard_map/all_gather | solution.py:208
  151.3 1265.6 %reduce-scatter.21.cloned.1.call-start = ((), (), s32[]{:S(2)}) async-start(), calls=%async_computation.12 | async-start | bytes 15728640 | tf_op jit(solution)/shard_map/reduce_scatter | solution.py:227
  955.1 84.8 %copy-start.34 = (bf16[1,512,256]{1,2,0:T(8,128)(2,1)}, bf16[1,512,256]{1,2,0:T(8,128)(2,1)S(1)}, u32[]{:S(2)}) copy-start(bf16[1,512,256]{1,2,0:T(8,128)(2,1)S(1)} %get-tuple-element.405) | copy-start | bytes 786436
  955.1 122.3 %copy-start.32 = (bf16[1,512,256]{1,2,0:T(8,128)(2,1)}, bf16[1,512,256]{1,2,0:T(8,128)(2,1)S(1)}, u32[]{:S(2)}) copy-start(bf16[1,512,256]{1,2,0:T(8,128)(2,1)S(1)} %get-tuple-element.404) | copy-start | bytes 786436
  958.0 81.8 %copy-start.18 = (bf16[1,2560,256]{1,2,0:T(8,128)(2,1)}, bf16[1,2560,256]{1,2,0:T(8,128)(2,1)S(1)}, u32[]{:S(2)}) copy-start(bf16[1,2560,256]{1,2,0:T(8,128)(2,1)S(1)} %get-tuple-element.412) | copy-start | bytes 3932164
  959.4 118.0 %copy-start.13 = (bf16[1,3072,256]{1,2,0:T(8,128)(2,1)}, bf16[1,3072,256]{1,2,0:T(8,128)(2,1)S(1)}, u32[]{:S(2)}) copy-start(bf16[1,3072,256]{1,2,0:T(8,128)(2,1)S(1)} %get-tuple-element.402) | copy-start | bytes 4718596
  964.6 156.9 %copy-start.100 = (f32[4,512]{1,0:T(4,128)}, f32[4,512]{1,0:T(4,128)S(1)}, u32[]{:S(2)}) copy-start(f32[4,512]{1,0:T(4,128)S(1)} %get-tuple-element.446) | copy-start | bytes 24580
  985.2 141.0 %copy-start.97 = (f32[4,512]{1,0:T(4,128)}, f32[4,512]{1,0:T(4,128)S(1)}, u32[]{:S(2)}) copy-start(f32[4,512]{1,0:T(4,128)S(1)} %get-tuple-element.448) | copy-start | bytes 24580
  1007.4 128.7 %copy-start.94 = (f32[4,512]{1,0:T(4,128)}, f32[4,512]{1,0:T(4,128)S(1)}, u32[]{:S(2)}) copy-start(f32[4,512]{1,0:T(4,128)S(1)} %get-tuple-element.450) | copy-start | bytes 24580
  1039.8 108.7 %copy-start.106 = (f32[4,512]{1,0:T(4,128)}, f32[4,512]{1,0:T(4,128)S(1)}, u32[]{:S(2)}) copy-start(f32[4,512]{1,0:T(4,128)S(1)} %get-tuple-element.452) | copy-start | bytes 24580
  1077.4 84.6 %copy-start.104 = (f32[4,512]{1,0:T(4,128)}, f32[4,512]{1,0:T(4,128)S(1)}, u32[]{:S(2)}) copy-start(f32[4,512]{1,0:T(4,128)S(1)} %get-tuple-element.454) | copy-start | bytes 24580
  1204.4 212.5 %copy-start.7 = (bf16[768,1024]{1,0:T(8,128)(2,1)S(1)}, bf16[768,1024]{1,0:T(8,128)(2,1)}, u32[]{:S(2)}) copy-start(bf16[768,1024]{1,0:T(8,128)(2,1)} %param.91) | copy-start | bytes 4718596
  1204.4 216.5 %copy-start.86 = (f32[1,1024]{1,0:T(1,128)S(1)}, f32[1,1024]{1,0:T(1,128)}, u32[]{:S(2)}) copy-start(f32[1,1024]{1,0:T(1,128)} %get-tuple-element.433) | copy-start | bytes 12292
  1204.4 216.5 %copy-start.108 = (f32[1,1024]{1,0:T(1,128)S(1)}, f32[1,1024]{1,0:T(1,128)}, u32[]{:S(2)}) copy-start(f32[1,1024]{1,0:T(1,128)} %get-tuple-element.435) | copy-start | bytes 12292
  1204.4 243.7 %all-gather.16.cloned.1.call-start = ((), (), s32[]{:S(2)}) async-start(), calls=%async_computation.14 | async-start | bytes 2359296 | tf_op jit(solution)/shard_map/all_gather | solution.py:202
  1206.8 355.7 %all-gather.14.cloned.1.call-start = ((), (), s32[]{:S(2)}) async-start(), calls=%async_computation.13 | async-start | bytes 7864320 | tf_op jit(solution)/shard_map/all_gather | solution.py:235
  1419.7 155.1 %copy-start.91 = (f32[768]{0:T(1024)}, f32[768]{0:T(1024)S(1)}, u32[]{:S(2)}) copy-start(f32[768]{0:T(1024)S(1)} %multiply_reduce_fusion.8) | copy-start | bytes 9220
  1422.7 171.6 %all-gather.18.cloned.1.call-start = ((), (), s32[]{:S(2)}) async-start(), calls=%async_computation.15 | async-start | bytes 2359296 | tf_op jit(solution)/shard_map/all_gather | solution.py:203
  1424.1 284.2 %all-gather.20.cloned.1.call-start = ((), (), s32[]{:S(2)}) async-start(), calls=%async_computation.17 | async-start | bytes 7864320 | tf_op jit(solution)/shard_map/all_gather | solution.py:209
  1424.9 547.2 %reduce-scatter.25.cloned.1.call-start = ((), (), s32[]{:S(2)}) async-start(), calls=%async_computation.18 | async-start | bytes 15728640 | tf_op jit(solution)/shard_map/reduce_scatter | solution.py:250
  1574.8 174.8 %copy-start.125 = (bf16[1024,1024]{1,0:T(8,128)(2,1)S(1)}, bf16[1024,1024]{1,0:T(8,128)(2,1)}, u32[]{:S(2)}) copy-start(bf16[1024,1024]{1,0:T(8,128)(2,1)} %all-gather.16.cloned.1.call-done) | copy-start | bytes 6291460
  1758.9 327.4 %reduce-scatter.23.cloned.1.call-start = ((), (), s32[]{:S(2)}) async-start(), calls=%async_computation.16 | async-start | bytes 7864320 | tf_op jit(solution)/shard_map/reduce_scatter | solution.py:238
  1781.1 191.0 %copy-start.6 = (f32[768,1024]{1,0:T(8,128)S(1)}, f32[768,1024]{1,0:T(8,128)}, u32[]{:S(2)}) copy-start(f32[768,1024]{1,0:T(8,128)} %copy-done.5) | copy-start | bytes 9437188
  1781.1 191.0 %copy-start.77 = (f32[768]{0:T(1024)S(1)}, f32[768]{0:T(1024)}, u32[]{:S(2)}) copy-start(f32[768]{0:T(1024)} %copy-done.76) | copy-start | bytes 9220
  1781.1 191.0 %copy-start.85 = (f32[768]{0:T(1024)S(1)}, f32[768]{0:T(1024)}, u32[]{:S(2)}) copy-start(f32[768]{0:T(1024)} %copy-done.84) | copy-start | bytes 9220
  1781.1 191.0 %copy-start.87 = (f32[1,1024]{1,0:T(1,128)S(1)}, f32[1,1024]{1,0:T(1,128)}, u32[]{:S(2)}) copy-start(f32[1,1024]{1,0:T(1,128)} %get-tuple-element.433) | copy-start | bytes 12292
  1781.1 194.5 %copy-start.92 = (f32[768]{0:T(1024)S(1)}, f32[768]{0:T(1024)}, u32[]{:S(2)}) copy-start(f32[768]{0:T(1024)} %copy-done.91) | copy-start | bytes 9220
  1781.1 425.6 %all-gather.22.cloned.1.call-start = ((), (), s32[]{:S(2)}) async-start(), calls=%async_computation.19 | async-start | bytes 7864320 | tf_op jit(solution)/shard_map/all_gather | solution.py:256
  2093.7 423.7 %reduce-scatter.35.cloned.1.call-start = ((), (), s32[]{:S(2)}) async-start(), calls=%async_computation.24 | async-start | bytes 2359296
  2107.1 99.7 %copy-start.47 = (bf16[256,1024]{1,0:T(8,128)(2,1)S(1)}, bf16[256,1024]{1,0:T(8,128)(2,1)}, u32[]{:S(2)}) copy-start(bf16[256,1024]{1,0:T(8,128)(2,1)} %all_gather.38) | copy-start | bytes 1572868
  2107.1 412.2 %reduce-scatter.29.cloned.1.call-start = ((), (), s32[]{:S(2)}) async-start(), calls=%async_computation.21 | async-start | bytes 2359296 | tf_op jit(solution)/shard_map/reduce_scatter | solution.py:301
  2119.3 93.8 %copy-start.101 = (f32[4,512]{1,0:T(4,128)S(1)}, f32[4,512]{1,0:T(4,128)}, u32[]{:S(2)}) copy-start(f32[4,512]{1,0:T(4,128)} %copy-done.100) | copy-start | bytes 24580
  2119.3 1888.0 %reduce-scatter.33.cloned.1.call-start = ((), (), s32[]{:S(2)}) async-start(), calls=%async_computation.23 | async-start | bytes 589824
  2486.1 1522.8 %reduce-scatter.31.cloned.1.call-start = ((), (), s32[]{:S(2)}) async-start(), calls=%async_computation.22 | async-start | bytes 1769472
  2500.2 1510.6 %reduce-scatter.27.cloned.1.call-start = ((), (), s32[]{:S(2)}) async-start(), calls=%async_computation.20 | async-start | bytes 7864320 | tf_op jit(solution)/shard_map/reduce_scatter | solution.py:268
  2509.9 1640.1 %reduce-scatter.37.cloned.1.call-start = ((), (), s32[]{:S(2)}) async-start(), calls=%async_computation.25 | async-start | bytes 540672
  2518.5 87.3 %copy-start.45 = (bf16[1024,128]{1,0:T(8,128)(2,1)}, bf16[1024,128]{1,0:T(8,128)(2,1)S(1)}, u32[]{:S(2)}) copy-start(bf16[1024,128]{1,0:T(8,128)(2,1)S(1)} %copy.218) | copy-start | bytes 786436
  3960.2 378.5 %copy-start.25 = (f32[3,128,256]{1,2,0:T(8,128)S(1)}, f32[3,128,256]{1,2,0:T(8,128)}, u32[]{:S(2)}) copy-start(f32[3,128,256]{1,2,0:T(8,128)} %copy-done.24) | copy-start | bytes 1179652
  4013.9 346.7 %copy-start.20 = (bf16[768,1024]{1,0:T(8,128)(2,1)S(1)}, bf16[768,1024]{1,0:T(8,128)(2,1)}, u32[]{:S(2)}) copy-start(bf16[768,1024]{1,0:T(8,128)(2,1)} %reduce-scatter.27.cloned.1.call-done) | copy-start | bytes 4718596
  4020.7 262.8 %reduce-scatter.39.cloned.1.call-start = ((), (), s32[]{:S(2)}) async-start(), calls=%async_computation.26 | async-start | bytes 540672
  (114 other events, 1628.5 us)
Sparse Core Ops, SparseCore 0:
  10.6 27.0 all-gather.11
  151.4 110.6 all-gather.9
  1204.5 212.3 reduce-scatter.20
  1419.2 28.9 all-gather.15
  1450.2 112.3 all-gather.13
  1564.9 29.3 all-gather.17
  1595.9 112.3 all-gather.19
  1759.0 213.0 reduce-scatter.24
  1974.4 111.7 reduce-scatter.22
  2093.8 112.8 all-gather.21
  2210.0 42.4 reduce-scatter.34
  2256.0 41.2 reduce-scatter.28
  2486.2 35.8 reduce-scatter.32
  2525.6 38.4 reduce-scatter.30
  2566.4 110.6 reduce-scatter.26
  4020.8 129.1 reduce-scatter.36
  4152.7 130.7 reduce-scatter.38
where the time goes:
time: 4520 us; the launch traced here: 4430 us
  local copies, waits for them, and re-layouts  2190 us (48%)
  waiting for transfers between devices  1130 us (25%)
  matrix products  467 us (10%)
  blocking collectives  313 us (7%)
  other arithmetic  310 us (7%)
    unnamed x348, local copies, waits for them, and re-layouts  1000 us
    rev x6, local copies, waits for them, and re-layouts, diagonal_sums(): flipped = block[:, :, ::-1]  655 us
    unnamed x22, waiting for transfers between devices  258 us
    reduce_scatter x1, waiting for transfers between devices, per_device(): lax.psum_scatter(jnp.dot(attn_out, proj_full, preferred_element_type=jnp....  210 us
    reduce_scatter x1, waiting for transfers between devices, per_device(): lax.psum_scatter(contract_cols(grad_pre, up_full), 'tensor', scatter_dime...  191 us
    reshape x6, local copies, waits for them, and re-layouts, toeplitz_bias(): return tiled.reshape(heads_here, rows, period - 1)[:, :, :width]  164 us
    reshape x6, local copies, waits for them, and re-layouts, diagonal_sums(): skewed = flat.reshape(heads_here, rows, full_width - 1)  163 us
    all_gather x1, waiting for transfers between devices, per_device(): lax.all_gather(second_norm.astype(jnp.bfloat16), 'tensor', axis=0, tiled=...  114 us
  transfers between devices with their start and end apart: 17, of which 10 were waited for; matrix products, arithmetic and copies ran while one was open for 58% of the time, Pallas kernels for 0%

commit v1 on v0

v1 whole, which is shorter than its diff:
```python
import functools

import jax
import jax.numpy as jnp
from jax import lax
from jax.experimental import pallas as pl
from jax.experimental.pallas import tpu as pltpu
from jax.sharding import Mesh
from jax.sharding import PartitionSpec as P

H = 16
DH = 64
BUCKETS = 32
BLK = 512
NEG = -1e30
LOG2E = 1.4426950408889634
F32 = jnp.float32
BF = jnp.bfloat16
MESH = pl.DeviceIdType.MESH
HIGHEST = lax.Precision.HIGHEST
ALL = ("xy", "core", "zh", "zl")
DP = ("xy", "core")
TENSOR = ("zh", "zl")


def dot(left, right, left_dim, right_dim):
    return lax.dot_general(
        left, right, (((left_dim,), (right_dim,)), ((), ())), preferred_element_type=F32
    )


def make_slab(pattern, slab):
    width = slab.shape[1]
    slab[0:8, :] = pltpu.roll(jnp.broadcast_to(pattern, (8, width)), 0, 1, stride=1, stride_axis=0)
    done = 8
    while done < slab.shape[0]:
        slab[done : 2 * done, :] = pltpu.roll(slab[0:done, :], done, 1)
        done *= 2


def fold_slab(slab):
    width = slab.shape[1]
    half = slab.shape[0] // 2
    while half >= 8:
        slab[0:half, :] = slab[0:half, :] + pltpu.roll(slab[half : 2 * half, :], width - half, 1)
        half //= 2
    total = slab[0:1, :]
    for row in range(1, 8):
        total = total + pltpu.roll(slab[row : row + 1, :], width - row, 1)
    return total


def split_three(values):
    high = values.astype(BF).astype(F32)
    rest = values - high
    middle = rest.astype(BF).astype(F32)
    return high, middle, (rest - middle).astype(BF).astype(F32)


def put_queries(queries, split, minus, tok, dst):
    scaled = queries.astype(F32) * (DH**-0.5 * LOG2E)
    high = scaled.astype(BF)
    dst[0:DH, :] = high
    dst[DH : 2 * DH, :] = (scaled - high.astype(F32)).astype(BF)
    position = lax.broadcasted_iota(jnp.int32, (16, tok), 1)
    row = lax.broadcasted_iota(jnp.int32, (16, tok), 0)
    extra = jnp.where((row == 0) & (position >= split), 1.0, 0.0)
    if minus is not None:
        first, second, third = split_three(minus)
        extra = jnp.where(
            row == 1, first, jnp.where(row == 2, second, jnp.where(row == 3, third, extra))
        )
    dst[2 * DH : 2 * DH + 16, :] = extra.astype(BF)


def put_keys(keys, split, tok, dst):
    for start in range(0, tok, BLK):
        position = start + lax.broadcasted_iota(jnp.int32, (16, BLK), 1)
        row = lax.broadcasted_iota(jnp.int32, (16, BLK), 0)
        extra = jnp.where(
            row == 0, jnp.where(position < split, NEG, 0.0), jnp.where(row < 4, 1.0, 0.0)
        )
        block = keys[:, start : start + BLK].astype(F32)
        whole = jnp.concatenate([block, block, extra], axis=0)
        dst[start : start + BLK, :] = whole.T.astype(BF)


def block_at(index):
    return pl.ds(pl.multiple_of(index * BLK, BLK), BLK)


def attend_kernel(split_ref, pattern_ref, q_ref, k_ref, v_ref, o_ref, lse_ref, slab, kx, qx):
    tok = q_ref.shape[1]
    split = split_ref[0]
    make_slab(pattern_ref[0], slab)
    put_queries(q_ref[...], split, None, tok, qx)
    put_keys(k_ref, split, tok, kx)

    def step(i, j, top, total, out):
        scores = dot(kx[block_at(j), :], qx[:, block_at(i)], 1, 0) + slab[:, block_at(i - j)]
        new_top = jnp.maximum(top, jnp.max(scores, axis=0, keepdims=True))
        weights = jnp.exp2(scores - new_top)
        scale = jnp.exp2(top - new_top)
        total = total * scale + jnp.sum(weights, axis=0, keepdims=True)
        out = out * scale + dot(v_ref[:, block_at(j)], weights.astype(BF), 1, 0)
        return new_top, total, out

    def row(i, carry):
        start = (
            jnp.full((1, BLK), NEG, F32),
            jnp.zeros((1, BLK), F32),
            jnp.zeros((DH, BLK), F32),
        )
        top, total, out = lax.fori_loop(0, i + 1, lambda t, c: step(i, i - t, *c), start)
        o_ref[:, block_at(i)] = (out / total).astype(BF)
        lse_ref[0, :, block_at(i)] = top + jnp.log2(total)
        return carry

    lax.fori_loop(0, tok // BLK, row, 0)


def attend(qkv, pattern, split, heads):
    tok = qkv.shape[1]
    width = pattern.shape[-1]
    return pl.pallas_call(
        attend_kernel,
        grid=(heads,),
        in_specs=[
            pl.BlockSpec(memory_space=pltpu.SMEM),
            pl.BlockSpec((1, 1, width), lambda h: (h, 0, 0)),
            pl.BlockSpec((DH, tok), lambda h: (h, 0)),
            pl.BlockSpec((DH, tok), lambda h: (h + heads, 0)),
            pl.BlockSpec((DH, tok), lambda h: (h + 2 * heads, 0)),
        ],
        out_specs=[
            pl.BlockSpec((DH, tok), lambda h: (h, 0)),
            pl.BlockSpec((1, 1, tok), lambda h: (h, 0, 0)),
        ],
        out_shape=[
            jax.ShapeDtypeStruct((heads * DH, tok), BF),
            jax.ShapeDtypeStruct((heads, 1, tok), F32),
        ],
        scratch_shapes=[
            pltpu.VMEM((BLK, width), F32),
            pltpu.VMEM((tok, 2 * DH + 16), BF),
            pltpu.VMEM((2 * DH + 16, tok), BF),
        ],
        compiler_params=pltpu.CompilerParams(vmem_limit_bytes=56 * 2**20),
        cost_estimate=pl.CostEstimate(
            flops=heads * tok * tok * 800, bytes_accessed=8 * heads * DH * tok, transcendentals=0
        ),
        name="attend",
    )(split, pattern, qkv, qkv, qkv)


def attend_back_kernel(
    split_ref, pattern_ref, q_ref, k_ref, v_ref, o_ref, do_ref, lse_ref,
    dq_ref, dk_ref, dv_ref, dpattern_ref,
    slab, dslab, kx, qx, vx, dox, qn, don, dk, dv,
):
    tok = q_ref.shape[1]
    split = split_ref[0]
    make_slab(pattern_ref[0], slab)
    put_queries(q_ref[...], split, -lse_ref[0], tok, qx)
    put_keys(k_ref, split, tok, kx)
    dslab[...] = jnp.zeros_like(dslab)
    dk[...] = jnp.zeros_like(dk)
    dv[...] = jnp.zeros_like(dv)
    row = lax.broadcasted_iota(jnp.int32, (16, BLK), 0)
    ones = jnp.where(row < 3, 1.0, 0.0)
    for start in range(0, tok, BLK):
        here = slice(start, start + BLK)
        grad = do_ref[:, here].astype(F32)
        inner = jnp.sum(grad * o_ref[:, here].astype(F32), axis=0, keepdims=True)
        first, second, third = split_three(-inner)
        extra = jnp.where(
            row == 0, first, jnp.where(row == 1, second, jnp.where(row == 2, third, 0.0))
        )
        dox[0:DH, here] = do_ref[:, here]
        dox[DH : DH + 16, here] = extra.astype(BF)
        vx[here, :] = jnp.concatenate([v_ref[:, here].astype(F32), ones], axis=0).T.astype(BF)
        both = jnp.concatenate([q_ref[:, here].astype(F32), grad], axis=0).T
        qn[here, :] = both[:, 0:DH].astype(BF)
        don[here, :] = both[:, DH : 2 * DH].astype(BF)

    def tile(i, j):
        qs, ks, diagonal = block_at(i), block_at(j), block_at(i - j)
        shares = jnp.exp2(dot(kx[ks, :], qx[:, qs], 1, 0) + slab[:, diagonal])
        grad_scores = shares * dot(vx[ks, :], dox[:, qs], 1, 0)
        dslab[:, diagonal] += grad_scores
        low = grad_scores.astype(BF)
        dv[ks, :] += dot(shares.astype(BF), don[qs, :], 1, 0)
        dk[ks, :] += dot(low, qn[qs, :], 1, 0)
        return dot(k_ref[:, ks], low, 1, 0)

    def query_row(i, carry):
        total = lax.fori_loop(
            0, i + 1, lambda t, c: c + tile(i, i - t), jnp.zeros((DH, BLK), F32)
        )
        dq_ref[:, block_at(i)] = (total * DH**-0.5).astype(BF)
        return carry

    lax.fori_loop(0, tok // BLK, query_row, 0)
    for start in range(0, tok, BLK):
        here = slice(start, start + BLK)
        dk_ref[:, here] = (dk[here, :] * DH**-0.5).T.astype(BF)
        dv_ref[:, here] = dv[here, :].T.astype(BF)
    dpattern_ref[0] = fold_slab(dslab)


def attend_back(qkv, out, grad, lse, pattern, split, heads):
    tok = qkv.shape[1]
    width = pattern.shape[-1]
    flat = pl.BlockSpec((DH, tok), lambda h: (h, 0))
    return pl.pallas_call(
        attend_back_kernel,
        grid=(heads,),
        in_specs=[
            pl.BlockSpec(memory_space=pltpu.SMEM),
            pl.BlockSpec((1, 1, width), lambda h: (h, 0, 0)),
            flat,
            pl.BlockSpec((DH, tok), lambda h: (h + heads, 0)),
            pl.BlockSpec((DH, tok), lambda h: (h + 2 * heads, 0)),
            flat,
            flat,
            pl.BlockSpec((1, 1, tok), lambda h: (h, 0, 0)),
        ],
        out_specs=[flat] * 3 + [pl.BlockSpec((1, 1, width), lambda h: (h, 0, 0))],
        out_shape=[jax.ShapeDtypeStruct((heads * DH, tok), BF)] * 3
        + [jax.ShapeDtypeStruct((heads, 1, width), F32)],
        scratch_shapes=[
            pltpu.VMEM((BLK, width), F32),
            pltpu.VMEM((BLK, width), F32),
            pltpu.VMEM((tok, 2 * DH + 16), BF),
            pltpu.VMEM((2 * DH + 16, tok), BF),
            pltpu.VMEM((tok, DH + 16), BF),
            pltpu.VMEM((DH + 16, tok), BF),
            pltpu.VMEM((tok, DH), BF),
            pltpu.VMEM((tok, DH), BF),
            pltpu.VMEM((tok, DH), F32),
            pltpu.VMEM((tok, DH), F32),
        ],
        compiler_params=pltpu.CompilerParams(vmem_limit_bytes=60 * 2**20),
        cost_estimate=pl.CostEstimate(
            flops=heads * tok * tok * 1200, bytes_accessed=16 * heads * DH * tok, transcendentals=0
        ),
        name="attend_back",
    )(split, pattern, qkv, qkv, qkv, out, grad, lse)


def place():
    return tuple(lax.axis_index(axis) for axis in ALL)


def exchange_kernel(shape, to_owners, src_ref, dst_ref, send_sem, recv_sem, local_sem):
    places = shape["zl"]
    parts = shape["zh"] * places
    rows = dst_ref.shape[-1] if to_owners else src_ref.shape[-1]
    xy, core, zh, zl = place()
    mine_row = zh * places + zl
    mine_head = zl * 2 + core

    def owner(group, n):
        return (xy, group, n // places, n % places)

    def header(group, n):
        return (xy, n % 2, group, n // 2)

    def is_me(device):
        return (device[1] == core) & (device[2] == zh) & (device[3] == zl)

    if to_owners:
        def target(n):
            return owner(zh, n)

        def source(n):
            return header(core, n)

        mine = mine_head
    else:
        def target(n):
            return header(core, n)

        def source(n):
            return owner(zh, n)

        mine = mine_row
    barrier = pltpu.get_barrier_semaphore()
    for n in range(parts):
        device = source(n)

        @pl.when(jnp.logical_not(is_me(device)))
        def _():
            pl.semaphore_signal(barrier, inc=1, device_id=device, device_id_type=MESH)

    has_self = (zh == core).astype(jnp.int32)
    pl.semaphore_wait(barrier, parts - has_self)

    def piece(n):
        if to_owners:
            return src_ref.at[:, pl.ds(n * rows, rows)]
        return src_ref.at[n]

    def slot(n):
        if to_owners:
            return dst_ref.at[n]
        return dst_ref.at[:, pl.ds(pl.multiple_of(n * rows, rows), rows)]

    def remote(n, device):
        return pltpu.make_async_remote_copy(
            src_ref=piece(n),
            dst_ref=slot(mine),
            send_sem=send_sem.at[n],
            recv_sem=recv_sem.at[mine],
            device_id=device,
            device_id_type=MESH,
        )

    for n in range(parts):
        device = target(n)

        @pl.when(is_me(device))
        def _():
            pltpu.make_async_copy(piece(n), slot(mine), local_sem).start()

        @pl.when(jnp.logical_not(is_me(device)))
        def _():
            remote(n, device).start()

    for n in range(parts):
        device = target(n)

        @pl.when(is_me(device))
        def _():
            pltpu.make_async_copy(piece(n), slot(mine), local_sem).wait()

        @pl.when(jnp.logical_not(is_me(device)))
        def _():
            remote(n, device).wait_send()

    for n in range(parts):
        device = source(n)

        @pl.when(jnp.logical_not(is_me(device)))
        def _():
            pltpu.make_async_remote_copy(
                src_ref=piece(n),
                dst_ref=slot(n),
                send_sem=send_sem.at[n],
                recv_sem=recv_sem.at[n],
                device_id=device,
                device_id_type=MESH,
            ).wait_recv()


def exchange(shape, pieces, to_owners, collective_id):
    parts = shape["zh"] * shape["zl"]
    if to_owners:
        depth, rows = pieces.shape[0], pieces.shape[1] // parts
        out = (parts, depth, rows)
    else:
        depth, rows = pieces.shape[1], pieces.shape[2]
        out = (depth, parts * rows)
    return pl.pallas_call(
        functools.partial(exchange_kernel, shape, to_owners),
        out_shape=jax.ShapeDtypeStruct(out, pieces.dtype),
        in_specs=[pl.BlockSpec(memory_space=pl.ANY)],
        out_specs=pl.BlockSpec(memory_space=pl.ANY),
        scratch_shapes=[
            pltpu.SemaphoreType.DMA((parts,)),
            pltpu.SemaphoreType.DMA((parts,)),
            pltpu.SemaphoreType.DMA,
        ],
        compiler_params=pltpu.CompilerParams(collective_id=collective_id, has_side_effects=True),
        name="exchange",
    )(pieces)


def norm_parts(values):
    center = values - jnp.mean(values, axis=-1, keepdims=True)
    inverse = lax.rsqrt(jnp.mean(center * center, axis=-1, keepdims=True) + 1e-05)
    return center * inverse, inverse


def norm_back(normed, inverse, gain, grad):
    inner = grad * gain
    return inverse * (
        inner
        - jnp.mean(inner, axis=-1, keepdims=True)
        - normed * jnp.mean(inner * normed, axis=-1, keepdims=True)
    )


def gelu_exact(values):
    return jax.nn.gelu(values, approximate=False)


def squares_of(arrays):
    qkv, proj, up, down = arrays
    return jnp.concatenate(
        [
            jnp.sum(qkv * qkv, axis=(1, 2)),
            jnp.stack([jnp.sum(proj * proj), jnp.sum(up * up), jnp.sum(down * down)]),
        ]
    )


def small_squares(table, gain, shift):
    return jnp.concatenate(
        [jnp.sum(table * table)[None], jnp.sum(gain * gain, axis=1), jnp.sum(shift * shift, axis=1)]
    )


def expand(values):
    return (
        values[0:3][:, None, None],
        values[3],
        values[4],
        values[5],
        values[6],
        values[7:9][:, None],
        values[9:11][:, None],
    )


def per_device(
    shape,
    tokens, cotangent, item_len, bucket_table,
    w_qkv, w_proj, w_up, w_down, rel_bias, ln_gain, ln_shift,
    mean_qkv, mean_proj, mean_up, mean_down, mean_bias, mean_gain, mean_shift,
    square_qkv, square_proj, square_up, square_down, square_bias, square_gain, square_shift,
):
    columns, places = shape["xy"], shape["zl"]
    parts = 2 * places
    devices = columns * 2 * parts
    rows, width = tokens.shape
    heads = w_qkv.shape[2] // DH
    tok = rows * parts
    xy, core, zh, zl = place()
    me = ((xy * 2 + core) * 2 + zh) * places + zl
    head_block = zl * 2 + core

    to_heads = [
        (((c * 2 + k) * parts + z), ((c * 2 + z % 2) * 2 + k) * places + z // 2)
        for c in range(columns)
        for k in range(2)
        for z in range(parts)
    ]
    to_owner = [(b, a) for a, b in to_heads]
    w_heads = lax.all_gather(
        lax.ppermute(w_qkv.astype(BF), ALL, to_heads), ("xy", "zh"), axis=1, tiled=True
    )
    ff_local = w_up.shape[1]
    local = jnp.concatenate([w_proj.T, w_up, w_down.T], axis=1).astype(BF)
    shared = lax.all_gather(
        lax.all_gather(local, TENSOR, axis=0), DP, axis=1, tiled=True
    )
    heads_cols = w_proj.shape[0]
    proj_full = shared[:, :, :heads_cols]
    up_full = shared[:, :, heads_cols : heads_cols + ff_local]
    down_full = shared[:, :, heads_cols + ff_local :]

    small_local = jnp.concatenate([rel_bias, ln_gain.reshape(-1), ln_shift.reshape(-1)])
    small = lax.all_gather(small_local, ALL, axis=0)
    n_bias, n_gain = rel_bias.shape[0], ln_gain.shape[1]

    def columns_of(start):
        part = small[:, start : start + 2 * n_gain].reshape(devices, 2, n_gain)
        return part.transpose(1, 0, 2).reshape(2, width)

    table_flat = small[:, :n_bias].reshape(-1)
    gains, shifts = columns_of(n_bias), columns_of(n_bias + 2 * n_gain)

    swap = [(k * 2 + h, h * 2 + k) for k in range(2) for h in range(2)]
    group_rows = lax.all_gather(
        lax.ppermute(tokens, ("core", "zh"), swap), ("core", "zl"), axis=0, tiled=True
    )
    other_len = lax.ppermute(item_len, "core", [(0, 1), (1, 0)])
    split = jnp.where(zh == core, item_len, other_len)[0, 0:1]

    normed_all, _ = norm_parts(group_rows.astype(F32))
    a_first = (normed_all * gains[0] + shifts[0]).astype(BF)
    qkv = lax.dot_general(
        w_heads, a_first, (((1,), (1,)), ((), ())), preferred_element_type=F32
    ).astype(BF).reshape(3 * heads * DH, tok)

    table = lax.dynamic_slice_in_dim(
        table_flat.reshape(BUCKETS, H), head_block * heads, heads, 1
    )
    one_hot = (jnp.arange(BUCKETS)[:, None] == bucket_table[None, :]).astype(F32)
    dist_bias = lax.dot_general(
        table, one_hot, (((0,), (0,)), ((), ())), precision=HIGHEST, preferred_element_type=F32
    )
    pattern = jnp.concatenate(
        [dist_bias * LOG2E, jnp.full((heads, BLK), NEG, F32)], axis=1
    )[:, None, :]
    out, lse = attend(qkv, pattern, split, heads)

    attn_rows = exchange(shape, out, True, 0)
    x_rows = tokens.astype(F32)
    mixed = lax.dot_general(
        attn_rows, proj_full, (((0, 1), (0, 2)), ((), ())), preferred_element_type=F32
    )
    middle = x_rows + mixed
    normed_two, inverse_two = norm_parts(middle)
    a_second = (normed_two * gains[1] + shifts[1]).astype(BF)
    hidden_pre = jnp.einsum("nd,zdf->znf", a_second, up_full, preferred_element_type=F32)
    hidden = gelu_exact(hidden_pre).astype(BF)
    ffn = jnp.einsum("znf,zdf->nd", hidden, down_full, preferred_element_type=F32)
    block_out = (middle + ffn).astype(BF)
    _, gelu_back = jax.vjp(gelu_exact, hidden_pre)
    grad_down = jnp.einsum("nd,znf->zdf", cotangent, hidden, preferred_element_type=F32).astype(BF)
    grad_hidden = jnp.einsum("nd,zdf->znf", cotangent, down_full, preferred_element_type=F32)
    grad_pre = gelu_back(grad_hidden)[0].astype(BF)
    grad_up = jnp.einsum("nd,znf->zdf", a_second, grad_pre, preferred_element_type=F32).astype(BF)
    grad_second = jnp.einsum("znf,zdf->nd", grad_pre, up_full, preferred_element_type=F32)
    grad_middle = cotangent.astype(F32) + norm_back(normed_two, inverse_two, gains[1], grad_second)
    gain_two, shift_two = jnp.sum(grad_second * normed_two, axis=0), jnp.sum(grad_second, axis=0)
    grad_mid_low = grad_middle.astype(BF)
    grad_attn = jnp.einsum(
        "nd,tde->ten", grad_mid_low, proj_full, preferred_element_type=F32
    ).astype(BF)
    grad_proj = jnp.einsum(
        "nd,ten->tde", grad_mid_low, attn_rows, preferred_element_type=F32
    ).astype(BF)

    grad_out = exchange(shape, grad_attn, False, 1)
    grad_q, grad_k, grad_v, grad_pattern = attend_back(
        qkv, out, grad_out, lse, pattern, split, heads
    )
    grad_heads = jnp.stack([grad_q, grad_k, grad_v])
    grad_qkv = jnp.einsum("td,cet->cde", a_first, grad_heads, preferred_element_type=F32).astype(BF)
    grad_first = jnp.einsum(
        "cet,cde->td", grad_heads, w_heads, preferred_element_type=F32
    )
    gain_one, shift_one = jnp.sum(grad_first * normed_all, axis=0), jnp.sum(grad_first, axis=0)
    first_rows = lax.ppermute(
        lax.psum_scatter(grad_first.astype(BF), ("core", "zl"), scatter_dimension=0, tiled=True),
        ("core", "zh"),
        swap,
    ).astype(F32)
    normed_one, inverse_one = norm_parts(x_rows)
    grad_tokens = (
        grad_middle + norm_back(normed_one, inverse_one, gains[0], first_rows)
    ).astype(BF)

    def scatter(grad):
        part = lax.psum_scatter(grad, DP, scatter_dimension=1, tiled=True)
        return lax.psum_scatter(part, TENSOR, scatter_dimension=0, tiled=False).astype(F32)

    sum_down, sum_up, sum_proj = scatter(grad_down).T, scatter(grad_up), scatter(grad_proj).T
    sum_qkv = lax.ppermute(
        lax.psum_scatter(grad_qkv, ("xy", "zh"), scatter_dimension=1, tiled=True), ALL, to_owner
    ).astype(F32)
    bias_grad = lax.dot_general(
        one_hot, grad_pattern[:, 0, :tok], (((1,), (1,)), ((), ())),
        precision=HIGHEST, preferred_element_type=F32,
    )
    table_grad = lax.dynamic_update_slice(
        jnp.zeros((BUCKETS, H), F32), bias_grad, (0, head_block * heads)
    ).reshape(-1)
    small_sum = lax.psum(
        jnp.concatenate([table_grad, gain_one, gain_two, shift_one, shift_two]), ALL
    )
    full_table = small_sum[: BUCKETS * H]
    full_gain = small_sum[BUCKETS * H : BUCKETS * H + 2 * width].reshape(2, width)
    full_shift = small_sum[BUCKETS * H + 2 * width :].reshape(2, width)
    sum_table = lax.dynamic_slice_in_dim(full_table, me * n_bias, n_bias, 0)
    sum_gain = lax.dynamic_slice_in_dim(full_gain, me * n_gain, n_gain, 1)
    sum_shift = lax.dynamic_slice_in_dim(full_shift, me * n_gain, n_gain, 1)

    params = (w_qkv, w_proj, w_up, w_down, rel_bias, ln_gain, ln_shift)
    grads = (sum_qkv, sum_proj, sum_up, sum_down, sum_table, sum_gain, sum_shift)
    means = (mean_qkv, mean_proj, mean_up, mean_down, mean_bias, mean_gain, mean_shift)
    squares = (
        square_qkv, square_proj, square_up, square_down, square_bias, square_gain, square_shift,
    )
    sq_weight = lax.psum(
        jnp.concatenate([squares_of(params[:4]), small_squares(*params[4:])]), ALL
    )
    sq_grad = jnp.concatenate(
        [lax.psum(squares_of(grads[:4]), ALL), small_squares(full_table, full_gain, full_shift)]
    )
    grad_norm = jnp.sqrt(jnp.sum(sq_grad))
    clip = jnp.minimum(1.0, 1.0 / grad_norm)
    new_means = [0.5 * m + 0.5 * (clip * g) for m, g in zip(means, grads)]
    new_squares = [0.5 * s + 0.5 * (clip * g) * (clip * g) for s, g in zip(squares, grads)]
    updates = [
        nm / (jnp.sqrt(ns) + 1e-06) + 0.01 * w for nm, ns, w in zip(new_means, new_squares, params)
    ]
    sq_update = lax.psum(
        jnp.concatenate([squares_of(updates[:4]), small_squares(*updates[4:])]), ALL
    )
    trust = jnp.sqrt(sq_weight) / jnp.sqrt(sq_update)
    factors = expand(trust)
    new_weights = [w - 0.3 * f * u for w, f, u in zip(params, factors, updates)]
    param_norms = jnp.stack([jnp.sqrt(sq_weight), jnp.sqrt(sq_update)])
    return (block_out, grad_tokens, grad_norm, param_norms, *new_weights, *new_means, *new_squares)


def solution(mesh):
    shape = {"xy": mesh.shape["dp"] // 2, "core": 2, "zh": 2, "zl": mesh.shape["tensor"] // 2}
    split_mesh = Mesh(mesh.devices.reshape(tuple(shape[axis] for axis in ALL)), ALL)
    weights = (
        P(None, DP, TENSOR),
        P(TENSOR, DP),
        P(DP, TENSOR),
        P(TENSOR, DP),
        P(ALL),
        P(None, ALL),
        P(None, ALL),
    )
    rows = P(ALL, None)
    return jax.shard_map(
        functools.partial(per_device, shape),
        mesh=split_mesh,
        in_specs=(rows, rows, P(DP, None), P(), *weights, *weights, *weights),
        out_specs=(rows, rows, P(), P(), *weights, *weights, *weights),
        check_vma=False,
    )
```

time: 4520 us -> 1110 us (0.25); the launches traced: 4430 us -> 1090 us
  local copies, waits for them, and re-layouts: 2190 us -> 123 us
  waiting for transfers between devices: 1130 us -> 304 us
  matrix products: 467 us -> 155 us
  other arithmetic: 310 us -> 62.9 us
  Pallas kernels: 0 us -> 218 us
  blocking collectives: 313 us -> 122 us
  starting transfers between devices: 0.7 us -> 87.7 us
    unnamed x348 -> x129, local copies, waits for them, and re-layouts: 1000 us -> 109 us
    rev x6 -> x0, local copies, waits for them, and re-layouts: 655 us -> none  [diagonal_sums(): flipped = block[:, :, ::-1]]
    reduce_scatter x5 -> x4, waiting for transfers between devices: 512 us -> 134 us  [the longest x1 76.3 us: per_device(): lax.psum_scatter(grad_first.astype(BF), ('core', 'zl'), scatter_dimension...]
    reshape x14 -> x7, local copies, waits for them, and re-layouts: 327 us -> 3.03 us  [the longest x1 1.31 us: per_device(): full_gain = small_sum[BUCKETS * H:BUCKETS * H + 2 * width].reshape(2, width)]
    dot_general x50 -> x14, matrix products: 467 us -> 155 us  [the longest x1 41.4 us: per_device(): jnp.einsum('nd,zdf->znf', a_second, up_full, preferred_element_type=F32)]
    all_gather x7 -> x4, waiting for transfers between devices: 359 us -> 108 us  [the longest x1 59.7 us: per_device(): lax.all_gather(lax.ppermute(tokens, ('core', 'zh'), swap), ('core', 'zl')...]
    pallas_call x0 -> x4, Pallas kernels: none -> 218 us  [the longest x1 84.3 us: attend_back(): pl.pallas_call(attend_back_kernel, grid=(heads,), in_specs=[pl.BlockSpec(...]
    unnamed x22 -> x16, waiting for transfers between devices: 258 us -> 53.7 us
  transfers between devices with their start and end apart: 17 -> 17, of which waited for: 10 -> 9; matrix products, arithmetic and copies ran while one was open for 58% -> 16% of each run, Pallas kernels for 0% -> 20%
where the time goes in v1:
time: 1110 us; the launch traced here: 1090 us
  waiting for transfers between devices  304 us (27%)
  Pallas kernels  218 us (20%)
  matrix products  155 us (14%)
  local copies, waits for them, and re-layouts  123 us (11%)
  blocking collectives  122 us (11%)
  starting transfers between devices  87.7 us (8%)
  other arithmetic  62.9 us (6%)
  between operations  21.7 us (2%)
    unnamed x129, local copies, waits for them, and re-layouts  109 us
    pallas_call x1, Pallas kernels, attend_back(): pl.pallas_call(attend_back_kernel, grid=(heads,), in_specs=[pl.BlockSpec(...  84.3 us
    ppermute x1, starting transfers between devices, per_device(): lax.ppermute(w_qkv.astype(BF), ALL, to_heads)  77.6 us
    reduce_scatter x1, waiting for transfers between devices, per_device(): lax.psum_scatter(grad_first.astype(BF), ('core', 'zl'), scatter_dimension...  76.3 us
    pallas_call x2, Pallas kernels, exchange(): pl.pallas_call(functools.partial(exchange_kernel, shape, to_owners), out_...  72.8 us
    pallas_call x1, Pallas kernels, attend(): pl.pallas_call(attend_kernel, grid=(heads,), in_specs=[pl.BlockSpec(memor...  61.2 us
    all_gather x1, waiting for transfers between devices, per_device(): lax.all_gather(lax.ppermute(tokens, ('core', 'zh'), swap), ('core', 'zl')...  59.7 us
    reduce_scatter x3, waiting for transfers between devices, scatter(): lax.psum_scatter(part, TENSOR, scatter_dimension=0, tiled=False).astype(F32)  57.9 us
  transfers between devices with their start and end apart: 17, of which 9 were waited for; matrix products, arithmetic and copies ran while one was open for 16% of the time, Pallas kernels for 20%

profile of v1, /device:TPU:8, one launch (start us, length us, event | category | flops | bytes accessed | tf_op | source)
XLA Modules:
  0.0 1094.0 jit_solution(14526976890364569252)
XLA Ops:
  16.9 77.6 %collective-permute-start.2 = (bf16[3,128,256]{1,2,0:T(8,128)(2,1)S(1)}, bf16[3,128,256]{1,2,0:T(8,128)(2,1)S(1)}, u32[]{:S(2)}, u32[]{:S(2)}) collective-permute-start(bf16[3,128,256]{1,2,0:T(8,128)(2,1)S(1)} %convert_element_type.99), channel_id=1, source_target_pairs={{0,0},{1,4},{2,1},{3,5},{4,2},{5,6},{6,3},{7,7},{8,8},{9,12},{10,9... | collective-permute-start | bytes 589832 | tf_op jit(solution)/shard_map/ppermute | solution.py:451
  94.5 3.2 collective-permute-done.2
  99.0 2.6 collective-permute-start
  102.0 40.4 %all-reduce.1 = f32[4608]{0:T(1024)S(1)} all-reduce(f32[4608]{0:T(1024)S(1)} %maximum_dynamic-update-slice_fusion), channel_id=2, replica_groups=mesh['xy'=4,'core'=2,'zh'=2,'zl'=2] {'xy','core','zh','zl'}, use_global_device_ids=true, to_apply=%add.1 | all-reduce | flops 4608 | bytes 36864
  144.8 59.7 %all-gather.6.cloned.1.call-done = bf16[3072,1024]{1,0:T(8,128)(2,1)} async-done(((bf16[768,1024]{1,0:T(8,128)(2,1)}), bf16[3072,1024]{1,0:T(8,128)(2,1)}) %all-gather.6.cloned.1.call-update) | async-done | bytes 6291472 | tf_op jit(solution)/shard_map/all_gather | solution.py:475
  204.6 3.8 convert_reduce_fusion
  211.3 48.6 %all-gather.8.cloned.1.call-done = bf16[3,1024,256]{1,2,0:T(8,128)(2,1)} async-done(((bf16[3,128,256]{1,2,0:T(8,128)(2,1)}), bf16[3,1024,256]{1,2,0:T(8,128)(2,1)}) %all-gather.8.cloned.1.call-update) | async-done | bytes 1572880 | tf_op jit(solution)/shard_map/all_gather | solution.py:450
  259.9 9.8 convolution_convert_fusion
  269.7 61.2 %attend.1 = (bf16[256,3072]{1,0:T(8,128)(2,1)}, f32[4,1,3072]{2,1,0:T(1,128)}) custom-call(s32[1]{0:T(128)} %bitcast.258, f32[4,1,3584]{2,1,0:T(1,128)} %broadcast_in_dim.8.pattern_ref, bf16[768,3072]{1,0:T(8,128)(2,1)} %bitcast.260, bf16[768,3072]{1,0:T(8,128)(2,1)} %bitcast.261, bf16[768,3072]{1,0:T(8,128)(2,1)} %bitcast.262), custom_call_target="tpu_custom_call" | custom-call | flops 30198988800 | bytes 6291456 | tf_op jit(solution)/shard_map/attend/pallas_call | solution.py:125
  330.8 38.3 %exchange.2 = bf16[4,256,768]{2,1,0:T(8,128)(2,1)} custom-call(bf16[256,3072]{1,0:T(8,128)(2,1)} %get-tuple-element.31.src_ref.o_ref), custom_call_target="tpu_custom_call" | custom-call | tf_op jit(solution)/shard_map/exchange/pallas_call | solution.py:364
  369.1 4.0 fusion.116
  373.6 41.4 %fusion.17 = (bf16[4,768,1024]{1,2,0:T(8,128)(2,1)}, f32[4,768,1024]{1,2,0:T(8,128)}, f32[4,1024,768]{2,1,0:T(8,128)}) fusion(f32[768,1024]{1,0:T(8,128)S(1)} %get-tuple-element.179, f32[1024]{0:T(1024)S(1)} %add.213, f32[1024]{0:T(1024)S(1)} %mul.546, f32[768]{0:T(1024)S(1)} %add_rsqrt_fusion.2, f32[768]{0:T(1024)S(1)} %broadcast_multiply_fusion.6, ...), kind=kOutput, calls=%fused_computation.29 | convolution fusion | flops 6650855424 | bytes 43005952 | tf_op jit(solution)/shard_map/nd,zdf->znf/dot_general | solution.py:507
  415.0 19.4 %fusion.14 = bf16[4,768,1024]{1,2,0:T(8,128)(2,1)} fusion(f32[4,768,1024]{1,2,0:T(8,128)} %get-tuple-element.157, f32[4,1024,768]{2,1,0:T(8,128)} %get-tuple-element.180, bf16[4,1024,2304]{2,1,0:T(8,128)(2,1)} %all-gather.12.cloned.1.call-done, bf16[768,1024]{1,0:T(8,128)(2,1)} %param.26), kind=kOutput, calls=%fused_computation.21 | convolution fusion | flops 6486491136 | bytes 41418752 | tf_op jit(solution)/shard_map/nd,zdf->znf/dot_general | solution.py:513
  434.4 13.0 %fusion.51 = (f32[1024]{0:T(1024)S(1)}, f32[768]{0:T(1024)S(1)}, f32[768]{0:T(1024)S(1)}, f32[1024]{0:T(1024)}, f32[768,1024,1]{1,0,2:T(8,128)S(1)}) fusion(f32[768,1024]{1,0:T(8,128)S(1)} %copy-done.5, f32[768]{0:T(1024)S(1)} %add_rsqrt_fusion.2, f32[768]{0:T(1024)S(1)} %broadcast_multiply_fusion.6, f32[1024]{0:T(1024)S(1)} %mul.546, ...), kind=kOutput, calls=%fused_computation.73 | convolution fusion | flops 6449524736 | bytes 20996096 | tf_op jit(solution)/shard_map/znf,zdf->nd/dot_general | solution.py:516
  448.8 3.1 convert_bitcast_fusion.2
  451.9 4.3 copy.138
  456.2 3.4 copy.146
  459.6 12.7 %convert_bitcast_fusion.1 = bf16[4,1024,1024]{1,2,0:T(8,128)(2,1)} fusion(bf16[4,768,1024]{1,2,0:T(8,128)(2,1)} %fusion.14, f32[768,1024]{1,0:T(8,128)} %copy-done.4, f32[1024]{0:T(1024)S(1)} %add.213, f32[1024]{0:T(1024)S(1)} %mul.546, f32[768]{0:T(1024)S(1)} %add_rsqrt_fusion.2, f32[768]{0:T(1024)S(1)} %broadcast_multiply_fusion.6), kind=kOutput, calls=%fused_computation.44 | convolution fusion | flops 6450577408 | bytes 17840128 | tf_op jit(solution)/shard_map/nd,znf->zdf/dot_general | solution.py:515
  472.4 15.1 %copy.140 = bf16[4,1024,1024]{2,0,1:T(4,128)(2,1)} copy(bf16[4,1024,1024]{1,2,0:T(8,128)(2,1)} %convert_bitcast_fusion.1) | data formatting | bytes 16777216
  487.4 12.3 %copy.147 = bf16[128,8,4,1024]{3,1,2,0:T(8,128)(2,1)} copy(bf16[128,8,4,1024]{3,2,1,0:T(4,128)(2,1)} %bitcast.243) | data formatting | bytes 16777216
  499.7 11.7 %convert_bitcast_fusion = bf16[4,1024,1024]{1,2,0:T(8,128)(2,1)} fusion(bf16[4,768,1024]{1,2,0:T(8,128)(2,1)} %get-tuple-element.156, bf16[768,1024]{1,0:T(8,128)(2,1)} %param.26), kind=kOutput, calls=%fused_computation.43 | convolution fusion | flops 6446645248 | bytes 16252928 | tf_op jit(solution)/shard_map/nd,znf->zdf/dot_general | solution.py:512
  511.5 15.7 %copy.142 = bf16[4,1024,1024]{2,0,1:T(4,128)(2,1)} copy(bf16[4,1024,1024]{1,2,0:T(8,128)(2,1)} %convert_bitcast_fusion) | data formatting | bytes 16777216
  527.1 12.1 %copy.148 = bf16[128,8,4,1024]{3,1,2,0:T(8,128)(2,1)} copy(bf16[128,8,4,1024]{3,2,1,0:T(4,128)(2,1)} %bitcast.244) | data formatting | bytes 16777216
  539.3 4.6 fusion.67.src_ref
  543.9 34.5 %exchange.3.do_ref = bf16[256,3072]{1,0:T(8,128)(2,1)} custom-call(bf16[4,256,768]{2,1,0:T(8,128)(2,1)} %fusion.67.src_ref), custom_call_target="tpu_custom_call" | custom-call | tf_op jit(solution)/shard_map/exchange/pallas_call | solution.py:364
  578.5 84.3 %attend_back.1 = (bf16[256,3072]{1,0:T(8,128)(2,1)}, bf16[256,3072]{1,0:T(8,128)(2,1)}, bf16[256,3072]{1,0:T(8,128)(2,1)}, f32[4,1,3584]{2,1,0:T(1,128)}) custom-call(s32[1]{0:T(128)} %bitcast.259, f32[4,1,3584]{2,1,0:T(1,128)} %broadcast_in_dim.8.pattern_ref, bf16[768,3072]{1,0:T(8,128)(2,1)} %bitcast.263, bf16[768,3072]{1,0:T(8,128)(2,1)} %bitcast.264, ...), custom_call_target="tpu_custom_call" | custom-call | flops 45298483200 | bytes 12582912 | tf_op jit(solution)/shard_map/attend_back/pallas_call | solution.py:215
  662.8 11.9 %bitcast_reduce_fusion = (f32[1024]{0:T(1024)}, f32[1024]{0:T(1024)}, bf16[3072,1024,1]{1,0,2:T(8,128)(2,1)}) fusion(f32[3072]{0:T(1024)S(1)} %copy-done.30, f32[3072]{0:T(1024)S(1)} %copy-done.24, bf16[3072,1024]{1,0:T(8,128)(2,1)} %all-gather.6.cloned.1.call-done, bf16[3,1024,256]{1,2,0:T(8,128)(2,1)S(1)} %copy-done.42, ...), kind=kOutput, calls=%fused_computation.12 | convolution fusion | flops 4858574848 | bytes 18907136 | tf_op jit(solution)/shard_map/cet,cde->td/dot_general | solution.py:533
  676.6 9.7 fusion.75
  686.3 3.1 copy.136
  713.0 76.3 %reduce-scatter.17.cloned.1.call-done = bf16[768,1024]{1,0:T(8,128)(2,1)} async-done(((bf16[3072,1024]{1,0:T(8,128)(2,1)}), bf16[768,1024]{1,0:T(8,128)(2,1)}) %reduce-scatter.17.cloned.1.call-update) | async-done | bytes 1572880 | tf_op jit(solution)/shard_map/reduce_scatter | solution.py:538
  789.3 2.3 collective-permute-start.3
  791.6 12.7 %fusion.52 = bf16[768,1024]{1,0:T(8,128)(2,1)} fusion(f32[768,1024]{1,0:T(8,128)} %copy-done.4, bf16[4,768,1024]{1,2,0:T(8,128)(2,1)} %get-tuple-element.156, bf16[4,1024,2304]{2,1,0:T(8,128)(2,1)} %all-gather.12.cloned.1.call-done), kind=kOutput, calls=%fused_computation.75 | convolution fusion | flops 6444023808 | bytes 19398656 | tf_op jit(solution)/shard_map/znf,zdf->nd/dot_general | solution.py:509
  804.3 53.0 %reduce-scatter.25.cloned.1.call-done = bf16[128,768]{1,0:T(8,128)(2,1)} async-done(((bf16[1024,768]{1,0:T(8,128)(2,1)}), bf16[128,768]{1,0:T(8,128)(2,1)}) %reduce-scatter.25.cloned.1.call-update) | async-done | bytes 196624
  860.8 2.4 collective-permute-start.4
  865.9 4.3 collective-permute-done.4
  871.5 5.9 reduce-scatter.19.cloned.1.call-done
  880.3 25.7 %reduce-scatter.21.cloned.1.call-done = bf16[1,128,1024]{1,2,0:T(8,128)(2,1)} async-done(((bf16[4,128,1024]{1,2,0:T(8,128)(2,1)}), bf16[1,128,1024]{1,2,0:T(8,128)(2,1)}) %reduce-scatter.21.cloned.1.call-update) | async-done | bytes 262160 | tf_op jit(solution)/shard_map/reduce_scatter | solution.py:549
  907.7 26.4 %reduce-scatter.23.cloned.1.call-done = bf16[1,128,1024]{1,2,0:T(8,128)(2,1)} async-done(((bf16[4,128,1024]{1,2,0:T(8,128)(2,1)}), bf16[1,128,1024]{1,2,0:T(8,128)(2,1)}) %reduce-scatter.23.cloned.1.call-update) | async-done | bytes 262160 | tf_op jit(solution)/shard_map/reduce_scatter | solution.py:549
  935.8 3.2 pad_maximum_fusion.9
  940.2 41.9 %all-reduce.3 = (f32[6]{0:T(128)}, f32[4608]{0:T(1024)}) all-reduce(f32[6]{0:T(128)} %pad_maximum_fusion.9, f32[4608]{0:T(1024)} %constant_dynamic-update-slice_fusion), channel_id=1, replica_groups=mesh['xy'=4,'core'=2,'zh'=2,'zl'=2] {'xy','core','zh','zl'}, use_global_device_ids=true, to_apply=%region_22.23 | all-reduce | flops 4614 | bytes 36912 | tf_op jit(solution)/shard_map/psum | solution.py:582
  998.5 3.5 multiply_reduce_fusion.4
  1002.0 2.5 multiply_reduce_fusion.9
  1004.5 3.9 concatenate.44
  1008.4 2.9 multiply_reduce_fusion.6
  1011.3 3.4 multiply_reduce_fusion.3
  1014.7 3.9 concatenate.45
  1018.6 3.7 fusion.49
  1022.3 39.5 %all-reduce.2 = (f32[11]{0:T(128)S(1)}, f32[11]{0:T(128)S(1)}) all-reduce(f32[11]{0:T(128)} %concatenate.45, f32[11]{0:T(128)} %concatenate.44), channel_id=1, replica_groups=mesh['xy'=4,'core'=2,'zh'=2,'zl'=2] {'xy','core','zh','zl'}, use_global_device_ids=true, to_apply=%region_47.48 | all-reduce | flops 22 | bytes 176 | tf_op jit(solution)/shard_map/psum | solution.py:591
  (223 shorter events, 93.9 us)
Async XLA Ops:
  7.2 91.8 %copy-start.41 = (s32[1,2]{1,0:T(1,128)S(1)}, s32[1,2]{1,0:T(1,128)}, u32[]{:S(2)}) copy-start(s32[1,2]{1,0:T(1,128)} %param.27) | copy-start | bytes 28
  7.2 94.5 %copy-start.37 = (f32[2,32]{1,0:T(2,128)S(1)}, f32[2,32]{1,0:T(2,128)}, u32[]{:S(2)}) copy-start(f32[2,32]{1,0:T(2,128)} %param.34) | copy-start | bytes 772
  7.2 94.6 %copy-start.35 = (f32[2,32]{1,0:T(2,128)S(1)}, f32[2,32]{1,0:T(2,128)}, u32[]{:S(2)}) copy-start(f32[2,32]{1,0:T(2,128)} %param.35) | copy-start | bytes 772
  7.2 94.6 %copy-start.31 = (f32[16]{0:T(128)S(1)}, f32[16]{0:T(128)}, u32[]{:S(2)}) copy-start(f32[16]{0:T(128)} %param.33) | copy-start | bytes 196
  7.2 135.9 %copy-start.43 = (s32[3072]{0:T(1024)S(1)}, s32[3072]{0:T(1024)}, u32[]{:S(2)}) copy-start(s32[3072]{0:T(1024)} %param.28) | copy-start | bytes 36868
  7.3 91.2 %all-gather.10.cloned.1.call-start = ((), (), s32[]{:S(2)}) async-start(), calls=%async_computation.10 | async-start | bytes 2949120 | tf_op jit(solution)/shard_map/all_gather | solution.py:456
  12.3 192.2 %all-gather.6.cloned.1.call-start = ((), (), s32[]{:S(2)}) async-start(), calls=%async_computation.8 | async-start | bytes 7864320 | tf_op jit(solution)/shard_map/all_gather | solution.py:475
  12.4 2.1 collective-permute-start.1
  15.6 244.2 %all-gather.8.cloned.1.call-start = ((), (), s32[]{:S(2)}) async-start(), calls=%async_computation.9 | async-start | bytes 1769472 | tf_op jit(solution)/shard_map/all_gather | solution.py:450
  16.8 194.4 %copy-start.7 = (f32[3,128,256]{1,2,0:T(8,128)}, f32[3,128,256]{1,2,0:T(8,128)S(1)}, u32[]{:S(2)}) copy-start(f32[3,128,256]{1,2,0:T(8,128)S(1)} %copy.101) | copy-start | bytes 1179652
  16.9 80.8 %collective-permute-start.2 = (bf16[3,128,256]{1,2,0:T(8,128)(2,1)S(1)}, bf16[3,128,256]{1,2,0:T(8,128)(2,1)S(1)}, u32[]{:S(2)}, u32[]{:S(2)}) collective-permute-start(bf16[3,128,256]{1,2,0:T(8,128)(2,1)S(1)} %convert_element_type.99), channel_id=1, source_target_pairs={{0,0},{1,4},{2,1},{3,5},{4,2},{5,6},{6,3},{7,7},{8,8},{9,12},{10,9... | collective-permute-start | bytes 589832 | tf_op jit(solution)/shard_map/ppermute | solution.py:451
  98.4 270.7 %all-gather.12.cloned.1.call-start = ((), (), s32[]{:S(2)}) async-start(), calls=%async_computation.11 | async-start | bytes 21233664 | tf_op jit(solution)/shard_map/all_gather | solution.py:455
  99.0 592.0 %reduce-scatter.27.cloned.1.call-start = ((), (), s32[]{:S(2)}) async-start(), calls=%async_computation.17 | async-start | bytes 2359296
  99.0 45.3 %collective-permute-start = (s32[1,2]{1,0:T(1,128)S(1)}, s32[1,2]{1,0:T(1,128)S(1)}, u32[]{:S(2)}, u32[]{:S(2)}) collective-permute-start(s32[1,2]{1,0:T(1,128)S(1)} %copy-done.41), channel_id=1, source_target_pairs={{0,4},{4,0},{1,5},{5,1},{2,6},{6,2},{3,7},{7,3},{8,12},{12,8},{9,1... | collective-permute-start | bytes 32 | tf_op jit(solution)/shard_map/ppermute | solution.py:478
  143.1 116.8 %copy-start.26 = (f32[1024]{0:T(1024)}, f32[1024]{0:T(1024)S(1)}, u32[]{:S(2)}) copy-start(f32[1024]{0:T(1024)S(1)} %mul.540) | copy-start | bytes 12292
  143.2 116.7 %copy-start.33 = (f32[1024]{0:T(1024)}, f32[1024]{0:T(1024)S(1)}, u32[]{:S(2)}) copy-start(f32[1024]{0:T(1024)S(1)} %add.208) | copy-start | bytes 12292
  209.2 60.5 %copy-start.23 = (f32[3072]{0:T(1024)}, f32[3072]{0:T(1024)S(1)}, u32[]{:S(2)}) copy-start(f32[3072]{0:T(1024)S(1)} %broadcast_multiply_fusion) | copy-start | bytes 36868
  211.3 58.3 %copy-start.29 = (f32[3072]{0:T(1024)}, f32[3072]{0:T(1024)S(1)}, u32[]{:S(2)}) copy-start(f32[3072]{0:T(1024)S(1)} %add_rsqrt_fusion) | copy-start | bytes 36868
  269.6 99.5 %copy-start.1 = (bf16[768,1024]{1,0:T(8,128)(2,1)S(1)}, bf16[768,1024]{1,0:T(8,128)(2,1)}, u32[]{:S(2)}) copy-start(bf16[768,1024]{1,0:T(8,128)(2,1)} %param.25) | copy-start | bytes 4718596
  373.1 41.9 %copy-start.4 = (f32[768,1024]{1,0:T(8,128)}, f32[768,1024]{1,0:T(8,128)S(1)}, u32[]{:S(2)}) copy-start(f32[768,1024]{1,0:T(8,128)S(1)} %get-tuple-element.179) | copy-start | bytes 9437188
  415.0 19.4 %copy-start.5 = (f32[768,1024]{1,0:T(8,128)S(1)}, f32[768,1024]{1,0:T(8,128)}, u32[]{:S(2)}) copy-start(f32[768,1024]{1,0:T(8,128)} %copy-done.4) | copy-start | bytes 9437188
  448.8 90.5 %copy-start.3 = (f32[768,1024]{1,0:T(8,128)}, f32[768,1024]{1,0:T(8,128)S(1)}, u32[]{:S(2)}) copy-start(f32[768,1024]{1,0:T(8,128)S(1)} %multiply_add_fusion) | copy-start | bytes 9437188
  459.6 233.6 %reduce-scatter.29.cloned.1.call-start = ((), (), s32[]{:S(2)}) async-start(), calls=%async_computation.18 | async-start | bytes 9437184
  499.7 209.7 %reduce-scatter.31.cloned.1.call-start = ((), (), s32[]{:S(2)}) async-start(), calls=%async_computation.19 | async-start | bytes 9437184
  539.3 250.1 %reduce-scatter.17.cloned.1.call-start = ((), (), s32[]{:S(2)}) async-start(), calls=%async_computation.12 | async-start | bytes 7864320 | tf_op jit(solution)/shard_map/reduce_scatter | solution.py:538
  578.4 84.3 %copy-start.24 = (f32[3072]{0:T(1024)S(1)}, f32[3072]{0:T(1024)}, u32[]{:S(2)}) copy-start(f32[3072]{0:T(1024)} %copy-done.23) | copy-start | bytes 36868
  578.4 84.3 %copy-start.30 = (f32[3072]{0:T(1024)S(1)}, f32[3072]{0:T(1024)}, u32[]{:S(2)}) copy-start(f32[3072]{0:T(1024)} %copy-done.29) | copy-start | bytes 36868
  578.4 84.3 %copy-start.42 = (bf16[3,1024,256]{1,2,0:T(8,128)(2,1)S(1)}, bf16[3,1024,256]{1,2,0:T(8,128)(2,1)}, u32[]{:S(2)}) copy-start(bf16[3,1024,256]{1,2,0:T(8,128)(2,1)} %all-gather.8.cloned.1.call-done) | copy-start | bytes 4718596
  674.7 182.7 %reduce-scatter.25.cloned.1.call-start = ((), (), s32[]{:S(2)}) async-start(), calls=%async_computation.16 | async-start | bytes 1769472
  690.9 15.6 %copy-start.2 = (bf16[768,1024]{1,0:T(8,128)(2,1)S(1)}, bf16[768,1024]{1,0:T(8,128)(2,1)}, u32[]{:S(2)}) copy-start(bf16[768,1024]{1,0:T(8,128)(2,1)} %param.25) | copy-start | bytes 4718596
  690.9 186.5 %reduce-scatter.19.cloned.1.call-start = ((), (), s32[]{:S(2)}) async-start(), calls=%async_computation.13 | async-start | bytes 327680 | tf_op jit(solution)/shard_map/reduce_scatter | solution.py:549
  693.2 212.9 %reduce-scatter.21.cloned.1.call-start = ((), (), s32[]{:S(2)}) async-start(), calls=%async_computation.14 | async-start | bytes 1310720 | tf_op jit(solution)/shard_map/reduce_scatter | solution.py:549
  696.8 237.3 %reduce-scatter.23.cloned.1.call-start = ((), (), s32[]{:S(2)}) async-start(), calls=%async_computation.15 | async-start | bytes 1310720 | tf_op jit(solution)/shard_map/reduce_scatter | solution.py:549
  713.0 151.6 %copy-start.40 = (f32[1024]{0:T(1024)S(1)}, f32[1024]{0:T(1024)}, u32[]{:S(2)}) copy-start(f32[1024]{0:T(1024)} %get-tuple-element.117) | copy-start | bytes 12292
  789.3 89.5 %collective-permute-start.3 = (bf16[768,1024]{1,0:T(8,128)(2,1)}, bf16[768,1024]{1,0:T(8,128)(2,1)S(1)}, u32[]{:S(2)}, u32[]{:S(2)}) collective-permute-start(bf16[768,1024]{1,0:T(8,128)(2,1)} %reduce-scatter.17.cloned.1.call-done), channel_id=1, source_target_pairs={{0,0},{2,4},{4,2},{6,6},{1,1},{3,5},{5,3},{7,7},{8,8},{10,12},{12,... | collective-permute-start | bytes 4718600 | tf_op jit(solution)/shard_map/ppermute | solution.py:537
  804.3 204.1 %copy-start.8 = (f32[3,128,256]{1,2,0:T(8,128)S(1)}, f32[3,128,256]{1,2,0:T(8,128)}, u32[]{:S(2)}) copy-start(f32[3,128,256]{1,2,0:T(8,128)} %copy-done.7) | copy-start | bytes 1179652
  860.8 9.3 collective-permute-start.4
  1022.2 53.0 %copy-start.10 = (f32[3,128,256]{1,2,0:T(8,128)S(1)}, f32[3,128,256]{1,2,0:T(8,128)}, u32[]{:S(2)}) copy-start(f32[3,128,256]{1,2,0:T(8,128)} %get-tuple-element.154) | copy-start | bytes 1179652
  1022.2 53.9 %copy-start.11 = (f32[3,128,256]{1,2,0:T(8,128)S(1)}, f32[3,128,256]{1,2,0:T(8,128)}, u32[]{:S(2)}) copy-start(f32[3,128,256]{1,2,0:T(8,128)} %get-tuple-element.155) | copy-start | bytes 1179652
  1022.2 55.7 %copy-start.36 = (f32[2,32]{1,0:T(2,128)S(1)}, f32[2,32]{1,0:T(2,128)}, u32[]{:S(2)}) copy-start(f32[2,32]{1,0:T(2,128)} %param.35) | copy-start | bytes 772
  1022.2 55.7 %copy-start.39 = (f32[2,32]{1,0:T(2,128)S(1)}, f32[2,32]{1,0:T(2,128)}, u32[]{:S(2)}) copy-start(f32[2,32]{1,0:T(2,128)} %get-tuple-element.135) | copy-start | bytes 772
  1022.3 57.0 %copy-start.38 = (f32[2,32]{1,0:T(2,128)S(1)}, f32[2,32]{1,0:T(2,128)}, u32[]{:S(2)}) copy-start(f32[2,32]{1,0:T(2,128)} %param.34) | copy-start | bytes 772
  1022.3 58.3 %copy-start.32 = (f32[16]{0:T(128)S(1)}, f32[16]{0:T(128)}, u32[]{:S(2)}) copy-start(f32[16]{0:T(128)} %param.33) | copy-start | bytes 196
  1022.3 60.6 %copy-start.9 = (f32[1024,128]{1,0:T(8,128)S(1)}, f32[1024,128]{1,0:T(8,128)}, u32[]{:S(2)}) copy-start(f32[1024,128]{1,0:T(8,128)} %param.32) | copy-start | bytes 1572868
  1022.3 60.6 %copy-start.13 = (f32[1024,128]{1,0:T(8,128)S(1)}, f32[1024,128]{1,0:T(8,128)}, u32[]{:S(2)}) copy-start(f32[1024,128]{1,0:T(8,128)} %get-tuple-element.146) | copy-start | bytes 1572868
  1022.3 60.5 %copy-start.14 = (f32[1024,128]{1,0:T(8,128)S(1)}, f32[1024,128]{1,0:T(8,128)}, u32[]{:S(2)}) copy-start(f32[1024,128]{1,0:T(8,128)} %get-tuple-element.147) | copy-start | bytes 1572868
  1022.3 61.6 %copy-start.19 = (f32[256,128]{1,0:T(8,128)S(1)}, f32[256,128]{1,0:T(8,128)}, u32[]{:S(2)}) copy-start(f32[256,128]{1,0:T(8,128)} %param.30) | copy-start | bytes 393220
  1022.3 61.6 %copy-start.21 = (f32[256,128]{1,0:T(8,128)S(1)}, f32[256,128]{1,0:T(8,128)}, u32[]{:S(2)}) copy-start(f32[256,128]{1,0:T(8,128)} %get-tuple-element.151) | copy-start | bytes 393220
  (16 other events, 83.5 us)
Sparse Core Ops, SparseCore 0:
  12.5 69.4 all-gather.9
  84.1 120.4 all-gather.5
  207.3 52.4 all-gather.7
  261.6 100.9 all-gather.11
  459.7 43.2 reduce-scatter.26
  506.7 71.2 reduce-scatter.28
  581.4 71.3 reduce-scatter.30
  674.8 114.4 reduce-scatter.16
  794.0 63.2 reduce-scatter.24
  860.1 17.2 reduce-scatter.18
  879.7 26.2 reduce-scatter.20
  908.3 25.7 reduce-scatter.22

commit v2 on v1

v2 whole, which is shorter than its diff:
```python
import functools

import jax
import jax.numpy as jnp
from jax import lax
from jax.experimental import pallas as pl
from jax.experimental.pallas import tpu as pltpu
from jax.sharding import Mesh
from jax.sharding import PartitionSpec as P

H = 16
DH = 64
BUCKETS = 32
BLK = 512
NEG = -1e30
LOG2E = 1.4426950408889634
F32 = jnp.float32
BF = jnp.bfloat16
MESH = pl.DeviceIdType.MESH
HIGHEST = lax.Precision.HIGHEST
ALL = ("xy", "core", "zh", "zl")
DP = ("xy", "core")
TENSOR = ("zh", "zl")


def dot(left, right, left_dim, right_dim):
    return lax.dot_general(
        left, right, (((left_dim,), (right_dim,)), ((), ())), preferred_element_type=F32
    )


def make_slab(pattern, slab):
    width = slab.shape[1]
    slab[0:8, :] = pltpu.roll(jnp.broadcast_to(pattern, (8, width)), 0, 1, stride=1, stride_axis=0)
    done = 8
    while done < slab.shape[0]:
        slab[done : 2 * done, :] = pltpu.roll(slab[0:done, :], done, 1)
        done *= 2


def fold_slab(slab):
    width = slab.shape[1]
    half = slab.shape[0] // 2
    while half >= 8:
        slab[0:half, :] = slab[0:half, :] + pltpu.roll(slab[half : 2 * half, :], width - half, 1)
        half //= 2
    total = slab[0:1, :]
    for row in range(1, 8):
        total = total + pltpu.roll(slab[row : row + 1, :], width - row, 1)
    return total


def split_three(values):
    high = values.astype(BF).astype(F32)
    rest = values - high
    middle = rest.astype(BF).astype(F32)
    return high, middle, (rest - middle).astype(BF).astype(F32)


def put_queries(queries, split, minus, tok, dst):
    scaled = queries.astype(F32) * (DH**-0.5 * LOG2E)
    high = scaled.astype(BF)
    dst[0:DH, :] = high
    dst[DH : 2 * DH, :] = (scaled - high.astype(F32)).astype(BF)
    position = lax.broadcasted_iota(jnp.int32, (16, tok), 1)
    row = lax.broadcasted_iota(jnp.int32, (16, tok), 0)
    extra = jnp.where((row == 0) & (position >= split), 1.0, 0.0)
    if minus is not None:
        first, second, third = split_three(minus)
        extra = jnp.where(
            row == 1, first, jnp.where(row == 2, second, jnp.where(row == 3, third, extra))
        )
    dst[2 * DH : 2 * DH + 16, :] = extra.astype(BF)


def put_keys(keys, split, tok, dst):
    for start in range(0, tok, BLK):
        position = start + lax.broadcasted_iota(jnp.int32, (16, BLK), 1)
        row = lax.broadcasted_iota(jnp.int32, (16, BLK), 0)
        extra = jnp.where(
            row == 0, jnp.where(position < split, NEG, 0.0), jnp.where(row < 4, 1.0, 0.0)
        )
        block = keys[:, start : start + BLK].astype(F32)
        whole = jnp.concatenate([block, block, extra], axis=0)
        dst[start : start + BLK, :] = whole.T.astype(BF)


def block_at(index):
    return pl.ds(pl.multiple_of(index * BLK, BLK), BLK)


def attend_kernel(
    shape, split_ref, pattern_ref, q_ref, k_ref, v_ref, out_ref, rows_ref, lse_ref,
    slab, kx, qx, outs, local_sem, send_sem, recv_sem,
):
    head = pl.program_id(0)
    tok = q_ref.shape[1]
    split = split_ref[0]
    trade = Trade(shape, tok)

    @pl.when(head == 0)
    def _():
        greet_column(shape)

    make_slab(pattern_ref[0], slab)
    put_queries(q_ref[...], split, None, tok, qx)
    put_keys(k_ref, split, tok, kx)

    def step(i, j, top, total, out):
        scores = dot(kx[block_at(j), :], qx[:, block_at(i)], 1, 0) + slab[:, block_at(i - j)]
        new_top = jnp.maximum(top, jnp.max(scores, axis=0, keepdims=True))
        weights = jnp.exp2(scores - new_top)
        scale = jnp.exp2(top - new_top)
        total = total * scale + jnp.sum(weights, axis=0, keepdims=True)
        out = out * scale + dot(v_ref[:, block_at(j)], weights.astype(BF), 1, 0)
        return new_top, total, out

    def row(i, carry):
        start = (
            jnp.full((1, BLK), NEG, F32),
            jnp.zeros((1, BLK), F32),
            jnp.zeros((DH, BLK), F32),
        )
        top, total, out = lax.fori_loop(0, i + 1, lambda t, c: step(i, i - t, *c), start)
        outs[head, :, block_at(i)] = (out / total).astype(BF)
        lse_ref[0, :, block_at(i)] = top + jnp.log2(total)
        return carry

    lax.fori_loop(0, tok // BLK, row, 0)

    def keep(h):
        return pltpu.make_async_copy(outs.at[h], out_ref.at[h], local_sem.at[0, h])

    def piece(h, n):
        return outs.at[h, :, pl.ds(pl.multiple_of(n * trade.rows, trade.rows), trade.rows)]

    def slot(h, n):
        return rows_ref.at[n, h]

    keep(head).start()
    trade.give(head, piece, slot, trade.owner, trade.head, local_sem.at[1, head], send_sem, recv_sem)

    @pl.when(head == pl.num_programs(0) - 1)
    def _():
        for h in range(rows_ref.shape[1]):
            keep(h).wait()
            trade.given(h, piece, slot, trade.owner, trade.head, local_sem.at[1, h], send_sem, recv_sem)
            trade.take(h, piece, slot, trade.header, send_sem, recv_sem)


def attend(shape, qkv, pattern, split, heads):
    tok = qkv.shape[1]
    width = pattern.shape[-1]
    parts = shape["zh"] * shape["zl"]
    dma = pltpu.SemaphoreType.DMA
    return pl.pallas_call(
        functools.partial(attend_kernel, shape),
        grid=(heads,),
        in_specs=[
            pl.BlockSpec(memory_space=pltpu.SMEM),
            pl.BlockSpec((1, 1, width), lambda h: (h, 0, 0)),
            pl.BlockSpec((DH, tok), lambda h: (h, 0)),
            pl.BlockSpec((DH, tok), lambda h: (h + heads, 0)),
            pl.BlockSpec((DH, tok), lambda h: (h + 2 * heads, 0)),
        ],
        out_specs=[
            pl.BlockSpec(memory_space=pl.ANY),
            pl.BlockSpec(memory_space=pl.ANY),
            pl.BlockSpec((1, 1, tok), lambda h: (h, 0, 0)),
        ],
        out_shape=[
            jax.ShapeDtypeStruct((heads, DH, tok), BF),
            jax.ShapeDtypeStruct((parts, heads, DH, tok // parts), BF),
            jax.ShapeDtypeStruct((heads, 1, tok), F32),
        ],
        scratch_shapes=[
            pltpu.VMEM((BLK, width), F32),
            pltpu.VMEM((tok, 2 * DH + 16), BF),
            pltpu.VMEM((2 * DH + 16, tok), BF),
            pltpu.VMEM((heads, DH, tok), BF),
            dma((2, heads)),
            dma((heads, parts)),
            dma((heads, parts)),
        ],
        compiler_params=pltpu.CompilerParams(
            vmem_limit_bytes=56 * 2**20, collective_id=0, has_side_effects=True
        ),
        name="attend",
    )(split, pattern, qkv, qkv, qkv)


def attend_back_kernel(
    shape, first_head, split_ref, pattern_ref, q_ref, k_ref, v_ref, o_ref, lse_ref, given_ref,
    grads_ref, dpattern_ref,
    slab, dslab, kx, qx, vx, dox, qn, don, dk, dv, taken,
    local_sem, in_send, in_recv,
):
    head = pl.program_id(0)
    tok = q_ref.shape[1]
    split = split_ref[0]
    trade = Trade(shape, tok)
    heads = taken.shape[0]

    def in_piece(h, n):
        return given_ref.at[n, first_head + h]

    def in_slot(h, n):
        return taken.at[h, :, pl.ds(pl.multiple_of(n * trade.rows, trade.rows), trade.rows)]

    @pl.when(head == 0)
    def _():
        greet_column(shape)
        for h in range(heads):
            trade.give(
                h, in_piece, in_slot, trade.header, trade.row, local_sem.at[h], in_send, in_recv
            )

    make_slab(pattern_ref[0], slab)
    put_queries(q_ref[...], split, -lse_ref[0], tok, qx)
    put_keys(k_ref, split, tok, kx)
    dslab[...] = jnp.zeros_like(dslab)
    dk[...] = jnp.zeros_like(dk)
    dv[...] = jnp.zeros_like(dv)
    row = lax.broadcasted_iota(jnp.int32, (16, BLK), 0)
    ones = jnp.where(row < 3, 1.0, 0.0)
    trade.given(
        head, in_piece, in_slot, trade.header, trade.row, local_sem.at[head], in_send, in_recv
    )
    trade.take(head, in_piece, in_slot, trade.owner, in_send, in_recv)
    for start in range(0, tok, BLK):
        here = slice(start, start + BLK)
        low_grad = taken[head, :, here]
        grad = low_grad.astype(F32)
        inner = jnp.sum(grad * o_ref[0, :, here].astype(F32), axis=0, keepdims=True)
        first, second, third = split_three(-inner)
        extra = jnp.where(
            row == 0, first, jnp.where(row == 1, second, jnp.where(row == 2, third, 0.0))
        )
        dox[0:DH, here] = low_grad
        dox[DH : DH + 16, here] = extra.astype(BF)
        vx[here, :] = jnp.concatenate([v_ref[:, here].astype(F32), ones], axis=0).T.astype(BF)
        both = jnp.concatenate([q_ref[:, here].astype(F32), grad], axis=0).T
        qn[here, :] = both[:, 0:DH].astype(BF)
        don[here, :] = both[:, DH : 2 * DH].astype(BF)

    def tile(i, j):
        qs, ks, diagonal = block_at(i), block_at(j), block_at(i - j)
        shares = jnp.exp2(dot(kx[ks, :], qx[:, qs], 1, 0) + slab[:, diagonal])
        grad_scores = shares * dot(vx[ks, :], dox[:, qs], 1, 0)
        dslab[:, diagonal] += grad_scores
        low = grad_scores.astype(BF)
        dv[ks, :] += dot(shares.astype(BF), don[qs, :], 1, 0)
        dk[ks, :] += dot(low, qn[qs, :], 1, 0)
        return dot(k_ref[:, ks], low, 1, 0)

    def query_row(i, carry):
        total = lax.fori_loop(
            0, i + 1, lambda t, c: c + tile(i, i - t), jnp.zeros((DH, BLK), F32)
        )
        grads_ref[0, 0, :, block_at(i)] = (total * DH**-0.5).astype(BF)
        return carry

    lax.fori_loop(0, tok // BLK, query_row, 0)
    for start in range(0, tok, BLK):
        here = slice(start, start + BLK)
        grads_ref[1, 0, :, here] = (dk[here, :] * DH**-0.5).T.astype(BF)
        grads_ref[2, 0, :, here] = dv[here, :].T.astype(BF)
    dpattern_ref[0] = fold_slab(dslab)


def attend_back(shape, qkv, out, given, lse, pattern, split, heads, first_head, count, collective_id):
    tok = qkv.shape[1]
    width = pattern.shape[-1]
    parts = shape["zh"] * shape["zl"]
    anywhere = pl.BlockSpec(memory_space=pl.ANY)
    dma = pltpu.SemaphoreType.DMA
    return pl.pallas_call(
        functools.partial(attend_back_kernel, shape, first_head),
        grid=(count,),
        in_specs=[
            pl.BlockSpec(memory_space=pltpu.SMEM),
            pl.BlockSpec((1, 1, width), lambda h: (first_head + h, 0, 0)),
            pl.BlockSpec((DH, tok), lambda h: (first_head + h, 0)),
            pl.BlockSpec((DH, tok), lambda h: (first_head + h + heads, 0)),
            pl.BlockSpec((DH, tok), lambda h: (first_head + h + 2 * heads, 0)),
            pl.BlockSpec((1, DH, tok), lambda h: (first_head + h, 0, 0)),
            pl.BlockSpec((1, 1, tok), lambda h: (first_head + h, 0, 0)),
            anywhere,
        ],
        out_specs=[
            pl.BlockSpec((3, 1, DH, tok), lambda h: (0, h, 0, 0)),
            pl.BlockSpec((1, 1, width), lambda h: (h, 0, 0)),
        ],
        out_shape=[
            jax.ShapeDtypeStruct((3, count, DH, tok), BF),
            jax.ShapeDtypeStruct((count, 1, width), F32),
        ],
        scratch_shapes=[
            pltpu.VMEM((BLK, width), F32),
            pltpu.VMEM((BLK, width), F32),
            pltpu.VMEM((tok, 2 * DH + 16), BF),
            pltpu.VMEM((2 * DH + 16, tok), BF),
            pltpu.VMEM((tok, DH + 16), BF),
            pltpu.VMEM((DH + 16, tok), BF),
            pltpu.VMEM((tok, DH), BF),
            pltpu.VMEM((tok, DH), BF),
            pltpu.VMEM((tok, DH), F32),
            pltpu.VMEM((tok, DH), F32),
            pltpu.VMEM((count, DH, tok), BF),
            dma((count,)),
            dma((count, parts)),
            dma((count, parts)),
        ],
        compiler_params=pltpu.CompilerParams(
            vmem_limit_bytes=60 * 2**20, collective_id=collective_id, has_side_effects=True
        ),
        name="attend_back",
    )(split, pattern, qkv, qkv, qkv, out, lse, given)


def place():
    return tuple(lax.axis_index(axis) for axis in ALL)


class Trade:
    def __init__(self, shape, tok):
        self.places = shape["zl"]
        self.parts = shape["zh"] * self.places
        self.rows = tok // self.parts
        self.me = place()
        _, core, zh, zl = self.me
        self.row = zh * self.places + zl
        self.head = zl * 2 + core

    def owner(self, n):
        return (self.me[0], self.me[2], lax.div(n, self.places), lax.rem(n, self.places))

    def header(self, n):
        return (self.me[0], lax.rem(n, 2), self.me[1], lax.div(n, 2))

    def each(self, device_of, local, remote):
        for index in range(self.parts):
            n = jnp.where(self.me[2] == 1, index, self.parts - 1 - index)
            device = device_of(n)
            if local is not None:

                @pl.when(is_same(device, self.me))
                def _():
                    local(n)

            @pl.when(jnp.logical_not(is_same(device, self.me)))
            def _():
                remote(n, device)

    def give(self, h, piece, slot, device_of, mine, local_sem, send_sem, recv_sem):
        def local(n):
            pltpu.make_async_copy(piece(h, n), slot(h, mine), local_sem).start()

        def remote(n, device):
            send(piece(h, n), slot(h, mine), send_sem.at[h, n], recv_sem.at[h, mine], device).start()

        self.each(device_of, local, remote)

    def given(self, h, piece, slot, device_of, mine, local_sem, send_sem, recv_sem):
        def local(n):
            pltpu.make_async_copy(piece(h, n), slot(h, mine), local_sem).wait()

        def remote(n, device):
            send(piece(h, n), slot(h, mine), send_sem.at[h, n], recv_sem.at[h, mine], device).wait_send()

        self.each(device_of, local, remote)

    def take(self, h, piece, slot, device_of, send_sem, recv_sem):
        def remote(n, device):
            send(piece(h, n), slot(h, n), send_sem.at[h, n], recv_sem.at[h, n], device).wait_recv()

        self.each(device_of, None, remote)


def is_same(left, right):
    same = left[0] == right[0]
    for one, other in zip(left[1:], right[1:]):
        same = same & (one == other)
    return same


def column_peers(shape, device):
    xy, core, zh, zl = device
    places = shape["zl"]
    total = 4 * places
    mine = (core * 2 + zh) * places + zl
    for step in range(1, total):
        there = lax.rem(mine + step, total)
        yield step, there, (xy, there // (2 * places), lax.rem(there // places, 2), lax.rem(there, places))


def plane_peers(shape, device):
    xy, core, zh, zl = device
    for step in range(1, shape["xy"]):
        there = lax.rem(xy + step, shape["xy"])
        yield step, there, (there, core, zh, zl)


def greet(shape):
    device = place()
    barrier = pltpu.get_barrier_semaphore()
    peers = [peer for _, _, peer in column_peers(shape, device)]
    peers += [peer for _, _, peer in plane_peers(shape, device)]
    for peer in peers:
        pl.semaphore_signal(barrier, inc=1, device_id=peer, device_id_type=MESH)
    pl.semaphore_wait(barrier, len(peers))


def greet_column(shape):
    barrier = pltpu.get_barrier_semaphore()
    peers = [peer for _, _, peer in column_peers(shape, place())]
    for peer in peers:
        pl.semaphore_signal(barrier, inc=1, device_id=peer, device_id_type=MESH)
    pl.semaphore_wait(barrier, len(peers))


def send(src, dst, send_sem, recv_sem, device):
    return pltpu.make_async_remote_copy(
        src_ref=src, dst_ref=dst, send_sem=send_sem, recv_sem=recv_sem,
        device_id=device, device_id_type=MESH,
    )


CHUNKS = 4


def gather_kernel(
    shape, tokens_ref, wq_ref, small_ref, wide_ref, rows_ref, heads_ref, all_small_ref, all_wide_ref,
    local_sems, in_send, fwd_send, share_send, x_recv, xs_recv,
    z_send, z_recv, p_send, p_recv, s_send, s_recv, w_send, w_recv, q_send, q_recv,
):
    me = place()
    xy, core, zh, zl = me
    places = shape["zl"]
    parts = 2 * places
    columns = shape["xy"]
    z = zh * places + zl
    sibling = (xy, 1 - core, zh, zl)
    size = tokens_ref.shape[0] // (2 * CHUNKS)
    dp = xy * 2 + core
    inside = core == zh
    outside = jnp.logical_not(inside)
    entry = jnp.where(zh < core, 0, places - 1)

    def chunk_of(ref, half, chunk):
        return ref.at[pl.ds(pl.multiple_of((half * CHUNKS + chunk) * size, size), size), :]

    def beside(step):
        there = z + step
        return (xy, core, there // places, lax.rem(there, places))

    greet(shape)

    depth = wq_ref.shape[1]
    head_block = zl * 2 + core

    def depth_of(index, count):
        return heads_ref.at[:, pl.ds(pl.multiple_of(index * depth, depth), count * depth), :]

    def wq_target(half):
        return (xy, lax.rem(z, 2), half, lax.div(z, 2))

    def wq_source(c):
        return (xy, c, lax.div(head_block, places), lax.rem(head_block, places))

    own_wq = pltpu.make_async_copy(wq_ref, depth_of(dp, 1), local_sems.at[1])
    own_small = pltpu.make_async_copy(small_ref, all_small_ref.at[dp, z], local_sems.at[2])
    own_wide = pltpu.make_async_copy(wide_ref, all_wide_ref.at[z], local_sems.at[3])
    own_small.start()
    for n in range(2):

        @pl.when(is_same(wq_target(n), me))
        def _():
            own_wq.start()

        @pl.when(jnp.logical_not(is_same(wq_target(n), me)))
        def _():
            send(wq_ref, depth_of(dp, 1), q_send.at[n], q_recv.at[core], wq_target(n)).start()

    for step in range(1, parts):
        there = lax.rem(z + step, parts)
        device = (xy, core, there // places, lax.rem(there, places))
        send(small_ref, all_small_ref.at[dp, z], z_send.at[step], z_recv.at[z], device).start()

    @pl.when(outside)
    def _():
        for chunk in range(CHUNKS):
            for half in range(2):
                send(
                    chunk_of(tokens_ref, half, chunk), chunk_of(rows_ref.at[z], half, chunk),
                    in_send.at[half, chunk], x_recv.at[z, chunk], (xy, half, core, entry),
                ).start()

    @pl.when(inside)
    def _():
        for chunk in range(CHUNKS):
            send(
                chunk_of(tokens_ref, 1 - core, chunk), chunk_of(rows_ref.at[z], 1 - core, chunk),
                in_send.at[0, chunk], x_recv.at[z, chunk], sibling,
            ).start()
        pltpu.make_async_copy(tokens_ref, rows_ref.at[z], local_sems.at[0]).start()

    def ways(shard):
        from_half, from_place = shard // places, lax.rem(shard, places)
        start = jnp.where(from_half == zh, from_place, jnp.where(from_half < zh, 0, places - 1))
        return (zl >= start) & (zl < places - 1), (zl <= start) & (zl > 0)

    def pass_on(shard, chunk, source):
        mine = chunk_of(rows_ref.at[shard], core, chunk)
        for n, (way, step) in enumerate(zip(ways(shard), (1, -1))):

            @pl.when(way)
            def _():
                send(
                    source, mine, fwd_send.at[n, shard, chunk], x_recv.at[shard, chunk],
                    (xy, core, zh, zl + step),
                ).start()

    def share(shard, chunk, source):
        mine = chunk_of(rows_ref.at[shard], core, chunk)
        send(source, mine, share_send.at[shard, chunk], xs_recv.at[shard, chunk], sibling).start()

    def got(shard, chunk):
        mine = chunk_of(rows_ref.at[shard], core, chunk)
        send(mine, mine, share_send.at[shard, chunk], x_recv.at[shard, chunk], sibling).wait_recv()

    @pl.when(inside)
    def _():
        for chunk in range(CHUNKS):
            mine = chunk_of(tokens_ref, core, chunk)
            pass_on(z, chunk, mine)
            share(z, chunk, mine)

    own_wide.start()
    for n, step in enumerate((1, -1)):

        @pl.when((z + step >= 0) & (z + step < parts))
        def _():
            send(
                wide_ref, all_wide_ref.at[z], w_send.at[n, z], w_recv.at[z], beside(step)
            ).start()

    @pl.when(outside)
    def _():
        for chunk in range(CHUNKS):
            got(z, chunk)
            pass_on(z, chunk, chunk_of(rows_ref.at[z], core, chunk))

    own_small.wait()
    for step in range(1, parts):
        there = lax.rem(z + step, parts)
        send(small_ref, all_small_ref.at[dp, there], z_send.at[step], z_recv.at[there], sibling).wait_recv()
    for c in range(2):

        @pl.when(is_same(wq_source(c), me))
        def _():
            own_wq.wait()

        @pl.when(jnp.logical_not(is_same(wq_source(c), me)))
        def _():
            here = depth_of(xy * 2 + c, 1)
            send(here, here, q_send.at[0], q_recv.at[c], wq_source(c)).wait_recv()

    def arrays_at(column):
        return depth_of(column * 2, 2), all_small_ref.at[column * 2 + core]

    for step, there, device in plane_peers(shape, me):
        for n, ref in enumerate(arrays_at(xy)):
            send(ref, ref, p_send.at[n, step], p_recv.at[n, xy], device).start()
    ref = all_small_ref.at[dp]
    send(ref, ref, s_send.at[xy], s_recv.at[xy], sibling).start()

    for distance in range(1, parts):
        for chunk in range(CHUNKS):
            for shard in (z + distance, z - distance):

                @pl.when((shard >= 0) & (shard < parts))
                def _():
                    got(shard, chunk)
                    mine = chunk_of(rows_ref.at[shard], core, chunk)
                    pass_on(shard, chunk, mine)
                    share(shard, chunk, mine)

        for n, step in enumerate((1, -1)):
            shard = z - step * distance

            @pl.when((shard >= 0) & (shard < parts))
            def _():
                piece = all_wide_ref.at[shard]
                send(piece, piece, w_send.at[n, shard], w_recv.at[shard], sibling).wait_recv()

            @pl.when((shard >= 0) & (shard < parts) & (z + step >= 0) & (z + step < parts))
            def _():
                piece = all_wide_ref.at[shard]
                send(piece, piece, w_send.at[n, shard], w_recv.at[shard], beside(step)).start()

    for step in range(1, columns):
        there = lax.rem(xy + columns - step, columns)
        for n, ref in enumerate(arrays_at(there)):
            send(ref, ref, p_send.at[n, step], p_recv.at[n, there], sibling).wait_recv()
        ref = all_small_ref.at[there * 2 + core]
        send(ref, ref, s_send.at[there], s_recv.at[there], sibling).start()

    for column in range(columns):
        ref = all_small_ref.at[column * 2 + 1 - core]
        copy = send(ref, ref, s_send.at[column], s_recv.at[column], sibling)
        copy.wait_recv()
        copy.wait_send()
    for step in range(1, columns):
        for n, ref in enumerate(arrays_at(xy)):
            send(ref, ref, p_send.at[n, step], p_recv.at[n, xy], sibling).wait_send()
    for step in range(1, parts):
        send(small_ref, all_small_ref.at[dp, z], z_send.at[step], z_recv.at[z], sibling).wait_send()
    for n in range(2):

        @pl.when(jnp.logical_not(is_same(wq_target(n), me)))
        def _():
            send(wq_ref, depth_of(dp, 1), q_send.at[n], q_recv.at[core], sibling).wait_send()

    own_wide.wait()
    for n, step in enumerate((1, -1)):
        for distance in range(parts):
            shard = z - step * distance

            @pl.when((shard >= 0) & (shard < parts) & (z + step >= 0) & (z + step < parts))
            def _():
                piece = all_wide_ref.at[shard]
                send(piece, piece, w_send.at[n, shard], w_recv.at[shard], beside(step)).wait_send()

    for shard in range(parts):
        for chunk in range(CHUNKS):
            mine = chunk_of(rows_ref.at[shard], core, chunk)
            other = chunk_of(rows_ref.at[shard], 1 - core, chunk)
            copy = send(mine, other, share_send.at[shard, chunk], xs_recv.at[shard, chunk], sibling)

            @pl.when(jnp.logical_not((shard == z) & outside))
            def _():
                copy.wait_send()

            @pl.when(jnp.logical_not((shard == z) & inside))
            def _():
                copy.wait_recv()

            for n, way in enumerate(ways(shard)):

                @pl.when(way)
                def _():
                    send(
                        mine, mine, fwd_send.at[n, shard, chunk], x_recv.at[shard, chunk], sibling
                    ).wait_send()

    for chunk in range(CHUNKS):
        first = chunk_of(tokens_ref, 0, chunk)
        send(first, first, in_send.at[0, chunk], x_recv.at[z, chunk], sibling).wait_send()

        @pl.when(outside)
        def _():
            send(first, first, in_send.at[1, chunk], x_recv.at[z, chunk], sibling).wait_send()

    @pl.when(inside)
    def _():
        pltpu.make_async_copy(tokens_ref, rows_ref.at[z], local_sems.at[0]).wait()


def gather(shape, tokens, wq, small, wide):
    parts, columns = shape["zh"] * shape["zl"], shape["xy"]
    anywhere = pl.BlockSpec(memory_space=pl.ANY)
    dma = pltpu.SemaphoreType.DMA
    return pl.pallas_call(
        functools.partial(gather_kernel, shape),
        out_shape=[
            jax.ShapeDtypeStruct((parts, *tokens.shape), tokens.dtype),
            jax.ShapeDtypeStruct((3, 2 * columns * wq.shape[1], wq.shape[2]), wq.dtype),
            jax.ShapeDtypeStruct((2 * columns, parts, *small.shape), small.dtype),
            jax.ShapeDtypeStruct((parts, *wide.shape), wide.dtype),
        ],
        in_specs=[anywhere] * 4,
        out_specs=[anywhere] * 4,
        scratch_shapes=[
            dma((4,)), dma((2, CHUNKS)), dma((2, parts, CHUNKS)), dma((parts, CHUNKS)),
            dma((parts, CHUNKS)), dma((parts, CHUNKS)),
            dma((parts,)), dma((parts,)), dma((2, columns)), dma((2, columns)), dma((columns,)),
            dma((columns,)), dma((2, parts)), dma((parts,)), dma((2,)), dma((2,)),
        ],
        compiler_params=pltpu.CompilerParams(collective_id=2, has_side_effects=True),
        name="gather",
    )(tokens, wq, small, wide)


def add_over_devices(shape, me, value, column_slots, plane_slots, sems):
    xy, core, zh, zl = me
    mine = (core * 2 + zh) * shape["zl"] + zl
    column_slots[mine] = value
    sent = []
    for step, there, device in column_peers(shape, me):
        copy = send(
            column_slots.at[mine], column_slots.at[mine], sems.at[0, step], sems.at[1, mine], device
        )
        copy.start()
        sent.append(copy)
    for step, there, device in column_peers(shape, me):
        send(
            column_slots.at[there], column_slots.at[there], sems.at[0, step], sems.at[1, there], device
        ).wait_recv()
    for copy in sent:
        copy.wait_send()
    total = column_slots[0]
    for slot in range(1, 4 * shape["zl"]):
        total = total + column_slots[slot]
    plane_slots[xy] = total
    sent = []
    for step, there, device in plane_peers(shape, me):
        copy = send(plane_slots.at[xy], plane_slots.at[xy], sems.at[2, step], sems.at[3, xy], device)
        copy.start()
        sent.append(copy)
    for step, there, device in plane_peers(shape, me):
        send(
            plane_slots.at[there], plane_slots.at[there], sems.at[2, step], sems.at[3, there], device
        ).wait_recv()
    for copy in sent:
        copy.wait_send()
    total = plane_slots[0]
    for slot in range(1, shape["xy"]):
        total = total + plane_slots[slot]
    return total


LANES = 256


def lane_sums(values, ranges):
    lane = lax.broadcasted_iota(jnp.int32, values.shape, 1)
    return [
        jnp.sum(jnp.where((lane >= low) & (lane < high), values, 0.0)) for low, high in ranges
    ]


def small_ranges(n_bias, n_gain):
    ends = [0, n_bias] + [n_bias + n_gain * (n + 1) for n in range(4)]
    return list(zip(ends[:-1], ends[1:]))


def row_of(values):
    lane = lax.broadcasted_iota(jnp.int32, (1, 128), 1)
    row = jnp.zeros((1, 128), F32)
    for n, value in enumerate(values):
        row = jnp.where(lane == n, value, row)
    return row


def sums_kernel(
    shape, n_bias, n_gain,
    grad_qkv_ref, small_ref, wide_ref, wq_ref, wp_ref, wu_ref, wd_ref, ws_ref,
    sum_ref, small_sum_ref, totals_ref,
    plane, both, pieces, small_column, small_plane, row_column, row_plane,
    p_send, p_recv, q_send, q_recv, local_sems, small_sems, row_sems,
):
    me = place()
    xy, core, zh, zl = me
    places, columns = shape["zl"], shape["xy"]
    z = zh * places + zl
    head_block = zl * 2 + core
    depth = both.shape[1] // 2
    greet(shape)

    def plane_part(column):
        return grad_qkv_ref.at[:, pl.ds(pl.multiple_of(column * 2 * depth, 2 * depth), 2 * depth), :]

    keep_part = pltpu.make_async_copy(plane_part(xy), plane.at[xy], local_sems.at[0])
    keep_part.start()
    for step, there, device in plane_peers(shape, me):
        send(plane_part(there), plane.at[xy], p_send.at[step], p_recv.at[xy], device).start()

    def square(values):
        wide = values.astype(F32)
        return jnp.sum(wide * wide)

    up, down, proj = parts_of(wide_ref, wu_ref, wp_ref)
    values = [square(proj), square(up), square(down)]
    values += [square(wq_ref[c]) for c in range(3)]
    values += [square(ref[...]) for ref in (wp_ref, wu_ref, wd_ref)]
    ranges = small_ranges(n_bias, n_gain)
    values += lane_sums(ws_ref[...] * ws_ref[...], ranges)

    keep_part.wait()
    for step, there, device in plane_peers(shape, me):
        send(plane_part(there), plane.at[there], p_send.at[step], p_recv.at[there], device).wait_recv()
    for c in range(3):
        total = plane[0, c].astype(F32)
        for n in range(1, columns):
            total = total + plane[n, c].astype(F32)
        both[c] = total.astype(BF)

    def target(c):
        return (xy, c, lax.div(head_block, places), lax.rem(head_block, places))

    def source(n):
        return (xy, lax.rem(z, 2), n, lax.div(z, 2))

    def part(c):
        return both.at[:, c * depth : (c + 1) * depth, :]

    for c in range(2):

        @pl.when(is_same(target(c), me))
        def _():
            pltpu.make_async_copy(part(c), pieces.at[zh], local_sems.at[1]).start()

        @pl.when(jnp.logical_not(is_same(target(c), me)))
        def _():
            send(part(c), pieces.at[zh], q_send.at[c], q_recv.at[zh], target(c)).start()

    small = add_over_devices(shape, me, small_ref[...], small_column, small_plane, small_sems)
    small_sum_ref[...] = small
    for n in range(2):

        @pl.when(is_same(target(n), me))
        def _():
            pltpu.make_async_copy(part(n), pieces.at[zh], local_sems.at[1]).wait()

        @pl.when(jnp.logical_not(is_same(target(n), me)))
        def _():
            send(part(n), pieces.at[zh], q_send.at[n], q_recv.at[zh], target(n)).wait_send()

        @pl.when(jnp.logical_not(is_same(source(n), me)))
        def _():
            send(part(n), pieces.at[n], q_send.at[n], q_recv.at[n], source(n)).wait_recv()

    squares = []
    for c in range(3):
        total = pieces[0, c].astype(F32) + pieces[1, c].astype(F32)
        sum_ref[c] = total
        squares.append(square(total))
    row = add_over_devices(shape, me, row_of(squares + values), row_column, row_plane, row_sems)
    lane = lax.broadcasted_iota(jnp.int32, (1, 128), 1)
    for n, value in enumerate(lane_sums(small * small, ranges)):
        row = jnp.where(lane == 17 + n, value, row)
    totals_ref[...] = row

    for step, there, device in plane_peers(shape, me):
        send(plane_part(there), plane.at[xy], p_send.at[step], p_recv.at[xy], device).wait_send()


def parts_of(wide_ref, up_like, proj_like):
    ff, heads = up_like.shape[1], proj_like.shape[0]
    return wide_ref[:, :ff], wide_ref[:, ff : 2 * ff], wide_ref[:, 2 * ff : 2 * ff + heads]


def sums(shape, n_bias, n_gain, grad_qkv, small, wide, weights):
    columns = shape["xy"]
    members = 4 * shape["zl"]
    depth = grad_qkv.shape[1] // (2 * columns)
    heads_cols = grad_qkv.shape[2]
    vmem = pl.BlockSpec(memory_space=pltpu.VMEM)
    dma = pltpu.SemaphoreType.DMA
    slots = max(members, columns)
    return pl.pallas_call(
        functools.partial(sums_kernel, shape, n_bias, n_gain),
        out_shape=[
            jax.ShapeDtypeStruct((3, depth, heads_cols), F32),
            jax.ShapeDtypeStruct(small.shape, F32),
            jax.ShapeDtypeStruct((1, 128), F32),
        ],
        in_specs=[pl.BlockSpec(memory_space=pl.ANY)] + [vmem] * 7,
        out_specs=[vmem] * 3,
        scratch_shapes=[
            pltpu.VMEM((columns, 3, 2 * depth, heads_cols), BF),
            pltpu.VMEM((3, 2 * depth, heads_cols), BF),
            pltpu.VMEM((2, 3, depth, heads_cols), BF),
            pltpu.VMEM((members, *small.shape), F32),
            pltpu.VMEM((columns, *small.shape), F32),
            pltpu.VMEM((members, 1, 128), F32),
            pltpu.VMEM((columns, 1, 128), F32),
            dma((columns,)), dma((columns,)), dma((2,)), dma((2,)), dma((2,)),
            dma((4, slots)), dma((4, slots)),
        ],
        compiler_params=pltpu.CompilerParams(
            collective_id=3, has_side_effects=True, vmem_limit_bytes=48 * 2**20
        ),
        name="sums",
    )(grad_qkv, small, wide, *weights)


def reduce_kernel(shape, row_ref, total_ref, row_column, row_plane, row_sems):
    greet(shape)
    total_ref[...] = add_over_devices(shape, place(), row_ref[...], row_column, row_plane, row_sems)


def reduce_row(shape, row):
    members = 4 * shape["zl"]
    vmem = pl.BlockSpec(memory_space=pltpu.VMEM)
    return pl.pallas_call(
        functools.partial(reduce_kernel, shape),
        out_shape=jax.ShapeDtypeStruct((1, 128), F32),
        in_specs=[vmem],
        out_specs=vmem,
        scratch_shapes=[
            pltpu.VMEM((members, 1, 128), F32),
            pltpu.VMEM((shape["xy"], 1, 128), F32),
            pltpu.SemaphoreType.DMA((4, max(members, shape["xy"]))),
        ],
        compiler_params=pltpu.CompilerParams(collective_id=4, has_side_effects=True),
        name="reduce_row",
    )(row)


def moments_kernel(
    n_bias, n_gain, spot_ref, totals_ref, small_ref,
    gq, wide, wq, wp, wu, wd, ws, mq, mp, mu, md, ms, sq, sp, su, sd, ss,
    nmq, nmp, nmu, nmd, nmb, nmg, nmt, nsq, nsp, nsu, nsd, nsb, nsg, nst, uq, up, uu, ud, us, row_ref,
):
    totals = totals_ref[...]
    lane = lax.broadcasted_iota(jnp.int32, (1, 128), 1)
    grads_here = (lane < 6) | ((lane >= 17) & (lane < 22))
    norm = jnp.sqrt(jnp.sum(jnp.where(grads_here, totals, 0.0), axis=1, keepdims=True))
    clip = jnp.minimum(1.0, 1.0 / norm)
    values = []

    def step(grad, weight, mean, square):
        scaled = clip * grad
        new_mean = 0.5 * mean + 0.5 * scaled
        new_square = 0.5 * square + 0.5 * scaled * scaled
        update = new_mean / (jnp.sqrt(new_square) + 1e-06) + 0.01 * weight
        return new_mean, new_square, update

    for c in range(3):
        nmq[c], nsq[c], update = step(gq[c], wq[c], mq[c], sq[c])
        uq[c] = update
        values.append(jnp.sum(update * update))
    grad_up, grad_down, grad_proj = parts_of(wide, wu, wp)
    for turned, g, w, m, s, nm, ns, u in (
        (True, grad_proj, wp, mp, sp, nmp, nsp, up),
        (False, grad_up, wu, mu, su, nmu, nsu, uu),
        (True, grad_down, wd, md, sd, nmd, nsd, ud),
    ):
        grad = g.astype(F32)
        nm[...], ns[...], update = step(grad.T if turned else grad, w[...], m[...], s[...])
        u[...] = update
        values.append(jnp.sum(update * update))
    spot = spot_ref[0]
    grad = small_ref[pl.ds(spot, 1), :]
    new_mean, new_square, update = step(grad, ws[...], ms[...], ss[...])
    us[...] = update
    ranges = small_ranges(n_bias, n_gain)
    values += lane_sums(update * update, ranges)
    row_ref[...] = row_of(values)
    put_small(ranges, new_mean, nmb, nmg, nmt)
    put_small(ranges, new_square, nsb, nsg, nst)


def put_small(ranges, row, bias, gain, shift):
    bias[...] = row[:, ranges[0][0] : ranges[0][1]]
    for n in range(2):
        gain[n : n + 1, :] = row[:, ranges[1 + n][0] : ranges[1 + n][1]]
        shift[n : n + 1, :] = row[:, ranges[3 + n][0] : ranges[3 + n][1]]


def weights_kernel(
    n_bias, n_gain, totals_ref, update_ref, wq, wp, wu, wd, ws, uq, up, uu, ud, us,
    nwq, nwp, nwu, nwd, nwb, nwg, nwt, norms_ref, norm_ref,
):
    totals, updates = totals_ref[...], update_ref[...]
    lane = lax.broadcasted_iota(jnp.int32, (1, 128), 1)
    grads_here = (lane < 6) | ((lane >= 17) & (lane < 22))
    norm_ref[...] = jnp.sqrt(jnp.sum(jnp.where(grads_here, totals, 0.0), axis=1, keepdims=True))
    weight_norm, update_norm = jnp.sqrt(totals), jnp.sqrt(updates)
    norms_ref[0:1, :] = weight_norm[:, 6:17]
    norms_ref[1:2, :] = update_norm[:, 0:11]

    def factor(n):
        return 0.3 * (weight_norm[:, 6 + n : 7 + n] / update_norm[:, n : n + 1])

    for c in range(3):
        nwq[c] = wq[c] - factor(c) * uq[c]
    for n, (w, u, out) in enumerate(((wp, up, nwp), (wu, uu, nwu), (wd, ud, nwd))):
        out[...] = w[...] - factor(3 + n) * u[...]
    ranges = small_ranges(n_bias, n_gain)
    column = lax.broadcasted_iota(jnp.int32, (1, LANES), 1)
    factors = jnp.zeros((1, LANES), F32)
    for n, (low, high) in enumerate(ranges):
        factors = jnp.where((column >= low) & (column < high), factor(6 + n), factors)
    put_small(ranges, ws[...] - factors * us[...], nwb, nwg, nwt)


def shapes_of(arrays):
    return [jax.ShapeDtypeStruct(array.shape, F32) for array in arrays]


def optimizer(shape, n_bias, n_gain, spot, totals, small, grads, weights, means, squares, small_like):
    vmem = pl.BlockSpec(memory_space=pltpu.VMEM)
    big = list(weights[:4])
    results = shapes_of(big) + shapes_of(small_like)
    row = jax.ShapeDtypeStruct((1, 128), F32)
    params = pltpu.CompilerParams(vmem_limit_bytes=48 * 2**20)
    out = pl.pallas_call(
        functools.partial(moments_kernel, n_bias, n_gain),
        out_shape=results * 2 + shapes_of(weights) + [row],
        in_specs=[pl.BlockSpec(memory_space=pltpu.SMEM)] + [vmem] * 19,
        out_specs=[vmem] * 20,
        compiler_params=params,
        name="moments",
    )(spot, totals, small, *grads, *weights, *means, *squares)
    new_means, new_squares, updates, row_here = out[:7], out[7:14], out[14:19], out[19]
    updates_total = reduce_row(shape, row_here)
    out = pl.pallas_call(
        functools.partial(weights_kernel, n_bias, n_gain),
        out_shape=results
        + [jax.ShapeDtypeStruct((2, 11), F32), jax.ShapeDtypeStruct((1, 1), F32)],
        in_specs=[vmem] * 12,
        out_specs=[vmem] * 9,
        compiler_params=params,
        name="weights",
    )(totals, updates_total, *weights, *updates)
    return updates_total, out[8], out[7], out[:7], new_means, new_squares


def turn_own_first(shape, core, src, dst):
    columns = shape["xy"]
    width = src.shape[1]
    depth = width // (2 * columns)
    for start in range(0, width, 128):
        turned = src[:, start : start + 128].T
        for offset in range(0, 128, depth):
            block = (start + offset) // depth
            slot = block // 2 + jnp.where(core == block % 2, 0, columns)
            dst[pl.ds(pl.multiple_of(slot * depth, depth), depth), :] = turned[offset : offset + depth]


def feed_kernel(
    shape, ff_local, x_ref, c_ref, attn_ref, norm_ref, proj_ref, up_ref, down_ref,
    block_ref, middle_ref, given_ref, wide_ref, sums_ref,
    middle, total, second, a_second, a_turned, c_turned, own, other, taken, proj_own, proj_other, proj_taken,
    out_sems, own_sems, swap_send, swap_recv, proj_sems,
):
    me = place()
    xy, core, zh, zl = me
    sibling = (xy, 1 - core, zh, zl)
    step = pl.program_id(0)
    steps = pl.num_programs(0)
    parts = attn_ref.shape[0]
    heads_cols = attn_ref.shape[1]
    half, chunk = own.shape[2], own.shape[3]
    per = ff_local // chunk
    wide = 2 * ff_local + heads_cols
    slot = lax.rem(step, 2)

    def swap(at, index):
        return send(other.at[at], taken.at[index], swap_send.at[index], swap_recv.at[index], sibling)

    def columns(index, which):
        start = lax.div(index, per) * wide + which * ff_local + lax.rem(index, per) * chunk
        return wide_ref.at[:, pl.ds(pl.multiple_of(start, 128), chunk)]

    def keep(at, index, which):
        return pltpu.make_async_copy(own.at[at, which], columns(index, which), own_sems.at[at, which])

    def add_swapped(at, index):
        swap(at, index).wait_recv()
        for which in range(2):
            own[at, which] = (
                own[at, which].astype(F32) + taken[index, which].astype(F32)
            ).astype(BF)
            keep(at, index, which).start()

    def normed():
        values = middle[...]
        center = values - jnp.mean(values, axis=-1, keepdims=True)
        inverse = lax.rsqrt(jnp.mean(center * center, axis=-1, keepdims=True) + 1e-05)
        return center * inverse, inverse

    @pl.when(step == 0)
    def _():
        barrier = pltpu.get_barrier_semaphore()
        pl.semaphore_signal(barrier, inc=1, device_id=sibling, device_id_type=MESH)
        mixed = x_ref[...].astype(F32)
        for part in range(parts):
            mixed = mixed + dot(attn_ref[part].T, proj_ref[part], 1, 1)
        middle[...] = mixed
        value, _ = normed()
        a_second[...] = (value * norm_ref[0:1, :] + norm_ref[1:2, :]).astype(BF)
        turn_own_first(shape, core, a_second, a_turned)
        turn_own_first(shape, core, c_ref, c_turned)
        total[...] = jnp.zeros_like(total)
        second[...] = jnp.zeros_like(second)
        pl.semaphore_wait(barrier, 1)

    @pl.when(step >= 2)
    def _():
        swap(slot, step - 2).wait_send()
        for which in range(2):
            keep(slot, step - 2, which).wait()

    up, down = up_ref[0], down_ref[0]
    pre = dot(a_second[...], up, 1, 0)
    grad_hidden = dot(c_ref[...], down, 1, 0)
    normal = 0.5 * (1.0 + lax.erf(pre * 2.0**-0.5))
    hidden = (pre * normal).astype(BF)
    slope = normal + pre * jnp.exp(-0.5 * pre * pre) * 0.3989422804014327
    grad_pre = (slope * grad_hidden).astype(BF)
    total[...] += dot(hidden, down, 1, 1)
    grad_down = dot(c_turned[...], hidden, 1, 0).astype(BF)
    own[slot, 1] = grad_down[:half]
    other[slot, 1] = grad_down[half:]
    second[...] += dot(grad_pre, up, 1, 1)
    grad_up = dot(a_turned[...], grad_pre, 1, 0).astype(BF)
    own[slot, 0] = grad_up[:half]
    other[slot, 0] = grad_up[half:]
    swap(slot, step).start()

    @pl.when(step >= 1)
    def _():
        add_swapped(1 - slot, step - 1)

    @pl.when(step == steps - 1)
    def _():
        a_second[...] = (middle[...] + total[...]).astype(BF)
        out_block = pltpu.make_async_copy(a_second, block_ref, out_sems.at[0])
        out_block.start()
        value, inverse = normed()
        grad = second[...]
        sums_ref[0:1, :] = jnp.sum(grad * value, axis=0, keepdims=True)
        sums_ref[1:2, :] = jnp.sum(grad, axis=0, keepdims=True)
        inner = grad * norm_ref[0:1, :]
        second[...] = c_ref[...].astype(F32) + inverse * (
            inner
            - jnp.mean(inner, axis=-1, keepdims=True)
            - value * jnp.mean(inner * value, axis=-1, keepdims=True)
        )
        out_middle = pltpu.make_async_copy(second, middle_ref, out_sems.at[1])
        out_middle.start()
        low = second[...].astype(BF)
        turn_own_first(shape, core, low, a_turned)
        for part in range(parts):
            grad_proj = dot(a_turned[...], attn_ref[part], 1, 1).astype(BF)
            proj_own[part] = grad_proj[:half]
            proj_other[part] = grad_proj[half:]
        swap_proj = send(proj_other, proj_taken, proj_sems.at[0], proj_sems.at[1], sibling)
        swap_proj.start()
        for part in range(parts):
            rows = pl.ds(part * heads_cols, heads_cols)
            c_turned[rows, :] = dot(low, proj_ref[part], 1, 0).T.astype(BF)
        out_given = pltpu.make_async_copy(c_turned, given_ref, out_sems.at[2])
        out_given.start()
        add_swapped(slot, step)
        swap_proj.wait_recv()
        kept = []
        for part in range(parts):
            proj_own[part] = (proj_own[part].astype(F32) + proj_taken[part].astype(F32)).astype(BF)
            there = wide_ref.at[:, pl.ds(part * wide + 2 * ff_local, heads_cols)]
            kept.append(pltpu.make_async_copy(proj_own.at[part], there, out_sems.at[3 + part]))
            kept[-1].start()

        @pl.when(step >= 1)
        def _():
            swap(1 - slot, step - 1).wait_send()
            for which in range(2):
                keep(1 - slot, step - 1, which).wait()

        swap(slot, step).wait_send()
        for which in range(2):
            keep(slot, step, which).wait()
        swap_proj.wait_send()
        for copy in (out_block, out_middle, out_given, *kept):
            copy.wait()


def feed_forward(shape, tokens, cotangent, attn_rows, norm, shared, ff_local):
    rows, width = tokens.shape
    parts, heads_cols = attn_rows.shape[:2]
    chunk = min(512, ff_local)
    per = ff_local // chunk
    steps = parts * per
    half = width // 2
    anywhere = pl.BlockSpec(memory_space=pl.ANY)

    def once(block, *index):
        return pl.BlockSpec(block, lambda s: index, pipeline_mode=pl.Buffered(1))

    dma = pltpu.SemaphoreType.DMA
    return pl.pallas_call(
        functools.partial(feed_kernel, shape, ff_local),
        grid=(steps,),
        in_specs=[
            once((rows, width), 0, 0),
            once((rows, width), 0, 0),
            once((parts, heads_cols, rows), 0, 0, 0),
            once((2, width), 0, 0),
            once((parts, width, heads_cols), 0, 0, 2 * ff_local // heads_cols),
            pl.BlockSpec((1, width, chunk), lambda s: (s // per, 0, s % per)),
            pl.BlockSpec((1, width, chunk), lambda s: (s // per, 0, per + s % per)),
        ],
        out_specs=[anywhere] * 4 + [pl.BlockSpec((2, width), lambda s: (0, 0))],
        out_shape=[
            jax.ShapeDtypeStruct((rows, width), BF),
            jax.ShapeDtypeStruct((rows, width), F32),
            jax.ShapeDtypeStruct((parts * heads_cols, rows), BF),
            jax.ShapeDtypeStruct((half, parts * (2 * ff_local + heads_cols)), BF),
            jax.ShapeDtypeStruct((2, width), F32),
        ],
        scratch_shapes=[
            pltpu.VMEM((rows, width), F32),
            pltpu.VMEM((rows, width), F32),
            pltpu.VMEM((rows, width), F32),
            pltpu.VMEM((rows, width), BF),
            pltpu.VMEM((width, rows), BF),
            pltpu.VMEM((width, rows), BF),
            pltpu.VMEM((2, 2, half, chunk), BF),
            pltpu.VMEM((2, 2, half, chunk), BF),
            pltpu.VMEM((steps, 2, half, chunk), BF),
            pltpu.VMEM((parts, half, heads_cols), BF),
            pltpu.VMEM((parts, half, heads_cols), BF),
            pltpu.VMEM((parts, half, heads_cols), BF),
            dma((3 + parts,)),
            dma((2, 2)),
            dma((steps,)),
            dma((steps,)),
            dma((2,)),
        ],
        compiler_params=pltpu.CompilerParams(
            vmem_limit_bytes=60 * 2**20, collective_id=5, has_side_effects=True
        ),
        name="feed_forward",
    )(tokens, cotangent, attn_rows, norm, shared, shared, shared)


def norm_parts(values):
    center = values - jnp.mean(values, axis=-1, keepdims=True)
    inverse = lax.rsqrt(jnp.mean(center * center, axis=-1, keepdims=True) + 1e-05)
    return center * inverse, inverse


def norm_back(normed, inverse, gain, grad):
    inner = grad * gain
    return inverse * (
        inner
        - jnp.mean(inner, axis=-1, keepdims=True)
        - normed * jnp.mean(inner * normed, axis=-1, keepdims=True)
    )


def per_device(
    shape,
    tokens, cotangent, item_len, bucket_table,
    w_qkv, w_proj, w_up, w_down, rel_bias, ln_gain, ln_shift,
    mean_qkv, mean_proj, mean_up, mean_down, mean_bias, mean_gain, mean_shift,
    square_qkv, square_proj, square_up, square_down, square_bias, square_gain, square_shift,
):
    columns, places = shape["xy"], shape["zl"]
    parts = 2 * places
    devices = columns * 2 * parts
    rows, width = tokens.shape
    heads = w_qkv.shape[2] // DH
    tok = rows * parts
    xy, core, zh, zl = place()
    me = ((xy * 2 + core) * 2 + zh) * places + zl
    head_block = zl * 2 + core

    ff_local, heads_cols = w_up.shape[1], w_proj.shape[0]
    local = jnp.concatenate([w_up, w_down.T, w_proj.T], axis=1).astype(BF)

    n_bias, n_gain = rel_bias.shape[0], ln_gain.shape[1]
    n_small = n_bias + 4 * n_gain

    def pack(bias, gain, shift):
        row = jnp.concatenate([bias, gain.reshape(-1), shift.reshape(-1)])
        return jnp.pad(row, (0, LANES - n_small))[None, :]

    small_weights = pack(rel_bias, ln_gain, ln_shift)
    group_rows, w_heads, small, wide = gather(
        shape, tokens, w_qkv.astype(BF), small_weights, local
    )
    shared = lax.all_gather(wide, DP, axis=1, tiled=True)
    small = small.reshape(devices, LANES)

    def columns_of(start):
        part = small[:, start : start + 2 * n_gain].reshape(devices, 2, n_gain)
        return part.transpose(1, 0, 2).reshape(2, width)

    table_flat = small[:, :n_bias].reshape(-1)
    gains, shifts = columns_of(n_bias), columns_of(n_bias + 2 * n_gain)
    other_len = lax.ppermute(item_len, "core", [(0, 1), (1, 0)])
    split = jnp.where(zh == core, item_len, other_len)[0, 0:1]

    normed_all, _ = norm_parts(group_rows.reshape(tok, width).astype(F32))
    a_first = (normed_all * gains[0] + shifts[0]).astype(BF)
    qkv = lax.dot_general(
        w_heads, a_first, (((1,), (1,)), ((), ())), preferred_element_type=F32
    ).astype(BF).reshape(3 * heads * DH, tok)

    table = lax.dynamic_slice_in_dim(
        table_flat.reshape(BUCKETS, H), head_block * heads, heads, 1
    )
    one_hot = (jnp.arange(BUCKETS)[:, None] == bucket_table[None, :]).astype(F32)
    dist_bias = lax.dot_general(
        table, one_hot, (((0,), (0,)), ((), ())), precision=HIGHEST, preferred_element_type=F32
    )
    pattern = jnp.concatenate(
        [dist_bias * LOG2E, jnp.full((heads, BLK), NEG, F32)], axis=1
    )[:, None, :]
    out, attn_rows, lse = attend(shape, qkv, pattern, split, heads)

    attn_rows = attn_rows.reshape(parts, heads * DH, rows)
    x_rows = tokens.astype(F32)
    norm_two = jnp.stack([gains[1], shifts[1]])
    block_out, grad_middle, grad_attn, wide_grad, sums_two = feed_forward(
        shape, tokens, cotangent, attn_rows, norm_two, shared, ff_local
    )
    gain_two, shift_two = sums_two[0], sums_two[1]
    given = grad_attn.reshape(parts, heads, DH, rows)
    early = heads - 1
    heads_early, pattern_early = attend_back(
        shape, qkv, out, given, lse, pattern, split, heads, 0, early, 1
    )
    heads_late, pattern_late = attend_back(
        shape, qkv, out, given, lse, pattern, split, heads, early, heads - early, 6
    )
    grad_pattern = jnp.concatenate([pattern_early, pattern_late])
    grad_heads = jnp.concatenate([heads_early, heads_late], axis=1).reshape(3, heads * DH, tok)

    half = width // 2

    def first_half(which):
        here = lax.dynamic_slice_in_dim(w_heads, which * half, half, 1)
        return lax.dot_general(
            grad_heads, here, (((0, 1), (0, 2)), ((), ())), preferred_element_type=F32
        )

    other_half = lax.ppermute(first_half(1 - core).astype(BF), "core", [(0, 1), (1, 0)])
    half_sum = (first_half(core) + other_half.astype(F32)).astype(BF)
    arrived = []
    for turn in range(parts):
        route = [
            (((c * 2 + b % 2) * 2 + g) * places + b // 2, (c * 2 + g) * parts + (b + turn) % parts)
            for c in range(columns)
            for g in range(2)
            for b in range(parts)
        ]
        shard = lax.rem(head_block + turn, parts)
        piece = lax.dynamic_slice_in_dim(half_sum, shard * rows, rows, 0)
        arrived.append(lax.ppermute(piece, ALL, route))

    grad_qkv = jnp.einsum("td,cet->cde", a_first, grad_heads, preferred_element_type=F32)
    head_sums = jnp.sum(grad_heads.astype(F32), axis=2)
    wide_heads = w_heads.astype(F32)
    shift_one = jnp.sum(wide_heads * head_sums[:, None, :], axis=(0, 2))
    gain_one = (
        jnp.sum(wide_heads * grad_qkv, axis=(0, 2)) - shifts[0] * shift_one
    ) / gains[0]
    grad_qkv = grad_qkv.astype(BF)

    part = lax.psum_scatter(wide_grad, "xy", scatter_dimension=0, tiled=True)
    part, heads_early = lax.optimization_barrier((part, heads_early))
    wide_sum = lax.psum_scatter(part, TENSOR, scatter_dimension=1, tiled=True)
    bias_grad = lax.dot_general(
        one_hot, grad_pattern[:, 0, :tok], (((1,), (1,)), ((), ())),
        precision=HIGHEST, preferred_element_type=F32,
    )
    table_grad = lax.dynamic_update_slice(
        jnp.zeros((BUCKETS, H), F32), bias_grad, (0, head_block * heads)
    )

    def by_device(*vectors):
        return jnp.stack(vectors).reshape(2, devices, n_gain).transpose(1, 0, 2).reshape(devices, -1)

    small_grad = jnp.concatenate(
        [
            table_grad.reshape(devices, n_bias),
            by_device(gain_one, gain_two),
            by_device(shift_one, shift_two),
            jnp.zeros((devices, LANES - n_small), F32),
        ],
        axis=1,
    )
    weights = (w_qkv, w_proj, w_up, w_down, small_weights)
    sum_qkv, small_sum, totals = sums(
        shape, n_bias, n_gain, grad_qkv, small_grad, wide_sum, weights
    )
    small_like = [rel_bias[None, :], ln_gain, ln_shift]
    updates_total, grad_norm, param_norms, *results = optimizer(
        shape, n_bias, n_gain, me[None].astype(jnp.int32), totals, small_sum,
        (sum_qkv, wide_sum), weights,
        (mean_qkv, mean_proj, mean_up, mean_down, pack(mean_bias, mean_gain, mean_shift)),
        (square_qkv, square_proj, square_up, square_down, pack(square_bias, square_gain, square_shift)),
        small_like,
    )
    arrived, _ = lax.optimization_barrier((arrived, updates_total))
    rounds = [sum(piece.astype(F32) for piece in arrived[n::2]) for n in range(2)]
    even = lax.rem(zh * places + zl, 2) == 0
    first_rows = jnp.concatenate(
        [jnp.where(even, rounds[0], rounds[1]), jnp.where(even, rounds[1], rounds[0])], axis=1
    )
    normed_one, inverse_one = norm_parts(x_rows)
    grad_tokens = (
        grad_middle + norm_back(normed_one, inverse_one, gains[0], first_rows)
    ).astype(BF)
    new = [array if n % 7 != 4 else array[0] for group in results for n, array in enumerate(group)]
    return (block_out, grad_tokens, grad_norm[0, 0], param_norms, *new)


def solution(mesh):
    shape = {"xy": mesh.shape["dp"] // 2, "core": 2, "zh": 2, "zl": mesh.shape["tensor"] // 2}
    split_mesh = Mesh(mesh.devices.reshape(tuple(shape[axis] for axis in ALL)), ALL)
    weights = (
        P(None, DP, TENSOR),
        P(TENSOR, DP),
        P(DP, TENSOR),
        P(TENSOR, DP),
        P(ALL),
        P(None, ALL),
        P(None, ALL),
    )
    rows = P(ALL, None)
    return jax.shard_map(
        functools.partial(per_device, shape),
        mesh=split_mesh,
        in_specs=(rows, rows, P(DP, None), P(), *weights, *weights, *weights),
        out_specs=(rows, rows, P(), P(), *weights, *weights, *weights),
        check_vma=False,
    )
```

time: 1110 us -> 596 us (0.54)
  waiting for transfers between devices: 304 us -> 8.45 us
  Pallas kernels: 218 us -> 457 us
  matrix products: 155 us -> 27.1 us
  blocking collectives: 122 us -> 0 us
  local copies, waits for them, and re-layouts: 123 us -> 20.2 us
  starting transfers between devices: 87.7 us -> 17.5 us
  other arithmetic: 62.9 us -> 39.2 us
    pallas_call x4 -> x9, Pallas kernels: 218 us -> 457 us  [the longest x2 107 us: attend_back(): pl.pallas_call(functools.partial(attend_back_kernel, shape, first_head),...]
    reduce_scatter x4 -> x2, waiting for transfers between devices: 134 us -> 7.03 us  [the longest x1 7.03 us: per_device(): wide_sum = lax.psum_scatter(part, TENSOR, scatter_dimension=1, tiled=True)]
    dot_general x10 -> x2, matrix products: 135 us -> 10.3 us  [first_half(): lax.dot_general(grad_heads, here, (((0, 1), (0, 2)), ((), ())), preferred...]
    all_gather x4 -> x1, waiting for transfers between devices: 108 us -> 1.36 us  [per_device(): shared = lax.all_gather(wide, DP, axis=1, tiled=True)]
    unnamed x129 -> x98, local copies, waits for them, and re-layouts: 109 us -> 10.5 us
    psum x2 -> x0, blocking collectives: 81.3 us -> none  [the longest x1 41.9 us: per_device(): lax.psum(squares_of(grads[:4]), ALL)]
    ppermute x4 -> x5, starting transfers between devices: 84.4 us -> 17.3 us  [the longest x4 16 us: per_device(): arrived.append(lax.ppermute(piece, ALL, route))]
    unnamed x16 -> x3, waiting for transfers between devices: 53.7 us -> 0.05 us
  transfers between devices with their start and end apart: 17 -> 9, of which waited for: 9 -> 2; matrix products, arithmetic and copies ran while one was open for 16% -> 11% of each run, Pallas kernels for 20% -> 48%
where the time goes in v2:
time: 596 us; the launch traced here: 585 us
  Pallas kernels  457 us (77%)
  other arithmetic  39.2 us (7%)
  matrix products  27.1 us (5%)
  local copies, waits for them, and re-layouts  20.2 us (3%)
  starting transfers between devices  17.5 us (3%)
  between operations  15.1 us (3%)
  waiting for transfers between devices  8.45 us (1%)
    pallas_call x2, Pallas kernels, attend_back(): pl.pallas_call(functools.partial(attend_back_kernel, shape, first_head),...  107 us
    pallas_call x1, Pallas kernels, gather(): pl.pallas_call(functools.partial(gather_kernel, shape), out_shape=[jax.Sh...  102 us
    pallas_call x1, Pallas kernels, sums(): pl.pallas_call(functools.partial(sums_kernel, shape, n_bias, n_gain), out...  79.4 us
    pallas_call x1, Pallas kernels, attend(): pl.pallas_call(functools.partial(attend_kernel, shape), grid=(heads,), in...  78.5 us
    pallas_call x1, Pallas kernels, feed_forward(): pl.pallas_call(functools.partial(feed_kernel, shape, ff_local), grid=(ste...  73.7 us
    ppermute x4, starting transfers between devices, per_device(): arrived.append(lax.ppermute(piece, ALL, route))  16 us
    convert_element_type x2, other arithmetic, per_device(): a_first = (normed_all * gains[0] + shifts[0]).astype(BF)  13.7 us
  transfers between devices with their start and end apart: 9, of which 2 were waited for; matrix products, arithmetic and copies ran while one was open for 11% of the time, Pallas kernels for 48%

profile of v2, /device:TPU:8, one launch (start us, length us, event | category | flops | bytes accessed | tf_op | source)
XLA Modules:
  0.0 584.7 jit_solution(8940547858226576477)
XLA Ops:
  7.2 0.8 reshape.198
  8.0 0.8 reshape.199
  8.8 1.2 copy.50
  9.9 1.1 convert.12
  11.0 1.0 copy.51
  12.1 1.7 convert_element_type.68.wq_ref
  13.7 1.3 select_maximum_fusion.4
  15.0 0.9 pad_maximum_fusion.wide_ref
  15.9 102.4 %gather.1 = (bf16[4,768,1024]{2,1,0:T(8,128)(2,1)}, bf16[3,1024,256]{2,1,0:T(8,128)(2,1)}, f32[8,4,1,256]{3,2,1,0:T(1,128)}, bf16[4,128,2304]{2,1,0:T(8,128)(2,1)}) custom-call(bf16[768,1024]{1,0:T(8,128)(2,1)} %x_ref.1, bf16[3,128,256]{2,1,0:T(8,128)(2,1)} %convert_element_type.68.wq_ref, f32[1,256]{1,0:T(1,128)} %bitcast.63, ...), custom_call_target="tpu_custom_call" | custom-call | tf_op jit(solution)/shard_map/gather/pallas_call | solution.py:674
  118.5 0.8 reduce.3
  119.9 3.7 convert_reduce_fusion
  123.7 4.6 multiply_reduce_fusion
  130.1 5.7 fusion.3
  135.8 6.8 %fusion.7 = bf16[3,256,3072]{2,1,0:T(8,128)(2,1)} fusion(bf16[3,1024,256]{2,1,0:T(8,128)(2,1)S(1)} %copy-done.23, bf16[3072,1024]{1,0:T(8,128)(2,1)S(1)} %fusion.3), kind=kOutput, calls=%fused_computation.14 | convolution fusion | flops 4834197504 | bytes 12582912 | tf_op jit(solution)/shard_map/dot_general | solution.py:1291
  143.1 78.5 %attend.1 = (bf16[4,64,3072]{2,1,0:T(8,128)(2,1)}, bf16[4,4,64,768]{3,2,1,0:T(8,128)(2,1)}, f32[4,1,3072]{2,1,0:T(1,128)}) custom-call(s32[1]{0:T(128)} %bitcast.95, f32[4,1,3584]{2,1,0:T(1,128)} %broadcast_in_dim.15.pattern_ref, bf16[768,3072]{1,0:T(8,128)(2,1)} %bitcast.69, bf16[768,3072]{1,0:T(8,128)(2,1)} %bitcast.70, bf16[768,3072]{1,0:T(8,128)(2,1)} %bitcast.71), custom_call_target="tpu_custom_call" | custom-call | tf_op jit(solution)/shard_map/attend/pallas_call | solution.py:156
  221.6 1.4 all-gather.2.cloned.1.call-done.proj_ref.up_ref.down_ref
  223.0 73.7 %feed_forward.1 = (bf16[768,1024]{1,0:T(8,128)(2,1)}, f32[768,1024]{1,0:T(8,128)}, bf16[1024,768]{1,0:T(8,128)(2,1)}, bf16[512,9216]{1,0:T(8,128)(2,1)}, f32[2,1024]{1,0:T(2,128)}) custom-call(bf16[768,1024]{1,0:T(8,128)(2,1)} %x_ref.1, bf16[768,1024]{1,0:T(8,128)(2,1)} %c_ref.1, bf16[4,256,768]{2,1,0:T(8,128)(2,1)} %bitcast.86, ...), custom_call_target="tpu_custom_call" | custom-call | tf_op jit(solution)/shard_map/feed_forward/pallas_call | solution.py:1185
  300.0 73.2 %attend_back.2 = (bf16[3,3,64,3072]{3,2,1,0:T(8,128)(2,1)}, f32[3,1,3584]{2,1,0:T(1,128)}) custom-call(s32[1]{0:T(128)} %bitcast.96, f32[4,1,3584]{2,1,0:T(1,128)} %broadcast_in_dim.15.pattern_ref, bf16[768,3072]{1,0:T(8,128)(2,1)} %bitcast.72, bf16[768,3072]{1,0:T(8,128)(2,1)} %bitcast.73, bf16[768,3072]{1,0:T(8,128)(2,1)} %bitcast.74, ...), custom_call_target="tpu_custom_call" | custom-call | tf_op jit(solution)/shard_map/attend_back/pallas_call | solution.py:277
  373.2 34.1 %attend_back.3 = (bf16[3,1,64,3072]{3,2,1,0:T(8,128)(2,1)}, f32[1,1,3584]{2,1,0:T(1,128)}) custom-call(s32[1]{0:T(128)} %bitcast.97, f32[4,1,3584]{2,1,0:T(1,128)} %broadcast_in_dim.15.pattern_ref, bf16[768,3072]{1,0:T(8,128)(2,1)} %bitcast.75, bf16[768,3072]{1,0:T(8,128)(2,1)} %bitcast.76, bf16[768,3072]{1,0:T(8,128)(2,1)} %bitcast.77, ...), custom_call_target="tpu_custom_call" | custom-call | tf_op jit(solution)/shard_map/attend_back/pallas_call | solution.py:277
  407.3 2.4 constant_dynamic-update-slice_fusion.1
  409.9 4.5 bitcast_convert_fusion
  414.4 1.3 collective-permute-start.1
  415.7 8.0 %add_convert_fusion = bf16[4,768,1024]{2,1,0:T(8,128)(2,1)} fusion(bf16[4,768,1024]{2,1,0:T(8,128)(2,1)} %get-tuple-element.80, f32[1024]{0:T(1024)S(1)} %add.113, f32[1024]{0:T(1024)S(1)} %mul.136, f32[4,768]{1,0:T(4,128)S(1)} %add_rsqrt_fusion, f32[4,768]{1,0:T(4,128)S(1)} %broadcast_multiply_fusion), kind=kLoop, calls=%fused_computation.5 | loop fusion | flops 18874368 | bytes 12615680 | tf_op jit(solution)/shard_map/convert_element_type | solution.py:1290
  423.7 0.7 convert_reduce_fusion.1
  424.5 8.8 %bitcast_convert_fusion.1 = (bf16[3,1024,256]{2,1,0:T(8,128)(2,1)S(1)}, f32[3,256,1024]{1,2,0:T(8,128)S(1)}) fusion(bf16[3,256,3072]{2,1,0:T(8,128)(2,1)} %bitcast.79, bf16[3072,1024,1]{1,0,2:T(8,128)(2,1)} %bitcast.85), kind=kOutput, calls=%fused_computation.33 | convolution fusion | flops 4832624640 | bytes 15728640 | tf_op jit(solution)/shard_map/td,cet->cde/dot_general | solution.py:1347
  433.4 0.8 fusion.20
  434.6 0.7 reshape.207
  436.1 5.8 fusion.4
  442.0 1.8 constant_dynamic-slice_fusion
  443.8 2.7 collective-permute-start.2
  446.5 3.5 collective-permute-start.3
  450.0 2.3 collective-permute-start.4
  452.3 7.4 %collective-permute-start.5 = (bf16[768,512]{1,0:T(8,128)(2,1)}, bf16[768,512]{1,0:T(8,128)(2,1)}, u32[]{:S(2)}, u32[]{:S(2)}) collective-permute-start(bf16[768,512]{1,0:T(8,128)(2,1)} %get-tuple-element.143), channel_id=1, source_target_pairs={{0,3},{4,0},{1,1},{5,2},{2,7},{6,4},{3,5},{7,6},{8,11},{12,8},{9,9... | collective-permute-start | bytes 2359304 | tf_op jit(solution)/shard_map/ppermute | solution.py:1345
  459.8 0.9 fusion.27
  461.3 1.4 dynamic_update_slice.3
  462.7 1.5 maximum_maximum_fusion.small_ref
  464.2 7.0 %reduce-scatter.5.cloned.1.call-done.wide_ref.wide = bf16[128,2304]{1,0:T(8,128)(2,1)} async-done(((bf16[128,9216]{1,0:T(8,128)(2,1)}), bf16[128,2304]{1,0:T(8,128)(2,1)}) %reduce-scatter.5.cloned.1.call-update) | async-done | bytes 589840 | tf_op jit(solution)/shard_map/reduce_scatter | solution.py:1358
  471.3 1.1 copy-done.3
  472.3 0.8 copy-done.10
  473.1 79.4 %sums.1 = (f32[3,128,256]{2,1,0:T(8,128)S(1)}, f32[32,256]{1,0:T(8,128)S(1)}, f32[1,128]{1,0:T(1,128)S(1)}) custom-call(bf16[3,1024,256]{2,1,0:T(8,128)(2,1)S(1)} %get-tuple-element.149.grad_qkv_ref, f32[32,256]{1,0:T(8,128)S(1)} %copy-done.10, bf16[128,2304]{1,0:T(8,128)(2,1)S(1)} %copy-done.3, f32[3,128,256]{2,1,0:T(8,128)S(1)} %copy-done.2, ...), custom_call_target="tpu_custom_call" | custom-call | tf_op jit(solution)/shard_map/sums/pallas_call | solution.py:862
  552.6 4.1 moments.1
  557.8 10.4 %reduce_row.1.update_ref = f32[1,128]{1,0:T(1,128)} custom-call(f32[1,128]{1,0:T(1,128)} %copy-done.17), custom_call_target="tpu_custom_call" | custom-call | tf_op jit(solution)/shard_map/reduce_row/pallas_call | solution.py:897
  568.3 2.5 fusion.24
  570.8 1.0 fusion.22
  571.8 0.8 copy-done.21
  572.6 2.1 fusion.18
  574.7 1.4 weights.1
  576.6 1.1 copy.73
  (153 shorter events, 9.9 us)
Async XLA Ops:
  7.2 215.8 %all-gather.2.cloned.1.call-start = ((), (), s32[]{:S(2)}) async-start(), calls=%async_computation.2 | async-start | bytes 21233664 | tf_op jit(solution)/shard_map/all_gather | solution.py:1277
  12.0 106.3 %copy-start.38 = (s32[1,2]{1,0:T(1,128)S(1)}, s32[1,2]{1,0:T(1,128)}, u32[]{:S(2)}) copy-start(s32[1,2]{1,0:T(1,128)} %param.27) | copy-start | bytes 28
  118.3 297.4 %reduce-scatter.3.cloned.1.call-start = ((), (), s32[]{:S(2)}) async-start(), calls=%async_computation.3 | async-start | bytes 11796480 | tf_op jit(solution)/shard_map/reduce_scatter | solution.py:1356
  118.4 24.3 %collective-permute-start = (s32[1,2]{1,0:T(1,128)S(1)}, s32[1,2]{1,0:T(1,128)S(1)}, u32[]{:S(2)}, u32[]{:S(2)}) collective-permute-start(s32[1,2]{1,0:T(1,128)S(1)} %copy-done.38), channel_id=1, source_target_pairs={{0,4},{4,0},{1,5},{5,1},{2,6},{6,2},{3,7},{7,3},{8,12},{12,8},{9,1... | collective-permute-start | bytes 32 | tf_op jit(solution)/shard_map/ppermute | solution.py:1286
  119.3 4.3 copy-start.26
  119.9 295.8 %copy-start.27 = (f32[1024]{0:T(1024)}, f32[1024]{0:T(1024)S(1)}, u32[]{:S(2)}) copy-start(f32[1024]{0:T(1024)S(1)} %mul.136) | copy-start | bytes 12292
  123.7 4.7 slice-start.2
  123.7 4.7 copy-start.39
  130.1 5.7 copy-start.23
  296.8 1.6 copy-start.36
  296.8 1.7 copy-start.37
  296.8 1.7 copy-start.18
  296.8 174.4 %reduce-scatter.5.cloned.1.call-start = ((), (), s32[]{:S(2)}) async-start(), calls=%async_computation.4 | async-start | bytes 2949120 | tf_op jit(solution)/shard_map/reduce_scatter | solution.py:1358
  407.3 2.5 copy-start.25
  409.9 4.5 copy-start.20
  414.4 21.7 %collective-permute-start.1 = (bf16[3072,512]{1,0:T(8,128)(2,1)}, bf16[3072,512]{1,0:T(8,128)(2,1)}, u32[]{:S(2)}, u32[]{:S(2)}) collective-permute-start(bf16[3072,512]{1,0:T(8,128)(2,1)} %bitcast_convert_fusion), channel_id=1, source_target_pairs={{0,4},{4,0},{1,5},{5,1},{2,6},{6,2},{3,7},{7,3},{8,12},{12,8},{9,1... | collective-permute-start | bytes 9437192 | tf_op jit(solution)/shard_map/ppermute | solution.py:1333
  415.7 8.1 %slice-start = ((s8[4718592]{0:T(1024)(128)(4,1)}), s8[524288]{0:T(1024)(128)(4,1)S(1)}, s32[]{:S(2)}) async-start(s8[4718592]{0:T(1024)(128)(4,1)} %bitcast.81), calls=%async_computation.5 | async-start | bytes 1048576
  415.7 8.0 %slice-start.1 = ((s8[4718592]{0:T(1024)(128)(4,1)}), s8[4194304]{0:T(1024)(128)(4,1)S(1)}, s32[]{:S(2)}) async-start(s8[4718592]{0:T(1024)(128)(4,1)} %bitcast.81), calls=%async_computation.6 | async-start | bytes 8388608
  424.5 8.8 %copy-start.24 = (bf16[3,1024,256]{2,1,0:T(8,128)(2,1)S(1)}, bf16[3,1024,256]{2,1,0:T(8,128)(2,1)}, u32[]{:S(2)}) copy-start(bf16[3,1024,256]{2,1,0:T(8,128)(2,1)} %get-tuple-element.79) | copy-start | bytes 4718596
  441.9 17.8 %copy-start.31 = (f32[3,1,3584]{2,1,0:T(1,128)S(1)}, f32[3,1,3584]{2,1,0:T(1,128)}, u32[]{:S(2)}) copy-start(f32[3,1,3584]{2,1,0:T(1,128)} %get-tuple-element.90) | copy-start | bytes 129028
  441.9 17.8 %copy-start.33 = (f32[1,1,3584]{2,1,0:T(1,128)S(1)}, f32[1,1,3584]{2,1,0:T(1,128)}, u32[]{:S(2)}) copy-start(f32[1,1,3584]{2,1,0:T(1,128)} %get-tuple-element.91) | copy-start | bytes 43012
  441.9 17.9 %copy-start.40 = (s32[3072]{0:T(1024)S(1)}, s32[3072]{0:T(1024)}, u32[]{:S(2)}) copy-start(s32[3072]{0:T(1024)} %param.28) | copy-start | bytes 36868
  441.9 20.8 %copy-start.35 = (f32[256]{0:T(256)S(1)}, f32[256]{0:T(256)}, u32[]{:S(2)}) copy-start(f32[256]{0:T(256)} %pad.25.clone) | copy-start | bytes 3076
  441.9 29.3 %copy-start = (f32[1024,128]{1,0:T(8,128)S(1)}, f32[1024,128]{1,0:T(8,128)}, u32[]{:S(2)}) copy-start(f32[1024,128]{1,0:T(8,128)} %wd.3) | copy-start | bytes 1572868
  442.0 29.3 %copy-start.1 = (f32[128,1024]{1,0:T(8,128)S(1)}, f32[128,1024]{1,0:T(8,128)}, u32[]{:S(2)}) copy-start(f32[128,1024]{1,0:T(8,128)} %wu.3) | copy-start | bytes 1572868
  442.0 29.3 %copy-start.2 = (f32[3,128,256]{2,1,0:T(8,128)S(1)}, f32[3,128,256]{2,1,0:T(8,128)}, u32[]{:S(2)}) copy-start(f32[3,128,256]{2,1,0:T(8,128)} %wq.3) | copy-start | bytes 1179652
  442.0 29.3 %copy-start.4 = (f32[256,128]{1,0:T(8,128)S(1)}, f32[256,128]{1,0:T(8,128)}, u32[]{:S(2)}) copy-start(f32[256,128]{1,0:T(8,128)} %wp.3) | copy-start | bytes 393220
  442.0 29.3 %copy-start.13 = (f32[256]{0:T(256)S(1)}, f32[256]{0:T(256)}, u32[]{:S(2)}) copy-start(f32[256]{0:T(256)} %select_maximum_fusion.4) | copy-start | bytes 3076
  443.8 108.8 %copy-start.8 = (f32[3,128,256]{2,1,0:T(8,128)S(1)}, f32[3,128,256]{2,1,0:T(8,128)}, u32[]{:S(2)}) copy-start(f32[3,128,256]{2,1,0:T(8,128)} %mq.1) | copy-start | bytes 1179652
  443.8 124.4 %collective-permute-start.2 = (bf16[768,512]{1,0:T(8,128)(2,1)}, bf16[768,512]{1,0:T(8,128)(2,1)}, u32[]{:S(2)}, u32[]{:S(2)}) collective-permute-start(bf16[768,512]{1,0:T(8,128)(2,1)} %get-tuple-element.146), channel_id=1, source_target_pairs={{0,0},{4,1},{1,2},{5,3},{2,4},{6,5},{3,6},{7,7},{8,8},{12,9},{9,10... | collective-permute-start | bytes 2359304 | tf_op jit(solution)/shard_map/ppermute | solution.py:1345
  446.5 121.7 %collective-permute-start.3 = (bf16[768,512]{1,0:T(8,128)(2,1)}, bf16[768,512]{1,0:T(8,128)(2,1)}, u32[]{:S(2)}, u32[]{:S(2)}) collective-permute-start(bf16[768,512]{1,0:T(8,128)(2,1)} %get-tuple-element.145), channel_id=1, source_target_pairs={{0,1},{4,2},{1,3},{5,0},{2,5},{6,6},{3,7},{7,4},{8,9},{12,10},{9,1... | collective-permute-start | bytes 2359304 | tf_op jit(solution)/shard_map/ppermute | solution.py:1345
  450.0 118.2 %collective-permute-start.4 = (bf16[768,512]{1,0:T(8,128)(2,1)}, bf16[768,512]{1,0:T(8,128)(2,1)}, u32[]{:S(2)}, u32[]{:S(2)}) collective-permute-start(bf16[768,512]{1,0:T(8,128)(2,1)} %get-tuple-element.144), channel_id=1, source_target_pairs={{0,2},{4,3},{1,0},{5,1},{2,6},{6,7},{3,4},{7,5},{8,10},{12,11},{9,... | collective-permute-start | bytes 2359304 | tf_op jit(solution)/shard_map/ppermute | solution.py:1345
  452.3 115.9 %collective-permute-start.5 = (bf16[768,512]{1,0:T(8,128)(2,1)}, bf16[768,512]{1,0:T(8,128)(2,1)}, u32[]{:S(2)}, u32[]{:S(2)}) collective-permute-start(bf16[768,512]{1,0:T(8,128)(2,1)} %get-tuple-element.143), channel_id=1, source_target_pairs={{0,3},{4,0},{1,1},{5,2},{2,7},{6,4},{3,5},{7,6},{8,11},{12,8},{9,9... | collective-permute-start | bytes 2359304 | tf_op jit(solution)/shard_map/ppermute | solution.py:1345
  471.3 1.1 copy-start.3
  473.1 79.5 %copy-start.5 = (f32[128,1024]{1,0:T(8,128)S(1)}, f32[128,1024]{1,0:T(8,128)}, u32[]{:S(2)}) copy-start(f32[128,1024]{1,0:T(8,128)} %mu.1) | copy-start | bytes 1572868
  473.1 79.5 %copy-start.6 = (f32[1024,128]{1,0:T(8,128)S(1)}, f32[1024,128]{1,0:T(8,128)}, u32[]{:S(2)}) copy-start(f32[1024,128]{1,0:T(8,128)} %md.1) | copy-start | bytes 1572868
  473.1 79.5 %copy-start.7 = (f32[128,1024]{1,0:T(8,128)S(1)}, f32[128,1024]{1,0:T(8,128)}, u32[]{:S(2)}) copy-start(f32[128,1024]{1,0:T(8,128)} %su.1) | copy-start | bytes 1572868
  473.1 79.5 %copy-start.9 = (f32[3,128,256]{2,1,0:T(8,128)S(1)}, f32[3,128,256]{2,1,0:T(8,128)}, u32[]{:S(2)}) copy-start(f32[3,128,256]{2,1,0:T(8,128)} %sq.1) | copy-start | bytes 1179652
  473.1 79.5 %copy-start.11 = (f32[256,128]{1,0:T(8,128)S(1)}, f32[256,128]{1,0:T(8,128)}, u32[]{:S(2)}) copy-start(f32[256,128]{1,0:T(8,128)} %mp.1) | copy-start | bytes 393220
  473.1 79.5 %copy-start.12 = (f32[256,128]{1,0:T(8,128)S(1)}, f32[256,128]{1,0:T(8,128)}, u32[]{:S(2)}) copy-start(f32[256,128]{1,0:T(8,128)} %sp.1) | copy-start | bytes 393220
  568.2 2.6 copy-start.19
  568.2 2.6 copy-start.28
  568.2 2.6 copy-start.30
  568.2 2.6 copy-start.32
  570.7 1.9 copy-start.21
  572.6 2.1 copy-start.15
  572.6 2.1 copy-start.16
  574.7 1.8 copy-start.22
  (9 other events, 6.6 us)
Sparse Core Ops, SparseCore 0:
  118.4 104.4 all-gather.1
  297.0 95.0 reduce-scatter.2
  415.8 55.3 reduce-scatter.4

commit v3 on v2

--- a/solution.py
+++ b/solution.py
@@ -1,4 +1,5 @@
 import functools
+import math
 
 import jax
 import jax.numpy as jnp
@@ -27,6 +28,45 @@
     return lax.dot_general(
         left, right, (((left_dim,), (right_dim,)), ((), ())), preferred_element_type=F32
     )
+
+
+def project_kernel(x_ref, norm_ref, w_ref, a_ref, qkv_ref, turned):
+    @pl.when(pl.program_id(0) == 0)
+    def _():
+        for c in range(3):
+            turned[c] = w_ref[c].T
+
+    values = x_ref[...].astype(F32)
+    center = values - jnp.mean(values, axis=-1, keepdims=True)
+    inverse = lax.rsqrt(jnp.mean(center * center, axis=-1, keepdims=True) + 1e-05)
+    a_ref[...] = (center * inverse * norm_ref[0:1, :] + norm_ref[1:2, :]).astype(BF)
+    for c in range(3):
+        qkv_ref[c] = dot(turned[c], a_ref[...], 1, 1).astype(BF)
+
+
+def project(rows, norm, weights):
+    tok, width = rows.shape
+    cols = weights.shape[2]
+    return pl.pallas_call(
+        project_kernel,
+        grid=(tok // BLK,),
+        in_specs=[
+            pl.BlockSpec((BLK, width), lambda s: (s, 0)),
+            pl.BlockSpec((2, width), lambda s: (0, 0)),
+            pl.BlockSpec((3, width, cols), lambda s: (0, 0, 0)),
+        ],
+        out_specs=[
+            pl.BlockSpec((BLK, width), lambda s: (s, 0)),
+            pl.BlockSpec((3, cols, BLK), lambda s: (0, 0, s)),
+        ],
+        out_shape=[
+            jax.ShapeDtypeStruct((tok, width), BF),
+            jax.ShapeDtypeStruct((3, cols, tok), BF),
+        ],
+        scratch_shapes=[pltpu.VMEM((3, cols, width), BF)],
+        compiler_params=pltpu.CompilerParams(vmem_limit_bytes=40 * 2**20),
+        name="project",
+    )(rows, norm, weights)
 
 
 def make_slab(pattern, slab):
@@ -190,10 +230,10 @@
 
 
 def attend_back_kernel(
-    shape, first_head, split_ref, pattern_ref, q_ref, k_ref, v_ref, o_ref, lse_ref, given_ref,
-    grads_ref, dpattern_ref,
-    slab, dslab, kx, qx, vx, dox, qn, don, dk, dv, taken,
-    local_sem, in_send, in_recv,
+    shape, segments, split_ref, pattern_ref, q_ref, k_ref, v_ref, o_ref, lse_ref, given_ref, wide_ref,
+    grads_ref, wide_parts_ref, dpattern_ref,
+    slab, dslab, kx, qx, vx, dox, qn, don, dk, dv, taken, wide_own, wide_in,
+    local_sem, in_send, in_recv, wide_sem, z_send, z_recv, w_send, w_recv,
 ):
     head = pl.program_id(0)
     tok = q_ref.shape[1]
@@ -202,18 +242,75 @@
     heads = taken.shape[0]
 
     def in_piece(h, n):
-        return given_ref.at[n, first_head + h]
+        return given_ref.at[n, h]
 
     def in_slot(h, n):
         return taken.at[h, :, pl.ds(pl.multiple_of(n * trade.rows, trade.rows), trade.rows)]
 
+    xy, core, zh, zl = trade.me
+    side = math.isqrt(shape["xy"])
+
+    def column_copies():
+        at = (lax.div(xy, side), lax.rem(xy, side))
+        for step in range(1, side):
+            for n, (start, size, axis) in enumerate(segments):
+                there = lax.rem(at[axis] + step, side)
+                column = there * side + at[1] if axis == 0 else at[0] * side + there
+                here = pl.ds(start, size)
+                yield send(
+                    wide_ref.at[step, :, here], wide_in.at[step - 1, :, here],
+                    w_send.at[step - 1, n], w_recv.at[step - 1, n], (column, core, zh, zl),
+                )
+
+    bring = pltpu.make_async_copy(wide_ref.at[0], wide_own, wide_sem.at[1])
+
     @pl.when(head == 0)
     def _():
-        greet_column(shape)
+        greet(shape)
+        bring.start()
+        for copy in column_copies():
+            copy.start()
         for h in range(heads):
             trade.give(
                 h, in_piece, in_slot, trade.header, trade.row, local_sem.at[h], in_send, in_recv
             )
+
+    size = wide_parts_ref.shape[2]
+
+    def wide_part(n):
+        return wide_own.at[:, pl.ds(pl.multiple_of(n * size, size), size)]
+
+    def along_z(step):
+        there = lax.rem(trade.row + step, trade.parts)
+        return there, (
+            trade.me[0], trade.me[1], lax.div(there, trade.places), lax.rem(there, trade.places),
+        )
+
+    def wide_copy(step):
+        there, device = along_z(step)
+        return send(
+            wide_part(there), wide_parts_ref.at[trade.row], z_send.at[step], z_recv.at[trade.row], device
+        )
+
+    keep_wide = pltpu.make_async_copy(
+        wide_part(trade.row), wide_parts_ref.at[trade.row], wide_sem.at[0]
+    )
+
+    @pl.when(head == min(1, heads - 1))
+    def _():
+        bring.wait()
+        for copy in column_copies():
+            copy.wait_recv()
+            copy.wait_send()
+        for n in range(trade.parts):
+            here = slice(n * size, (n + 1) * size)
+            total = wide_own[:, here].astype(F32)
+            for step in range(side - 1):
+                total = total + wide_in[step, :, here].astype(F32)
+            wide_own[:, here] = total.astype(BF)
+        keep_wide.start()
+        for step in range(1, trade.parts):
+            wide_copy(step).start()
 
     make_slab(pattern_ref[0], slab)
     put_queries(q_ref[...], split, -lse_ref[0], tok, qx)
@@ -267,33 +364,45 @@
         grads_ref[2, 0, :, here] = dv[here, :].T.astype(BF)
     dpattern_ref[0] = fold_slab(dslab)
 
-
-def attend_back(shape, qkv, out, given, lse, pattern, split, heads, first_head, count, collective_id):
+    @pl.when(head == heads - 1)
+    def _():
+        keep_wide.wait()
+        for step in range(1, trade.parts):
+            there, device = along_z(step)
+            here = wide_parts_ref.at[there]
+            wide_copy(step).wait_send()
+            send(here, here, z_send.at[step], z_recv.at[there], device).wait_recv()
+
+
+def attend_back(shape, segments, qkv, out, given, wide, lse, pattern, split, heads):
     tok = qkv.shape[1]
     width = pattern.shape[-1]
     parts = shape["zh"] * shape["zl"]
     anywhere = pl.BlockSpec(memory_space=pl.ANY)
     dma = pltpu.SemaphoreType.DMA
     return pl.pallas_call(
-        functools.partial(attend_back_kernel, shape, first_head),
-        grid=(count,),
+        functools.partial(attend_back_kernel, shape, segments),
+        grid=(heads,),
         in_specs=[
             pl.BlockSpec(memory_space=pltpu.SMEM),
-            pl.BlockSpec((1, 1, width), lambda h: (first_head + h, 0, 0)),
-            pl.BlockSpec((DH, tok), lambda h: (first_head + h, 0)),
-            pl.BlockSpec((DH, tok), lambda h: (first_head + h + heads, 0)),
-            pl.BlockSpec((DH, tok), lambda h: (first_head + h + 2 * heads, 0)),
-            pl.BlockSpec((1, DH, tok), lambda h: (first_head + h, 0, 0)),
-            pl.BlockSpec((1, 1, tok), lambda h: (first_head + h, 0, 0)),
+            pl.BlockSpec((1, 1, width), lambda h: (h, 0, 0)),
+            pl.BlockSpec((DH, tok), lambda h: (h, 0)),
+            pl.BlockSpec((DH, tok), lambda h: (h + heads, 0)),
+            pl.BlockSpec((DH, tok), lambda h: (h + 2 * heads, 0)),
+            pl.BlockSpec((1, DH, tok), lambda h: (h, 0, 0)),
+            pl.BlockSpec((1, 1, tok), lambda h: (h, 0, 0)),
+            anywhere,
             anywhere,
         ],
         out_specs=[
             pl.BlockSpec((3, 1, DH, tok), lambda h: (0, h, 0, 0)),
+            anywhere,
             pl.BlockSpec((1, 1, width), lambda h: (h, 0, 0)),
         ],
         out_shape=[
-            jax.ShapeDtypeStruct((3, count, DH, tok), BF),
-            jax.ShapeDtypeStruct((count, 1, width), F32),
+            jax.ShapeDtypeStruct((3, heads, DH, tok), BF),
+            jax.ShapeDtypeStruct((parts, wide.shape[1], wide.shape[2] // parts), BF),
+            jax.ShapeDtypeStruct((heads, 1, width), F32),
         ],
         scratch_shapes=[
             pltpu.VMEM((BLK, width), F32),
@@ -306,16 +415,20 @@
             pltpu.VMEM((tok, DH), BF),
             pltpu.VMEM((tok, DH), F32),
             pltpu.VMEM((tok, DH), F32),
-            pltpu.VMEM((count, DH, tok), BF),
-            dma((count,)),
-            dma((count, parts)),
-            dma((count, parts)),
+            pltpu.VMEM((heads, DH, tok), BF),
+            pltpu.VMEM(wide.shape[1:], BF),
+            pltpu.VMEM((wide.shape[0] - 1, *wide.shape[1:]), BF),
+            dma((heads,)),
+            dma((heads, parts)),
+            dma((heads, parts)),
+            dma((2,)), dma((parts,)), dma((parts,)),
+            *[dma((wide.shape[0] - 1, len(segments)))] * 2,
         ],
         compiler_params=pltpu.CompilerParams(
-            vmem_limit_bytes=60 * 2**20, collective_id=collective_id, has_side_effects=True
+            vmem_limit_bytes=60 * 2**20, collective_id=1, has_side_effects=True
         ),
         name="attend_back",
-    )(split, pattern, qkv, qkv, qkv, out, lse, given)
+    )(split, pattern, qkv, qkv, qkv, out, lse, given, wide)
 
 
 def place():
@@ -692,42 +805,38 @@
     )(tokens, wq, small, wide)
 
 
-def add_over_devices(shape, me, value, column_slots, plane_slots, sems):
-    xy, core, zh, zl = me
-    mine = (core * 2 + zh) * shape["zl"] + zl
-    column_slots[mine] = value
-    sent = []
-    for step, there, device in column_peers(shape, me):
-        copy = send(
-            column_slots.at[mine], column_slots.at[mine], sems.at[0, step], sems.at[1, mine], device
+class AllSum:
+    def __init__(self, shape, column_slots, plane_slots, sems):
+        self.shape, self.me = shape, place()
+        self.slots, self.sems = (column_slots, plane_slots), sems
+        xy, core, zh, zl = self.me
+        self.mine = ((core * 2 + zh) * shape["zl"] + zl, xy)
+
+    def peers(self, turn):
+        return (column_peers if turn == 0 else plane_peers)(self.shape, self.me)
+
+    def start(self, turn, value):
+        slots, mine = self.slots[turn], self.mine[turn]
+        slots[mine] = value
+        for step, _, device in self.peers(turn):
+            self.copy(turn, step, mine, device).start()
+
+    def copy(self, turn, step, slot, device):
+        here = self.slots[turn].at[slot]
+        return send(
+            here, here, self.sems.at[2 * turn, step], self.sems.at[2 * turn + 1, slot], device
         )
-        copy.start()
-        sent.append(copy)
-    for step, there, device in column_peers(shape, me):
-        send(
-            column_slots.at[there], column_slots.at[there], sems.at[0, step], sems.at[1, there], device
-        ).wait_recv()
-    for copy in sent:
-        copy.wait_send()
-    total = column_slots[0]
-    for slot in range(1, 4 * shape["zl"]):
-        total = total + column_slots[slot]
-    plane_slots[xy] = total
-    sent = []
-    for step, there, device in plane_peers(shape, me):
-        copy = send(plane_slots.at[xy], plane_slots.at[xy], sems.at[2, step], sems.at[3, xy], device)
-        copy.start()
-        sent.append(copy)
-    for step, there, device in plane_peers(shape, me):
-        send(
-            plane_slots.at[there], plane_slots.at[there], sems.at[2, step], sems.at[3, there], device
-        ).wait_recv()
-    for copy in sent:
-        copy.wait_send()
-    total = plane_slots[0]
-    for slot in range(1, shape["xy"]):
-        total = total + plane_slots[slot]
-    return total
+
+    def finish(self, turn):
+        slots = self.slots[turn]
+        for step, there, device in self.peers(turn):
+            self.copy(turn, step, there, device).wait_recv()
+        for step, _, device in self.peers(turn):
+            self.copy(turn, step, self.mine[turn], device).wait_send()
+        total = slots[0]
+        for slot in range(1, slots.shape[0]):
+            total = total + slots[slot]
+        return total
 
 
 LANES = 256
@@ -753,39 +862,116 @@
     return row
 
 
+class Rows:
+    def __init__(self, shape):
+        self.me = place()
+        self.places = shape["zl"]
+
+    def shard_at(self, index):
+        return jnp.where(self.me[2] == 1, index, 2 * self.places - 1 - index)
+
+    def early(self, group):
+        return jnp.where(group == 1, 0, 2 * self.places - 1)
+
+    def owner(self, shard):
+        return (self.me[0], self.me[2], lax.div(shard, self.places), lax.rem(shard, self.places))
+
+    def copy(self, src, dst, half, shard, send_sems, recv_sems):
+        xy, core, zh, zl = self.me
+        there = dst.at[zl, :, pl.ds(pl.multiple_of(core * half, half), half)]
+        return send(src, there, send_sems.at[shard], recv_sems.at[zl, core], self.owner(shard))
+
+    def take(self, dst, half, send_sems, recv_sems):
+        xy, core, zh, zl = self.me
+        for n in range(self.places):
+            for c in range(2):
+                here = dst.at[n, :, c * half : (c + 1) * half]
+                copy = send(here, here, send_sems.at[0], recv_sems.at[n, c], (xy, c, core, n))
+
+                @pl.when(jnp.logical_not(is_same((xy, c, core, n), self.me)))
+                def _():
+                    copy.wait_recv()
+
+
 def sums_kernel(
     shape, n_bias, n_gain,
-    grad_qkv_ref, small_ref, wide_ref, wq_ref, wp_ref, wu_ref, wd_ref, ws_ref,
-    sum_ref, small_sum_ref, totals_ref,
-    plane, both, pieces, small_column, small_plane, row_column, row_plane,
-    p_send, p_recv, q_send, q_recv, local_sems, small_sems, row_sems,
+    first_ref, grad_qkv_ref, small_ref, parts_ref, wq_ref, wp_ref, wu_ref, wd_ref, ws_ref,
+    rows_ref, added_ref, sum_ref, wide_ref, small_sum_ref, totals_ref,
+    taken, added, plane, both, pieces, small_column, small_plane, row_column, row_plane,
+    t_send, t_recv, o_send, o_recv, p_send, p_recv, q_send, q_recv, local_sems, small_sems, row_sems,
 ):
     me = place()
     xy, core, zh, zl = me
     places, columns = shape["zl"], shape["xy"]
+    parts = 2 * places
     z = zh * places + zl
+    sibling = (xy, 1 - core, zh, zl)
     head_block = zl * 2 + core
+    rows, half = taken.shape[1], taken.shape[2]
+    moves = Rows(shape)
+    shard_at = moves.shard_at
     depth = both.shape[1] // 2
-    greet(shape)
+    small_all = AllSum(shape, small_column, small_plane, small_sems)
+    row_all = AllSum(shape, row_column, row_plane, row_sems)
+
+    def columns_at(which):
+        return pl.ds(pl.multiple_of(which * half, half), half)
+
+    def to_sibling(shard):
+        part = first_ref.at[pl.ds(pl.multiple_of(shard * rows, rows), rows), columns_at(1 - core)]
+        return send(part, taken.at[shard], t_send.at[shard], t_recv.at[shard], sibling)
+
+    def to_owner():
+        shard = shard_at(0)
+        return moves.copy(added.at[shard], rows_ref, half, shard, o_send, o_recv)
+
+    keep_added = pltpu.make_async_copy(added, added_ref, local_sems.at[0])
+
+    def add_rows(index):
+        shard = shard_at(index)
+        to_sibling(shard).wait_recv()
+        here = first_ref[pl.ds(pl.multiple_of(shard * rows, rows), rows), columns_at(core)]
+        added[shard] = (here.astype(F32) + taken[shard].astype(F32)).astype(BF)
 
     def plane_part(column):
         return grad_qkv_ref.at[:, pl.ds(pl.multiple_of(column * 2 * depth, 2 * depth), 2 * depth), :]
 
-    keep_part = pltpu.make_async_copy(plane_part(xy), plane.at[xy], local_sems.at[0])
+    def target(c):
+        return (xy, c, lax.div(head_block, places), lax.rem(head_block, places))
+
+    def source(n):
+        return (xy, lax.rem(z, 2), n, lax.div(z, 2))
+
+    def part(c):
+        return both.at[:, c * depth : (c + 1) * depth, :]
+
+    greet(shape)
+    to_sibling(shard_at(0)).start()
+    small_all.start(0, small_ref[...])
+    keep_part = pltpu.make_async_copy(plane_part(xy), plane.at[xy], local_sems.at[1])
     keep_part.start()
     for step, there, device in plane_peers(shape, me):
         send(plane_part(there), plane.at[xy], p_send.at[step], p_recv.at[xy], device).start()
+    for index in range(1, parts):
+        to_sibling(shard_at(index)).start()
+    add_rows(0)
+    to_owner().start()
 
     def square(values):
         wide = values.astype(F32)
         return jnp.sum(wide * wide)
 
+    wide = parts_ref[0].astype(F32)
+    for n in range(1, parts):
+        wide = wide + parts_ref[n].astype(F32)
+    wide_ref[...] = wide
     up, down, proj = parts_of(wide_ref, wu_ref, wp_ref)
     values = [square(proj), square(up), square(down)]
     values += [square(wq_ref[c]) for c in range(3)]
     values += [square(ref[...]) for ref in (wp_ref, wu_ref, wd_ref)]
     ranges = small_ranges(n_bias, n_gain)
     values += lane_sums(ws_ref[...] * ws_ref[...], ranges)
+    small_all.start(1, small_all.finish(0))
 
     keep_part.wait()
     for step, there, device in plane_peers(shape, me):
@@ -795,33 +981,26 @@
         for n in range(1, columns):
             total = total + plane[n, c].astype(F32)
         both[c] = total.astype(BF)
-
-    def target(c):
-        return (xy, c, lax.div(head_block, places), lax.rem(head_block, places))
-
-    def source(n):
-        return (xy, lax.rem(z, 2), n, lax.div(z, 2))
-
-    def part(c):
-        return both.at[:, c * depth : (c + 1) * depth, :]
-
     for c in range(2):
 
         @pl.when(is_same(target(c), me))
         def _():
-            pltpu.make_async_copy(part(c), pieces.at[zh], local_sems.at[1]).start()
+            pltpu.make_async_copy(part(c), pieces.at[zh], local_sems.at[2]).start()
 
         @pl.when(jnp.logical_not(is_same(target(c), me)))
         def _():
             send(part(c), pieces.at[zh], q_send.at[c], q_recv.at[zh], target(c)).start()
 
-    small = add_over_devices(shape, me, small_ref[...], small_column, small_plane, small_sems)
+    for index in range(1, parts):
+        add_rows(index)
+    keep_added.start()
+    small = small_all.finish(1)
     small_sum_ref[...] = small
     for n in range(2):
 
         @pl.when(is_same(target(n), me))
         def _():
-            pltpu.make_async_copy(part(n), pieces.at[zh], local_sems.at[1]).wait()
+            pltpu.make_async_copy(part(n), pieces.at[zh], local_sems.at[2]).wait()
 
         @pl.when(jnp.logical_not(is_same(target(n), me)))
         def _():
@@ -836,7 +1015,9 @@
         total = pieces[0, c].astype(F32) + pieces[1, c].astype(F32)
         sum_ref[c] = total
         squares.append(square(total))
-    row = add_over_devices(shape, me, row_of(squares + values), row_column, row_plane, row_sems)
+    row_all.start(0, row_of(squares + values))
+    row_all.start(1, row_all.finish(0))
+    row = row_all.finish(1)
     lane = lax.broadcasted_iota(jnp.int32, (1, 128), 1)
     for n, value in enumerate(lane_sums(small * small, ranges)):
         row = jnp.where(lane == 17 + n, value, row)
@@ -844,6 +1025,99 @@
 
     for step, there, device in plane_peers(shape, me):
         send(plane_part(there), plane.at[xy], p_send.at[step], p_recv.at[xy], device).wait_send()
+    for shard in range(parts):
+        to_sibling(shard).wait_send()
+    keep_added.wait()
+    to_owner().wait_send()
+
+    @pl.when(z == moves.early(core))
+    def _():
+        moves.take(rows_ref, half, o_send, o_recv)
+
+
+def rows_kernel(
+    shape, added_ref, early_ref, x_ref, middle_ref, gain_ref, out_ref,
+    got, e_sem, keep_sem, o_send, o_recv,
+):
+    me = place()
+    xy, core, zh, zl = me
+    moves = Rows(shape)
+    parts = added_ref.shape[0]
+    half = added_ref.shape[2]
+    z = zh * moves.places + zl
+    is_early = z == moves.early(core)
+    early = pltpu.make_async_copy(early_ref, got, e_sem)
+    mine = got.at[zl, :, pl.ds(pl.multiple_of(core * half, half), half)]
+    keep = pltpu.make_async_copy(added_ref.at[z], mine, keep_sem)
+
+    def each(act):
+        for index in range(1, parts):
+            shard = moves.shard_at(index)
+
+            @pl.when(jnp.logical_not(is_same(moves.owner(shard), me)))
+            def _():
+                act(moves.copy(added_ref.at[shard], got, half, shard, o_send, o_recv))
+
+    greet_column(shape)
+    each(lambda copy: copy.start())
+
+    @pl.when(is_early)
+    def _():
+        early.start()
+
+    @pl.when(zh == core)
+    def _():
+        keep.start()
+
+    value, inverse = normed_of(x_ref[...].astype(F32))
+
+    @pl.when(zh == core)
+    def _():
+        keep.wait()
+
+    @pl.when(is_early)
+    def _():
+        early.wait()
+
+    @pl.when(jnp.logical_not(is_early))
+    def _():
+        moves.take(got, half, o_send, o_recv)
+
+    grad = got[0].astype(F32)
+    for n in range(1, moves.places):
+        grad = grad + got[n].astype(F32)
+    inner = grad * gain_ref[...]
+    out_ref[...] = (
+        middle_ref[...]
+        + inverse
+        * (
+            inner
+            - jnp.mean(inner, axis=-1, keepdims=True)
+            - value * jnp.mean(inner * value, axis=-1, keepdims=True)
+        )
+    ).astype(BF)
+    each(lambda copy: copy.wait_send())
+
+
+def finish_rows(shape, added, early, tokens, grad_middle, gain):
+    places = shape["zl"]
+    vmem = pl.BlockSpec(memory_space=pltpu.VMEM)
+    anywhere = pl.BlockSpec(memory_space=pl.ANY)
+    dma = pltpu.SemaphoreType.DMA
+    return pl.pallas_call(
+        functools.partial(rows_kernel, shape),
+        out_shape=jax.ShapeDtypeStruct(tokens.shape, BF),
+        in_specs=[anywhere, anywhere, vmem, vmem, vmem],
+        out_specs=vmem,
+        scratch_shapes=[
+            pltpu.VMEM((places, *tokens.shape), BF),
+            dma, dma, dma((2 * places,)), dma((places, 2)),
+        ],
+        compiler_params=pltpu.CompilerParams(
+            collective_id=6, has_side_effects=True, vmem_limit_bytes=56 * 2**20
+        ),
+        name="finish_rows",
+    )(added, early, tokens, grad_middle, gain)
 
 
 def parts_of(wide_ref, up_like, proj_like):
@@ -851,24 +1125,31 @@
     return wide_ref[:, :ff], wide_ref[:, ff : 2 * ff], wide_ref[:, 2 * ff : 2 * ff + heads]
 
 
-def sums(shape, n_bias, n_gain, grad_qkv, small, wide, weights):
-    columns = shape["xy"]
-    members = 4 * shape["zl"]
+def sums(shape, n_bias, n_gain, first, grad_qkv, small, wide, weights):
+    places, columns = shape["zl"], shape["xy"]
+    members, parts = 4 * places, 2 * places
+    rows, width = first.shape[0] // parts, first.shape[1]
     depth = grad_qkv.shape[1] // (2 * columns)
     heads_cols = grad_qkv.shape[2]
     vmem = pl.BlockSpec(memory_space=pltpu.VMEM)
+    anywhere = pl.BlockSpec(memory_space=pl.ANY)
     dma = pltpu.SemaphoreType.DMA
     slots = max(members, columns)
     return pl.pallas_call(
         functools.partial(sums_kernel, shape, n_bias, n_gain),
         out_shape=[
+            jax.ShapeDtypeStruct((places, rows, width), BF),
+            jax.ShapeDtypeStruct((parts, rows, width // 2), BF),
             jax.ShapeDtypeStruct((3, depth, heads_cols), F32),
+            jax.ShapeDtypeStruct(wide.shape[1:], F32),
             jax.ShapeDtypeStruct(small.shape, F32),
             jax.ShapeDtypeStruct((1, 128), F32),
         ],
-        in_specs=[pl.BlockSpec(memory_space=pl.ANY)] + [vmem] * 7,
-        out_specs=[vmem] * 3,
+        in_specs=[vmem, anywhere] + [vmem] * 7,
+        out_specs=[anywhere] * 2 + [vmem] * 4,
         scratch_shapes=[
+            pltpu.VMEM((parts, rows, width // 2), BF),
+            pltpu.VMEM((parts, rows, width // 2), BF),
             pltpu.VMEM((columns, 3, 2 * depth, heads_cols), BF),
             pltpu.VMEM((3, 2 * depth, heads_cols), BF),
             pltpu.VMEM((2, 3, depth, heads_cols), BF),
@@ -876,19 +1157,23 @@
             pltpu.VMEM((columns, *small.shape), F32),
             pltpu.VMEM((members, 1, 128), F32),
             pltpu.VMEM((columns, 1, 128), F32),
-            dma((columns,)), dma((columns,)), dma((2,)), dma((2,)), dma((2,)),
+            dma((parts,)), dma((parts,)), dma((parts,)), dma((places, 2)),
+            dma((columns,)), dma((columns,)), dma((2,)), dma((2,)), dma((3,)),
             dma((4, slots)), dma((4, slots)),
         ],
         compiler_params=pltpu.CompilerParams(
-            collective_id=3, has_side_effects=True, vmem_limit_bytes=48 * 2**20
+            collective_id=3, has_side_effects=True, vmem_limit_bytes=56 * 2**20
         ),
         name="sums",
-    )(grad_qkv, small, wide, *weights)
+    )(first, grad_qkv, small, wide, *weights)
 
 
 def reduce_kernel(shape, row_ref, total_ref, row_column, row_plane, row_sems):
     greet(shape)
-    total_ref[...] = add_over_devices(shape, place(), row_ref[...], row_column, row_plane, row_sems)
+    both = AllSum(shape, row_column, row_plane, row_sems)
+    both.start(0, row_ref[...])
+    both.start(1, both.finish(0))
+    total_ref[...] = both.finish(1)
 
 
 def reduce_row(shape, row):
@@ -1031,69 +1316,160 @@
             dst[pl.ds(pl.multiple_of(slot * depth, depth), depth), :] = turned[offset : offset + depth]
 
 
+def normed_of(values):
+    center = values - jnp.mean(values, axis=-1, keepdims=True)
+    inverse = lax.rsqrt(jnp.mean(center * center, axis=-1, keepdims=True) + 1e-05)
+    return center * inverse, inverse
+
+
+class Adder:
+    def __init__(self, side, taken, first, sems):
+        xy, core, zh, zl = place()
+        self.side, self.taken, self.first = side, taken, first
+        self.swap_send, self.swap_recv, *self.sems = sems
+        self.at = (lax.div(xy, side), lax.rem(xy, side))
+        self.rest = (core, zh, zl)
+        self.sibling = (xy, 1 - core, zh, zl)
+
+    def peers(self):
+        xy = self.at[0] * self.side + self.at[1]
+        columns = self.side * self.side
+        return [self.sibling] + [
+            (lax.rem(xy + step, columns), *self.rest) for step in range(1, columns)
+        ]
+
+    def swap(self, other, index):
+        return send(other, self.taken.at[index], self.swap_send.at[index], self.swap_recv.at[index], self.sibling)
+
+    def block(self, index, axis, there):
+        return self.taken.at[index, :, there] if axis == 0 else self.taken.at[index, :, :, there]
+
+    def owned(self, index, axis, step):
+        there = lax.rem(self.at[1 - axis] + step, self.side)
+        if axis == 0:
+            return self.taken.at[index, :, self.at[0], there]
+        return self.taken.at[index, :, there, self.at[1]]
+
+    def copies(self, index, axis):
+        for step in range(1, self.side):
+            there = lax.rem(self.at[axis] + step, self.side)
+            member = (there, self.at[1]) if axis == 0 else (self.at[0], there)
+            yield send(
+                self.block(index, axis, there), self.first.at[index, step - 1],
+                self.sems[0].at[index, step - 1], self.sems[1].at[index, step - 1],
+                (member[0] * self.side + member[1], *self.rest),
+            )
+
+    def by_parity(self, index, act):
+        if isinstance(index, int):
+            act(index % 2)
+            return
+        for parity in range(2):
+
+            @pl.when(lax.rem(index, 2) == parity)
+            def _():
+                act(parity)
+
+    def add_core(self, own, other, index):
+        self.swap(other, index).wait_recv()
+        for which in range(2):
+            self.taken[index, which] = (
+                own[which].astype(F32) + self.taken[index, which].astype(F32)
+            ).astype(BF)
+
+        def start(axis):
+            for copy in self.copies(index, axis):
+                copy.start()
+
+        self.by_parity(index, start)
+
+    def add_first(self, index, keep):
+        def act(axis):
+            mine = self.block(index, axis, self.at[axis])
+            total = mine[...].astype(F32)
+            for step, copy in enumerate(self.copies(index, axis)):
+                copy.wait_recv()
+                total = total + self.first[index, step].astype(F32)
+            mine[...] = total.astype(BF)
+            for copy in keep(index, axis):
+                copy.start()
+
+        self.by_parity(index, act)
+
+    def end(self, index, keep):
+        def act(axis):
+            for copy in self.copies(index, axis):
+                copy.wait_send()
+            for copy in keep(index, axis):
+                copy.wait()
+
+        self.by_parity(index, act)
+
+
 def feed_kernel(
     shape, ff_local, x_ref, c_ref, attn_ref, norm_ref, proj_ref, up_ref, down_ref,
     block_ref, middle_ref, given_ref, wide_ref, sums_ref,
-    middle, total, second, a_second, a_turned, c_turned, own, other, taken, proj_own, proj_other, proj_taken,
-    out_sems, own_sems, swap_send, swap_recv, proj_sems,
+    middle, total, second, a_second, a_turned, c_turned, own, other, taken, first_in,
+    out_sems, keep_sems, proj_sems, *sems,
 ):
-    me = place()
-    xy, core, zh, zl = me
-    sibling = (xy, 1 - core, zh, zl)
     step = pl.program_id(0)
-    steps = pl.num_programs(0)
-    parts = attn_ref.shape[0]
-    heads_cols = attn_ref.shape[1]
-    half, chunk = own.shape[2], own.shape[3]
+    steps = taken.shape[0] - 1
+    parts, heads_cols = attn_ref.shape[:2]
+    side, chunk = own.shape[2], own.shape[5]
+    half = c_turned.shape[0] // 2
     per = ff_local // chunk
     wide = 2 * ff_local + heads_cols
     slot = lax.rem(step, 2)
-
-    def swap(at, index):
-        return send(other.at[at], taken.at[index], swap_send.at[index], swap_recv.at[index], sibling)
-
-    def columns(index, which):
-        start = lax.div(index, per) * wide + which * ff_local + lax.rem(index, per) * chunk
-        return wide_ref.at[:, pl.ds(pl.multiple_of(start, 128), chunk)]
-
-    def keep(at, index, which):
-        return pltpu.make_async_copy(own.at[at, which], columns(index, which), own_sems.at[at, which])
-
-    def add_swapped(at, index):
-        swap(at, index).wait_recv()
-        for which in range(2):
-            own[at, which] = (
-                own[at, which].astype(F32) + taken[index, which].astype(F32)
-            ).astype(BF)
-            keep(at, index, which).start()
-
-    def normed():
-        values = middle[...]
-        center = values - jnp.mean(values, axis=-1, keepdims=True)
-        inverse = lax.rsqrt(jnp.mean(center * center, axis=-1, keepdims=True) + 1e-05)
-        return center * inverse, inverse
+    adder = Adder(side, taken, first_in, sems)
+    halves = own.shape[2:5]
+
+    def keep(index, axis):
+        for step in range(side):
+            for which in range(2):
+                start = index // per * wide + which * ff_local + index % per * chunk
+                if not isinstance(index, int):
+                    start = lax.div(index, per) * wide + which * ff_local + lax.rem(index, per) * chunk
+                    start = pl.multiple_of(start, 128)
+                yield pltpu.make_async_copy(
+                    adder.owned(index, axis, step).at[which], wide_ref.at[step, :, pl.ds(start, chunk)],
+                    keep_sems.at[index, step, which],
+                )
+
+    def keep_proj(index, axis):
+        for step in range(side):
+            for part in range(parts):
+                which, place_in = part // (parts // 2), part % (parts // 2)
+                yield pltpu.make_async_copy(
+                    adder.owned(index, axis, step).at[which, :, pl.ds(place_in * heads_cols, heads_cols)],
+                    wide_ref.at[step, :, pl.ds(part * wide + 2 * ff_local, heads_cols)],
+                    proj_sems.at[step, part],
+                )
+
+    def put(at, which, grad):
+        own[at, which] = grad[:half].reshape(*halves, grad.shape[1])
+        other[at, which] = grad[half:].reshape(*halves, grad.shape[1])
 
     @pl.when(step == 0)
     def _():
         barrier = pltpu.get_barrier_semaphore()
-        pl.semaphore_signal(barrier, inc=1, device_id=sibling, device_id_type=MESH)
+        for peer in adder.peers():
+            pl.semaphore_signal(barrier, inc=1, device_id=peer, device_id_type=MESH)
+        core = lax.axis_index("core")
         mixed = x_ref[...].astype(F32)
         for part in range(parts):
             mixed = mixed + dot(attn_ref[part].T, proj_ref[part], 1, 1)
         middle[...] = mixed
-        value, _ = normed()
+        value, _ = normed_of(mixed)
         a_second[...] = (value * norm_ref[0:1, :] + norm_ref[1:2, :]).astype(BF)
         turn_own_first(shape, core, a_second, a_turned)
         turn_own_first(shape, core, c_ref, c_turned)
         total[...] = jnp.zeros_like(total)
         second[...] = jnp.zeros_like(second)
-        pl.semaphore_wait(barrier, 1)
+        pl.semaphore_wait(barrier, len(adder.peers()))
 
     @pl.when(step >= 2)
     def _():
-        swap(slot, step - 2).wait_send()
-        for which in range(2):
-            keep(slot, step - 2, which).wait()
+        adder.swap(other.at[slot], step - 2).wait_send()
 
     up, down = up_ref[0], down_ref[0]
     pre = dot(a_second[...], up, 1, 0)
@@ -1103,25 +1479,30 @@
     slope = normal + pre * jnp.exp(-0.5 * pre * pre) * 0.3989422804014327
     grad_pre = (slope * grad_hidden).astype(BF)
     total[...] += dot(hidden, down, 1, 1)
-    grad_down = dot(c_turned[...], hidden, 1, 0).astype(BF)
-    own[slot, 1] = grad_down[:half]
-    other[slot, 1] = grad_down[half:]
+    put(slot, 1, dot(c_turned[...], hidden, 1, 0).astype(BF))
     second[...] += dot(grad_pre, up, 1, 1)
-    grad_up = dot(a_turned[...], grad_pre, 1, 0).astype(BF)
-    own[slot, 0] = grad_up[:half]
-    other[slot, 0] = grad_up[half:]
-    swap(slot, step).start()
+    put(slot, 0, dot(a_turned[...], grad_pre, 1, 0).astype(BF))
+    adder.swap(other.at[slot], step).start()
 
     @pl.when(step >= 1)
     def _():
-        add_swapped(1 - slot, step - 1)
+        adder.add_core(own.at[1 - slot], other.at[1 - slot], step - 1)
+
+    @pl.when(step >= 3)
+    def _():
+        adder.add_first(step - 3, keep)
 
     @pl.when(step == steps - 1)
     def _():
+        core = lax.axis_index("core")
+        last = steps - 1
+        here, free = last % 2, 1 - last % 2
+        adder.add_core(own.at[here], other.at[here], last)
+        adder.add_first(last - 2, keep)
         a_second[...] = (middle[...] + total[...]).astype(BF)
         out_block = pltpu.make_async_copy(a_second, block_ref, out_sems.at[0])
         out_block.start()
-        value, inverse = normed()
+        value, inverse = normed_of(middle[...])
         grad = second[...]
         sums_ref[0:1, :] = jnp.sum(grad * value, axis=0, keepdims=True)
         sums_ref[1:2, :] = jnp.sum(grad, axis=0, keepdims=True)
@@ -1135,38 +1516,44 @@
         out_middle.start()
         low = second[...].astype(BF)
         turn_own_first(shape, core, low, a_turned)
-        for part in range(parts):
-            grad_proj = dot(a_turned[...], attn_ref[part], 1, 1).astype(BF)
-            proj_own[part] = grad_proj[:half]
-            proj_other[part] = grad_proj[half:]
-        swap_proj = send(proj_other, proj_taken, proj_sems.at[0], proj_sems.at[1], sibling)
-        swap_proj.start()
+        adder.swap(other.at[free], last - 1).wait_send()
+        in_one = parts // 2
+        for which in range(2):
+            grads = [
+                dot(a_turned[...], attn_ref[which * in_one + n], 1, 1).astype(BF) for n in range(in_one)
+            ]
+            put(free, which, jnp.concatenate(grads, axis=1))
+        adder.swap(other.at[free], steps).start()
+        adder.add_first(last - 1, keep)
         for part in range(parts):
             rows = pl.ds(part * heads_cols, heads_cols)
             c_turned[rows, :] = dot(low, proj_ref[part], 1, 0).T.astype(BF)
         out_given = pltpu.make_async_copy(c_turned, given_ref, out_sems.at[2])
         out_given.start()
-        add_swapped(slot, step)
-        swap_proj.wait_recv()
-        kept = []
-        for part in range(parts):
-            proj_own[part] = (proj_own[part].astype(F32) + proj_taken[part].astype(F32)).astype(BF)
-            there = wide_ref.at[:, pl.ds(part * wide + 2 * ff_local, heads_cols)]
-            kept.append(pltpu.make_async_copy(proj_own.at[part], there, out_sems.at[3 + part]))
-            kept[-1].start()
-
-        @pl.when(step >= 1)
-        def _():
-            swap(1 - slot, step - 1).wait_send()
-            for which in range(2):
-                keep(1 - slot, step - 1, which).wait()
-
-        swap(slot, step).wait_send()
-        for which in range(2):
-            keep(slot, step, which).wait()
-        swap_proj.wait_send()
-        for copy in (out_block, out_middle, out_given, *kept):
+        adder.add_core(own.at[free], other.at[free], steps)
+        adder.add_first(last, keep)
+        adder.add_first(steps, keep_proj)
+        adder.swap(other.at[here], last).wait_send()
+        adder.swap(other.at[free], steps).wait_send()
+        for index in range(steps + 1):
+            adder.end(index, keep if index < steps else keep_proj)
+        for copy in (out_block, out_middle, out_given):
             copy.wait()
+
+
+def column_segments(parts, ff_local, heads_cols):
+    chunk = min(512, ff_local)
+    per = ff_local // chunk
+    wide = 2 * ff_local + heads_cols
+    segments = [
+        (part * wide + which * ff_local + n * chunk, chunk, 1 - (part * per + n) % 2)
+        for part in range(parts)
+        for which in range(2)
+        for n in range(per)
+    ]
+    return segments + [
+        (part * wide + 2 * ff_local, heads_cols, 1 - parts * per % 2) for part in range(parts)
+    ]
 
 
 def feed_forward(shape, tokens, cotangent, attn_rows, norm, shared, ff_local):
@@ -1175,7 +1562,8 @@
     chunk = min(512, ff_local)
     per = ff_local // chunk
     steps = parts * per
-    half = width // 2
+    side = math.isqrt(shape["xy"])
+    depth = width // (2 * shape["xy"])
     anywhere = pl.BlockSpec(memory_space=pl.ANY)
 
     def once(block, *index):
@@ -1199,7 +1587,7 @@
             jax.ShapeDtypeStruct((rows, width), BF),
             jax.ShapeDtypeStruct((rows, width), F32),
             jax.ShapeDtypeStruct((parts * heads_cols, rows), BF),
-            jax.ShapeDtypeStruct((half, parts * (2 * ff_local + heads_cols)), BF),
+            jax.ShapeDtypeStruct((side, depth, parts * (2 * ff_local + heads_cols)), BF),
             jax.ShapeDtypeStruct((2, width), F32),
         ],
         scratch_shapes=[
@@ -1209,20 +1597,20 @@
             pltpu.VMEM((rows, width), BF),
             pltpu.VMEM((width, rows), BF),
             pltpu.VMEM((width, rows), BF),
-            pltpu.VMEM((2, 2, half, chunk), BF),
-            pltpu.VMEM((2, 2, half, chunk), BF),
-            pltpu.VMEM((steps, 2, half, chunk), BF),
-            pltpu.VMEM((parts, half, heads_cols), BF),
-            pltpu.VMEM((parts, half, heads_cols), BF),
-            pltpu.VMEM((parts, half, heads_cols), BF),
-            dma((3 + parts,)),
-            dma((2, 2)),
-            dma((steps,)),
-            dma((steps,)),
-            dma((2,)),
+            pltpu.VMEM((2, 2, side, side, depth, chunk), BF),
+            pltpu.VMEM((2, 2, side, side, depth, chunk), BF),
+            pltpu.VMEM((steps + 1, 2, side, side, depth, chunk), BF),
+            pltpu.VMEM((steps + 1, side - 1, 2, side, depth, chunk), BF),
+            dma((3,)),
+            dma((steps, side, 2)),
+            dma((side, parts)),
+            dma((steps + 1,)),
+            dma((steps + 1,)),
+            dma((steps + 1, side - 1)),
+            dma((steps + 1, side - 1)),
         ],
         compiler_params=pltpu.CompilerParams(
-            vmem_limit_bytes=60 * 2**20, collective_id=5, has_side_effects=True
+            vmem_limit_bytes=62 * 2**20, collective_id=5, has_side_effects=True
         ),
         name="feed_forward",
     )(tokens, cotangent, attn_rows, norm, shared, shared, shared)
@@ -1286,11 +1674,10 @@
     other_len = lax.ppermute(item_len, "core", [(0, 1), (1, 0)])
     split = jnp.where(zh == core, item_len, other_len)[0, 0:1]
 
-    normed_all, _ = norm_parts(group_rows.reshape(tok, width).astype(F32))
-    a_first = (normed_all * gains[0] + shifts[0]).astype(BF)
-    qkv = lax.dot_general(
-        w_heads, a_first, (((1,), (1,)), ((), ())), preferred_element_type=F32
-    ).astype(BF).reshape(3 * heads * DH, tok)
+    a_first, qkv = project(
+        group_rows.reshape(tok, width), jnp.stack([gains[0], shifts[0]]), w_heads
+    )
+    qkv = qkv.reshape(3 * heads * DH, tok)
 
     table = lax.dynamic_slice_in_dim(
         table_flat.reshape(BUCKETS, H), head_block * heads, heads, 1
@@ -1305,45 +1692,21 @@
     out, attn_rows, lse = attend(shape, qkv, pattern, split, heads)
 
     attn_rows = attn_rows.reshape(parts, heads * DH, rows)
-    x_rows = tokens.astype(F32)
     norm_two = jnp.stack([gains[1], shifts[1]])
     block_out, grad_middle, grad_attn, wide_grad, sums_two = feed_forward(
         shape, tokens, cotangent, attn_rows, norm_two, shared, ff_local
     )
     gain_two, shift_two = sums_two[0], sums_two[1]
     given = grad_attn.reshape(parts, heads, DH, rows)
-    early = heads - 1
-    heads_early, pattern_early = attend_back(
-        shape, qkv, out, given, lse, pattern, split, heads, 0, early, 1
+    grad_heads, wide_parts, grad_pattern = attend_back(
+        shape, column_segments(parts, ff_local, w_proj.shape[0]), qkv, out, given, wide_grad, lse, pattern,
+        split, heads,
     )
-    heads_late, pattern_late = attend_back(
-        shape, qkv, out, given, lse, pattern, split, heads, early, heads - early, 6
-    )
-    grad_pattern = jnp.concatenate([pattern_early, pattern_late])
-    grad_heads = jnp.concatenate([heads_early, heads_late], axis=1).reshape(3, heads * DH, tok)
-
-    half = width // 2
-
-    def first_half(which):
-        here = lax.dynamic_slice_in_dim(w_heads, which * half, half, 1)
-        return lax.dot_general(
-            grad_heads, here, (((0, 1), (0, 2)), ((), ())), preferred_element_type=F32
-        )
-
-    other_half = lax.ppermute(first_half(1 - core).astype(BF), "core", [(0, 1), (1, 0)])
-    half_sum = (first_half(core) + other_half.astype(F32)).astype(BF)
-    arrived = []
-    for turn in range(parts):
-        route = [
-            (((c * 2 + b % 2) * 2 + g) * places + b // 2, (c * 2 + g) * parts + (b + turn) % parts)
-            for c in range(columns)
-            for g in range(2)
-            for b in range(parts)
-        ]
-        shard = lax.rem(head_block + turn, parts)
-        piece = lax.dynamic_slice_in_dim(half_sum, shard * rows, rows, 0)
-        arrived.append(lax.ppermute(piece, ALL, route))
-
+    grad_heads = grad_heads.reshape(3, heads * DH, tok)
+
+    first = lax.dot_general(
+        grad_heads, w_heads, (((0, 1), (0, 2)), ((), ())), preferred_element_type=F32
+    ).astype(BF)
     grad_qkv = jnp.einsum("td,cet->cde", a_first, grad_heads, preferred_element_type=F32)
     head_sums = jnp.sum(grad_heads.astype(F32), axis=2)
     wide_heads = w_heads.astype(F32)
@@ -1353,9 +1716,6 @@
     ) / gains[0]
     grad_qkv = grad_qkv.astype(BF)
 
-    part = lax.psum_scatter(wide_grad, "xy", scatter_dimension=0, tiled=True)
-    part, heads_early = lax.optimization_barrier((part, heads_early))
-    wide_sum = lax.psum_scatter(part, TENSOR, scatter_dimension=1, tiled=True)
     bias_grad = lax.dot_general(
         one_hot, grad_pattern[:, 0, :tok], (((1,), (1,)), ((), ())),
         precision=HIGHEST, preferred_element_type=F32,
@@ -1377,8 +1737,8 @@
         axis=1,
     )
     weights = (w_qkv, w_proj, w_up, w_down, small_weights)
-    sum_qkv, small_sum, totals = sums(
-        shape, n_bias, n_gain, grad_qkv, small_grad, wide_sum, weights
+    early_rows, added, sum_qkv, wide_sum, small_sum, totals = sums(
+        shape, n_bias, n_gain, first, grad_qkv, small_grad, wide_parts, weights
     )
     small_like = [rel_bias[None, :], ln_gain, ln_shift]
     updates_total, grad_norm, param_norms, *results = optimizer(
@@ -1388,16 +1748,8 @@
         (square_qkv, square_proj, square_up, square_down, pack(square_bias, square_gain, square_shift)),
         small_like,
     )
-    arrived, _ = lax.optimization_barrier((arrived, updates_total))
-    rounds = [sum(piece.astype(F32) for piece in arrived[n::2]) for n in range(2)]
-    even = lax.rem(zh * places + zl, 2) == 0
-    first_rows = jnp.concatenate(
-        [jnp.where(even, rounds[0], rounds[1]), jnp.where(even, rounds[1], rounds[0])], axis=1
-    )
-    normed_one, inverse_one = norm_parts(x_rows)
-    grad_tokens = (
-        grad_middle + norm_back(normed_one, inverse_one, gains[0], first_rows)
-    ).astype(BF)
+    added, _ = lax.optimization_barrier((added, updates_total))
+    grad_tokens = finish_rows(shape, added, early_rows, tokens, grad_middle, gains[0:1])
     new = [array if n % 7 != 4 else array[0] for group in results for n, array in enumerate(group)]
     return (block_out, grad_tokens, grad_norm[0, 0], param_norms, *new)
 

time: 596 us -> 576 us (0.966)
  Pallas kernels: 457 us -> 503 us
  other arithmetic: 39.2 us -> 13.9 us
  starting transfers between devices: 17.5 us -> 0.11 us
  matrix products: 27.1 us -> 15 us
    pallas_call x2 -> x3, Pallas kernels: 107 us -> 152 us  [the longest x1 97.2 us: attend_back(): pl.pallas_call(functools.partial(attend_back_kernel, shape, segments), gr...]
    ppermute x5 -> x0, starting transfers between devices: 17.3 us -> none  [the longest x4 16 us: per_device(): arrived.append(lax.ppermute(piece, ALL, route))]
    convert_element_type x3 -> x0, other arithmetic: 15.8 us -> none  [the longest x2 13.7 us: per_device(): a_first = (normed_all * gains[0] + shifts[0]).astype(BF)]
    pallas_call x1, Pallas kernels: 73.7 us -> 86 us  [feed_forward(): pl.pallas_call(functools.partial(feed_kernel, shape, ff_local), grid=(ste...]
    pallas_call x1, Pallas kernels: 79.4 us -> 67.5 us  [sums(): pl.pallas_call(functools.partial(sums_kernel, shape, n_bias, n_gain), out...]
    reduce_sum x5 -> x0, other arithmetic: 10.1 us -> none  [the longest x2 5.14 us: norm_parts(): jnp.mean(center * center, axis=-1, keepdims=True) + 1e-05]
    dot_general x3 -> x1, matrix products: 17.1 us -> 7.1 us  [per_device(): lax.dot_general(grad_heads, w_heads, (((0, 1), (0, 2)), ((), ())), prefer...]
    reduce_scatter x2 -> x0, waiting for transfers between devices: 7.03 us -> none  [the longest x1 7.03 us: per_device(): wide_sum = lax.psum_scatter(part, TENSOR, scatter_dimension=1, tiled=True)]
  transfers between devices with their start and end apart: 9 -> 2, of which waited for: 2 -> 1; matrix products, arithmetic and copies ran while one was open for 11% -> 1% of each run, Pallas kernels for 48% -> 16%
where the time goes in v3:
time: 576 us; the launch traced here: 570 us
  Pallas kernels  503 us (87%)
  local copies, waits for them, and re-layouts  17.6 us (3%)
  matrix products  15 us (3%)
  between operations  14.8 us (3%)
  other arithmetic  13.9 us (2%)
    pallas_call x1, Pallas kernels, gather(): pl.pallas_call(functools.partial(gather_kernel, shape), out_shape=[jax.Sh...  102 us
    pallas_call x1, Pallas kernels, attend_back(): pl.pallas_call(functools.partial(attend_back_kernel, shape, segments), gr...  97.2 us
    pallas_call x1, Pallas kernels, feed_forward(): pl.pallas_call(functools.partial(feed_kernel, shape, ff_local), grid=(ste...  86 us
    pallas_call x1, Pallas kernels, attend(): pl.pallas_call(functools.partial(attend_kernel, shape), grid=(heads,), in...  78.4 us
    pallas_call x1, Pallas kernels, sums(): pl.pallas_call(functools.partial(sums_kernel, shape, n_bias, n_gain), out...  67.5 us
    pallas_call x1, Pallas kernels, finish_rows(): pl.pallas_call(functools.partial(rows_kernel, shape), out_shape=jax.Shape...  43.8 us
    unnamed x78, local copies, waits for them, and re-layouts  13.2 us
  transfers between devices with their start and end apart: 2, of which 1 were waited for; matrix products, arithmetic and copies ran while one was open for 1% of the time, Pallas kernels for 16%

profile of v3, /device:TPU:8, one launch (start us, length us, event | category | flops | bytes accessed | tf_op | source)
XLA Modules:
  0.0 569.7 jit_solution(12067549824087904989)
XLA Ops:
  7.2 0.8 reshape.123
  8.0 0.8 reshape.124
  8.8 1.2 copy.57
  9.9 1.1 convert.11
  11.0 1.0 copy.58
  12.1 1.7 convert_element_type.22.wq_ref
  13.7 1.3 select_maximum_fusion.4
  15.1 0.9 pad_maximum_fusion.wide_ref
  15.9 102.4 %gather.1 = (bf16[4,768,1024]{2,1,0:T(8,128)(2,1)}, bf16[3,1024,256]{2,1,0:T(8,128)(2,1)}, f32[8,4,1,256]{3,2,1,0:T(1,128)}, bf16[4,128,2304]{2,1,0:T(8,128)(2,1)}) custom-call(bf16[768,1024]{1,0:T(8,128)(2,1)} %x_ref.3, bf16[3,128,256]{2,1,0:T(8,128)(2,1)} %convert_element_type.22.wq_ref, f32[1,256]{1,0:T(1,128)} %bitcast.51, ...), custom_call_target="tpu_custom_call" | custom-call | tf_op jit(solution)/shard_map/gather/pallas_call | solution.py:787
  118.4 0.9 reduce.1
  119.5 0.1 reshape.127
  119.6 0.1 reshape.128
  119.7 0.2 slice_reduce_fusion
  120.0 0.3 convolution_multiply_fusion
  120.4 0.7 broadcast_in_dim.26.pattern_ref
  121.7 11.4 %project.1 = (bf16[3072,1024]{1,0:T(8,128)(2,1)S(1)}, bf16[3,256,3072]{2,1,0:T(8,128)(2,1)S(1)}) custom-call(bf16[3072,1024]{1,0:T(8,128)(2,1)} %bitcast.59, f32[2,1024]{1,0:T(2,128)S(1)} %pad_maximum_fusion.1.norm_ref, bf16[3,1024,256]{2,1,0:T(8,128)(2,1)S(1)} %copy-done.4), custom_call_target="tpu_custom_call" | custom-call | tf_op jit(solution)/shard_map/project/pallas_call | solution.py:50
  133.1 2.2 copy-done
  135.3 2.6 copy-done.19
  138.1 0.6 pad_maximum_fusion.2.norm_ref
  138.8 0.5 broadcast_select_fusion
  139.3 78.4 %attend.1 = (bf16[4,64,3072]{2,1,0:T(8,128)(2,1)}, bf16[4,4,64,768]{3,2,1,0:T(8,128)(2,1)}, f32[4,1,3072]{2,1,0:T(1,128)}) custom-call(s32[1]{0:T(128)} %bitcast.72, f32[4,1,3584]{2,1,0:T(1,128)} %broadcast_in_dim.26.pattern_ref, bf16[768,3072]{1,0:T(8,128)(2,1)} %bitcast.45, bf16[768,3072]{1,0:T(8,128)(2,1)} %bitcast.46, bf16[768,3072]{1,0:T(8,128)(2,1)} %bitcast.47), custom_call_target="tpu_custom_call" | custom-call | tf_op jit(solution)/shard_map/attend/pallas_call | solution.py:196
  217.6 5.4 all-gather.2.cloned.1.call-done.proj_ref.up_ref.down_ref
  223.0 86.0 %feed_forward.1 = (bf16[768,1024]{1,0:T(8,128)(2,1)}, f32[768,1024]{1,0:T(8,128)}, bf16[1024,768]{1,0:T(8,128)(2,1)}, bf16[2,128,9216]{2,1,0:T(8,128)(2,1)}, f32[2,1024]{1,0:T(2,128)}) custom-call(bf16[768,1024]{1,0:T(8,128)(2,1)} %x_ref.3, bf16[768,1024]{1,0:T(8,128)(2,1)} %c_ref.1, bf16[4,256,768]{2,1,0:T(8,128)(2,1)} %bitcast.63, ...), custom_call_target="tpu_custom_call" | custom-call | tf_op jit(solution)/shard_map/feed_forward/pallas_call | solution.py:1573
  309.1 97.2 %attend_back.1 = (bf16[3,4,64,3072]{3,2,1,0:T(8,128)(2,1)}, bf16[4,128,2304]{2,1,0:T(8,128)(2,1)}, f32[4,1,3584]{2,1,0:T(1,128)}) custom-call(s32[1]{0:T(128)} %bitcast.73, f32[4,1,3584]{2,1,0:T(1,128)} %broadcast_in_dim.26.pattern_ref, bf16[768,3072]{1,0:T(8,128)(2,1)} %bitcast.48, bf16[768,3072]{1,0:T(8,128)(2,1)} %bitcast.49, bf16[768,3072]{1,0:T(8,128)(2,1)} %bitcast.50, ...), custom_call_target="tpu_custom_call" | custom-call | tf_op jit(solution)/shard_map/attend_back/pallas_call | solution.py:383
  406.3 3.2 convert_reduce_fusion
  409.5 0.5 copy-done.22
  410.0 7.1 %bitcast_convert_fusion.first_ref = bf16[3072,1024]{1,0:T(8,128)(2,1)} fusion(bf16[3,256,3072]{2,1,0:T(8,128)(2,1)S(1)} %bitcast.60, bf16[3,1024,256]{2,1,0:T(8,128)(2,1)S(1)} %copy-done.4), kind=kOutput, calls=%fused_computation | convolution fusion | flops 4834983936 | bytes 12582912 | tf_op jit(solution)/shard_map/dot_general | solution.py:1707
  417.1 7.3 %bitcast_convert_fusion.1 = (bf16[3,1024,256]{2,1,0:T(8,128)(2,1)}, f32[3,256,1024]{1,2,0:T(8,128)}) fusion(bf16[3,256,3072]{2,1,0:T(8,128)(2,1)S(1)} %bitcast.61, bf16[3072,1024]{1,0:T(8,128)(2,1)S(1)} %bitcast.58), kind=kOutput, calls=%fused_computation.9 | convolution fusion | flops 4832624640 | bytes 15728640 | tf_op jit(solution)/shard_map/td,cet->cde/dot_general | solution.py:1710
  424.5 2.7 fusion.2
  427.2 0.1 reduce_sum.32
  427.3 0.1 reduce_sum.35
  427.6 0.1 reshape.133
  427.8 0.1 reshape.134
  427.9 0.3 fusion.4
  428.2 0.4 dynamic_update_slice.3
  428.5 0.7 maximum_maximum_fusion.small_ref
  429.4 67.5 %sums.1 = (bf16[2,768,1024]{2,1,0:T(8,128)(2,1)}, bf16[4,768,512]{2,1,0:T(8,128)(2,1)}, f32[3,128,256]{2,1,0:T(8,128)}, f32[128,2304]{1,0:T(8,128)}, f32[32,256]{1,0:T(8,128)}, /*index=5*/f32[1,128]{1,0:T(1,128)}) custom-call(bf16[3072,1024]{1,0:T(8,128)(2,1)} %bitcast_convert_fusion.first_ref, bf16[3,1024,256]{2,1,0:T(8,128)(2,1)} %get-tuple-element.141.grad_qkv_ref, ...), custom_call_target="tpu_custom_call" | custom-call | tf_op jit(solution)/shard_map/sums/pallas_call | solution.py:1138
  497.0 1.0 copy-done.11
  498.0 0.8 copy-done.14
  498.7 0.7 copy-done.16
  499.4 4.3 moments.1
  503.7 0.5 copy-done.20
  504.2 10.5 %reduce_row.1.update_ref = f32[1,128]{1,0:T(1,128)} custom-call(f32[1,128]{1,0:T(1,128)} %copy-done.20), custom_call_target="tpu_custom_call" | custom-call | tf_op jit(solution)/shard_map/reduce_row/pallas_call | solution.py:1182
  514.7 43.8 %finish_rows.1 = bf16[768,1024]{1,0:T(8,128)(2,1)} custom-call(bf16[4,768,512]{2,1,0:T(8,128)(2,1)} %get-tuple-element.100.added_ref, bf16[2,768,1024]{2,1,0:T(8,128)(2,1)} %get-tuple-element.101.early_ref, bf16[768,1024]{1,0:T(8,128)(2,1)} %x_ref.3, f32[768,1024]{1,0:T(8,128)} %get-tuple-element.102.middle_ref, f32[1,1024]{1,0:T(1,128)} %copy-done.25), custom_call_target="tpu_custom_call" | custom-call | tf_op jit(solution)/shard_map/finish_rows/pallas_call | solution.py:1107
  558.6 1.4 weights.1
  560.0 0.3 copy-done.23
  560.3 1.1 copy.76
  561.5 1.1 copy.77
  (97 shorter events, 1.7 us)
Async XLA Ops:
  7.2 215.8 %all-gather.2.cloned.1.call-start = ((), (), s32[]{:S(2)}) async-start(), calls=%async_computation | async-start | bytes 21233664 | tf_op jit(solution)/shard_map/all_gather | solution.py:1665
  12.0 106.3 %copy-start.29 = (s32[1,2]{1,0:T(1,128)S(1)}, s32[1,2]{1,0:T(1,128)}, u32[]{:S(2)}) copy-start(s32[1,2]{1,0:T(1,128)} %param.27) | copy-start | bytes 28
  15.0 105.0 %copy-start.30 = (s32[3072]{0:T(1024)S(1)}, s32[3072]{0:T(1024)}, u32[]{:S(2)}) copy-start(s32[3072]{0:T(1024)} %param.28) | copy-start | bytes 36868
  15.0 106.2 %copy-start.31 = (f32[2,32]{1,0:T(2,128)S(1)}, f32[2,32]{1,0:T(2,128)}, u32[]{:S(2)}) copy-start(f32[2,32]{1,0:T(2,128)} %param.41) | copy-start | bytes 772
  15.0 106.3 %copy-start.32 = (f32[2,32]{1,0:T(2,128)S(1)}, f32[2,32]{1,0:T(2,128)}, u32[]{:S(2)}) copy-start(f32[2,32]{1,0:T(2,128)} %param.42) | copy-start | bytes 772
  15.0 106.3 %copy-start.33 = (f32[2,32]{1,0:T(2,128)S(1)}, f32[2,32]{1,0:T(2,128)}, u32[]{:S(2)}) copy-start(f32[2,32]{1,0:T(2,128)} %param.48) | copy-start | bytes 772
  15.1 106.4 %copy-start.34 = (f32[2,32]{1,0:T(2,128)S(1)}, f32[2,32]{1,0:T(2,128)}, u32[]{:S(2)}) copy-start(f32[2,32]{1,0:T(2,128)} %param.49) | copy-start | bytes 772
  118.3 3.3 copy-start.4
  118.4 20.4 %collective-permute-start = (s32[1,2]{1,0:T(1,128)S(1)}, s32[1,2]{1,0:T(1,128)S(1)}, u32[]{:S(2)}, u32[]{:S(2)}) collective-permute-start(s32[1,2]{1,0:T(1,128)S(1)} %copy-done.29), channel_id=1, source_target_pairs={{0,4},{4,0},{1,5},{5,1},{2,6},{6,2},{3,7},{7,3},{8,12},{12,8},{9,1... | collective-permute-start | bytes 32 | tf_op jit(solution)/shard_map/ppermute | solution.py:1674
  120.0 13.2 %copy-start.25 = (f32[1,1024]{1,0:T(1,128)}, f32[1,1024]{1,0:T(1,128)S(1)}, u32[]{:S(2)}) copy-start(f32[1,1024]{1,0:T(1,128)S(1)} %slice.52.gain_ref) | copy-start | bytes 12292
  121.7 16.3 %copy-start.27 = (f32[16]{0:T(128)S(1)}, f32[16]{0:T(128)}, u32[]{:S(2)}) copy-start(f32[16]{0:T(128)} %param.40) | copy-start | bytes 196
  121.7 16.4 %copy-start.28 = (f32[16]{0:T(128)S(1)}, f32[16]{0:T(128)}, u32[]{:S(2)}) copy-start(f32[16]{0:T(128)} %param.47) | copy-start | bytes 196
  133.1 2.2 copy-start
  135.3 2.7 copy-start.19
  406.3 3.8 copy-start.22
  406.3 10.8 %slice-start = ((s8[6291456]{0:T(1024)(128)(4,1)}), s8[4194304]{0:T(1024)(128)(4,1)S(1)}, s32[]{:S(2)}) async-start(s8[6291456]{0:T(1024)(128)(4,1)} %bitcast.57), calls=%async_computation.1 | async-start | bytes 8388608
  410.0 7.1 %slice-start.1 = ((s8[6291456]{0:T(1024)(128)(4,1)}), s8[2097152]{0:T(1024)(128)(4,1)S(1)}, s32[]{:S(2)}) async-start(s8[6291456]{0:T(1024)(128)(4,1)} %bitcast.57), calls=%async_computation.2 | async-start | bytes 4194304
  424.4 3.0 copy-start.26
  424.4 3.5 copy-start.24
  429.2 67.6 %copy-start.1 = (f32[1024,128]{1,0:T(8,128)S(1)}, f32[1024,128]{1,0:T(8,128)}, u32[]{:S(2)}) copy-start(f32[1024,128]{1,0:T(8,128)} %wd.3) | copy-start | bytes 1572868
  429.2 67.6 %copy-start.2 = (f32[128,1024]{1,0:T(8,128)S(1)}, f32[128,1024]{1,0:T(8,128)}, u32[]{:S(2)}) copy-start(f32[128,1024]{1,0:T(8,128)} %wu.3) | copy-start | bytes 1572868
  429.2 67.6 %copy-start.3 = (f32[3,128,256]{2,1,0:T(8,128)S(1)}, f32[3,128,256]{2,1,0:T(8,128)}, u32[]{:S(2)}) copy-start(f32[3,128,256]{2,1,0:T(8,128)} %wq.3) | copy-start | bytes 1179652
  429.3 67.7 %copy-start.5 = (f32[256,128]{1,0:T(8,128)S(1)}, f32[256,128]{1,0:T(8,128)}, u32[]{:S(2)}) copy-start(f32[256,128]{1,0:T(8,128)} %wp.3) | copy-start | bytes 393220
  429.3 67.7 %copy-start.6 = (f32[128,1024]{1,0:T(8,128)S(1)}, f32[128,1024]{1,0:T(8,128)}, u32[]{:S(2)}) copy-start(f32[128,1024]{1,0:T(8,128)} %mu.1) | copy-start | bytes 1572868
  429.3 67.7 %copy-start.7 = (f32[1024,128]{1,0:T(8,128)S(1)}, f32[1024,128]{1,0:T(8,128)}, u32[]{:S(2)}) copy-start(f32[1024,128]{1,0:T(8,128)} %md.1) | copy-start | bytes 1572868
  429.3 67.7 %copy-start.8 = (f32[128,1024]{1,0:T(8,128)S(1)}, f32[128,1024]{1,0:T(8,128)}, u32[]{:S(2)}) copy-start(f32[128,1024]{1,0:T(8,128)} %su.1) | copy-start | bytes 1572868
  429.3 67.7 %copy-start.9 = (f32[3,128,256]{2,1,0:T(8,128)S(1)}, f32[3,128,256]{2,1,0:T(8,128)}, u32[]{:S(2)}) copy-start(f32[3,128,256]{2,1,0:T(8,128)} %mq.1) | copy-start | bytes 1179652
  429.3 67.6 %copy-start.10 = (f32[3,128,256]{2,1,0:T(8,128)S(1)}, f32[3,128,256]{2,1,0:T(8,128)}, u32[]{:S(2)}) copy-start(f32[3,128,256]{2,1,0:T(8,128)} %sq.1) | copy-start | bytes 1179652
  429.3 67.6 %copy-start.12 = (f32[256,128]{1,0:T(8,128)S(1)}, f32[256,128]{1,0:T(8,128)}, u32[]{:S(2)}) copy-start(f32[256,128]{1,0:T(8,128)} %mp.1) | copy-start | bytes 393220
  429.3 67.6 %copy-start.13 = (f32[256,128]{1,0:T(8,128)S(1)}, f32[256,128]{1,0:T(8,128)}, u32[]{:S(2)}) copy-start(f32[256,128]{1,0:T(8,128)} %sp.1) | copy-start | bytes 393220
  429.3 67.6 %copy-start.15 = (f32[256]{0:T(256)S(1)}, f32[256]{0:T(256)}, u32[]{:S(2)}) copy-start(f32[256]{0:T(256)} %select_maximum_fusion.4) | copy-start | bytes 3076
  497.0 1.0 copy-start.11
  498.0 0.8 copy-start.14
  498.7 0.7 copy-start.16
  503.7 0.5 copy-start.20
  514.7 43.9 %copy-start.17 = (f32[1,128]{1,0:T(1,128)S(1)}, f32[1,128]{1,0:T(1,128)}, u32[]{:S(2)}) copy-start(f32[1,128]{1,0:T(1,128)} %get-tuple-element.95.totals_ref) | copy-start | bytes 1540
  514.7 43.9 %copy-start.18 = (f32[1,128]{1,0:T(1,128)S(1)}, f32[1,128]{1,0:T(1,128)}, u32[]{:S(2)}) copy-start(f32[1,128]{1,0:T(1,128)} %reduce_row.1.update_ref) | copy-start | bytes 1540
  558.6 1.8 copy-start.23
  558.6 2.9 copy-start.21
Sparse Core Ops, SparseCore 0:
  118.5 104.5 all-gather.1

commit v4 on v3

--- a/solution.py
+++ b/solution.py
@@ -64,9 +64,64 @@
             jax.ShapeDtypeStruct((3, cols, tok), BF),
         ],
         scratch_shapes=[pltpu.VMEM((3, cols, width), BF)],
-        compiler_params=pltpu.CompilerParams(vmem_limit_bytes=40 * 2**20),
+        compiler_params=pltpu.CompilerParams(vmem_limit_bytes=62 * 2**20),
         name="project",
     )(rows, norm, weights)
+
+
+def project_back_kernel(a_ref, grads_ref, w_ref, first_ref, grad_ref, sums_ref, low_ref, total, turned):
+    step = pl.program_id(0)
+
+    @pl.when(step == 0)
+    def _():
+        total[...] = jnp.zeros_like(total)
+        sums_ref[...] = jnp.zeros_like(sums_ref)
+        for c in range(3):
+            turned[c] = w_ref[c].T
+
+    first = jnp.zeros(first_ref.shape, F32)
+    for c in range(3):
+        grads = grads_ref[c]
+        first = first + dot(grads.T, turned[c], 1, 0)
+        total[c] += dot(grads, a_ref[...], 1, 0)
+        sums_ref[c] += jnp.sum(grads.astype(F32), axis=1, keepdims=True)
+    first_ref[...] = first.astype(BF)
+
+    @pl.when(step == pl.num_programs(0) - 1)
+    def _():
+        for c in range(3):
+            grad = total[c].T
+            grad_ref[c] = grad.astype(BF)
+            low_ref[:, c : c + 1] = jnp.sum(grad * w_ref[c].astype(F32), axis=1, keepdims=True)
+
+
+def project_back(a_first, grads, weights):
+    tok, width = a_first.shape
+    cols = grads.shape[1]
+    return pl.pallas_call(
+        project_back_kernel,
+        grid=(tok // BLK,),
+        in_specs=[
+            pl.BlockSpec((BLK, width), lambda s: (s, 0)),
+            pl.BlockSpec((3, cols, BLK), lambda s: (0, 0, s)),
+            pl.BlockSpec((3, width, cols), lambda s: (0, 0, 0)),
+        ],
+        out_specs=[
+            pl.BlockSpec((BLK, width), lambda s: (s, 0)),
+            pl.BlockSpec((3, width, cols), lambda s: (0, 0, 0)),
+            pl.BlockSpec((3, cols, 1), lambda s: (0, 0, 0)),
+            pl.BlockSpec((width, 3), lambda s: (0, 0)),
+        ],
+        out_shape=[
+            jax.ShapeDtypeStruct((tok, width), BF),
+            jax.ShapeDtypeStruct((3, width, cols), BF),
+            jax.ShapeDtypeStruct((3, cols, 1), F32),
+            jax.ShapeDtypeStruct((width, 3), F32),
+        ],
+        scratch_shapes=[pltpu.VMEM((3, cols, width), F32), pltpu.VMEM((3, cols, width), BF)],
+        compiler_params=pltpu.CompilerParams(vmem_limit_bytes=62 * 2**20),
+        name="project_back",
+    )(a_first, grads, weights)
 
 
 def make_slab(pattern, slab):
@@ -146,13 +201,19 @@
     put_queries(q_ref[...], split, None, tok, qx)
     put_keys(k_ref, split, tok, kx)
 
-    def step(i, j, top, total, out):
-        scores = dot(kx[block_at(j), :], qx[:, block_at(i)], 1, 0) + slab[:, block_at(i - j)]
-        new_top = jnp.maximum(top, jnp.max(scores, axis=0, keepdims=True))
-        weights = jnp.exp2(scores - new_top)
+    def steps(i, blocks, top, total, out):
+        scores = [
+            dot(kx[block_at(j), :], qx[:, block_at(i)], 1, 0) + slab[:, block_at(i - j)] for j in blocks
+        ]
+        new_top = top
+        for score in scores:
+            new_top = jnp.maximum(new_top, jnp.max(score, axis=0, keepdims=True))
         scale = jnp.exp2(top - new_top)
-        total = total * scale + jnp.sum(weights, axis=0, keepdims=True)
-        out = out * scale + dot(v_ref[:, block_at(j)], weights.astype(BF), 1, 0)
+        total, out = total * scale, out * scale
+        for j, score in zip(blocks, scores):
+            weights = jnp.exp2(score - new_top)
+            total = total + jnp.sum(weights, axis=0, keepdims=True)
+            out = out + dot(v_ref[:, block_at(j)], weights.astype(BF), 1, 0)
         return new_top, total, out
 
     def row(i, carry):
@@ -161,7 +222,10 @@
             jnp.zeros((1, BLK), F32),
             jnp.zeros((DH, BLK), F32),
         )
-        top, total, out = lax.fori_loop(0, i + 1, lambda t, c: step(i, i - t, *c), start)
+        pairs = lax.fori_loop(
+            0, (i + 1) // 2, lambda t, c: steps(i, (i - 2 * t, i - 2 * t - 1), *c), start
+        )
+        top, total, out = lax.fori_loop(0, (i + 1) % 2, lambda t, c: steps(i, (0,), *c), pairs)
         outs[head, :, block_at(i)] = (out / total).astype(BF)
         lse_ref[0, :, block_at(i)] = top + jnp.log2(total)
         return carry
@@ -253,10 +317,11 @@
     def column_copies():
         at = (lax.div(xy, side), lax.rem(xy, side))
         for step in range(1, side):
-            for n, (start, size, axis) in enumerate(segments):
+            for n, (distance, start, count, axis) in enumerate(segments):
                 there = lax.rem(at[axis] + step, side)
                 column = there * side + at[1] if axis == 0 else at[0] * side + there
-                here = pl.ds(start, size)
+                part = lax.rem(trade.row + distance, trade.parts)
+                here = pl.ds(pl.multiple_of(part * wide_parts_ref.shape[2] + start, 128), count)
                 yield send(
                     wide_ref.at[step, :, here], wide_in.at[step - 1, :, here],
                     w_send.at[step - 1, n], w_recv.at[step - 1, n], (column, core, zh, zl),
@@ -352,8 +417,12 @@
 
     def query_row(i, carry):
         total = lax.fori_loop(
-            0, i + 1, lambda t, c: c + tile(i, i - t), jnp.zeros((DH, BLK), F32)
+            0,
+            (i + 1) // 2,
+            lambda t, c: c + tile(i, i - 2 * t) + tile(i, i - 2 * t - 1),
+            jnp.zeros((DH, BLK), F32),
         )
+        total = lax.fori_loop(0, (i + 1) % 2, lambda t, c: c + tile(i, 0), total)
         grads_ref[0, 0, :, block_at(i)] = (total * DH**-0.5).astype(BF)
         return carry
 
@@ -583,7 +652,10 @@
 
     own_wq = pltpu.make_async_copy(wq_ref, depth_of(dp, 1), local_sems.at[1])
     own_small = pltpu.make_async_copy(small_ref, all_small_ref.at[dp, z], local_sems.at[2])
-    own_wide = pltpu.make_async_copy(wide_ref, all_wide_ref.at[z], local_sems.at[3])
+
+    def wide_at(shard, device_z):
+        return all_wide_ref.at[lax.rem(shard + parts - device_z, parts) - 1]
+
     own_small.start()
     for n in range(2):
 
@@ -649,13 +721,12 @@
             pass_on(z, chunk, mine)
             share(z, chunk, mine)
 
-    own_wide.start()
     for n, step in enumerate((1, -1)):
 
         @pl.when((z + step >= 0) & (z + step < parts))
         def _():
             send(
-                wide_ref, all_wide_ref.at[z], w_send.at[n, z], w_recv.at[z], beside(step)
+                wide_ref, wide_at(z, z + step), w_send.at[n, z], w_recv.at[z], beside(step)
             ).start()
 
     @pl.when(outside)
@@ -664,29 +735,30 @@
             got(z, chunk)
             pass_on(z, chunk, chunk_of(rows_ref.at[z], core, chunk))
 
-    own_small.wait()
-    for step in range(1, parts):
-        there = lax.rem(z + step, parts)
-        send(small_ref, all_small_ref.at[dp, there], z_send.at[step], z_recv.at[there], sibling).wait_recv()
-    for c in range(2):
-
-        @pl.when(is_same(wq_source(c), me))
-        def _():
-            own_wq.wait()
-
-        @pl.when(jnp.logical_not(is_same(wq_source(c), me)))
-        def _():
-            here = depth_of(xy * 2 + c, 1)
-            send(here, here, q_send.at[0], q_recv.at[c], wq_source(c)).wait_recv()
-
     def arrays_at(column):
         return depth_of(column * 2, 2), all_small_ref.at[column * 2 + core]
 
-    for step, there, device in plane_peers(shape, me):
-        for n, ref in enumerate(arrays_at(xy)):
-            send(ref, ref, p_send.at[n, step], p_recv.at[n, xy], device).start()
-    ref = all_small_ref.at[dp]
-    send(ref, ref, s_send.at[xy], s_recv.at[xy], sibling).start()
+    def spread():
+        own_small.wait()
+        for step in range(1, parts):
+            there = lax.rem(z + step, parts)
+            send(small_ref, all_small_ref.at[dp, there], z_send.at[step], z_recv.at[there], sibling).wait_recv()
+        for c in range(2):
+
+            @pl.when(is_same(wq_source(c), me))
+            def _():
+                own_wq.wait()
+
+            @pl.when(jnp.logical_not(is_same(wq_source(c), me)))
+            def _():
+                here = depth_of(xy * 2 + c, 1)
+                send(here, here, q_send.at[0], q_recv.at[c], wq_source(c)).wait_recv()
+
+        for step, there, device in plane_peers(shape, me):
+            for n, ref in enumerate(arrays_at(xy)):
+                send(ref, ref, p_send.at[n, step], p_recv.at[n, xy], device).start()
+        ref = all_small_ref.at[dp]
+        send(ref, ref, s_send.at[xy], s_recv.at[xy], sibling).start()
 
     for distance in range(1, parts):
         for chunk in range(CHUNKS):
@@ -699,18 +771,22 @@
                     pass_on(shard, chunk, mine)
                     share(shard, chunk, mine)
 
+        if distance == 1:
+            spread()
         for n, step in enumerate((1, -1)):
             shard = z - step * distance
 
             @pl.when((shard >= 0) & (shard < parts))
             def _():
-                piece = all_wide_ref.at[shard]
+                piece = wide_at(shard, z)
                 send(piece, piece, w_send.at[n, shard], w_recv.at[shard], sibling).wait_recv()
 
             @pl.when((shard >= 0) & (shard < parts) & (z + step >= 0) & (z + step < parts))
             def _():
-                piece = all_wide_ref.at[shard]
-                send(piece, piece, w_send.at[n, shard], w_recv.at[shard], beside(step)).start()
+                send(
+                    wide_at(shard, z), wide_at(shard, z + step), w_send.at[n, shard], w_recv.at[shard],
+                    beside(step),
+                ).start()
 
     for step in range(1, columns):
         there = lax.rem(xy + columns - step, columns)
@@ -735,15 +811,15 @@
         def _():
             send(wq_ref, depth_of(dp, 1), q_send.at[n], q_recv.at[core], sibling).wait_send()
 
-    own_wide.wait()
     for n, step in enumerate((1, -1)):
         for distance in range(parts):
             shard = z - step * distance
 
             @pl.when((shard >= 0) & (shard < parts) & (z + step >= 0) & (z + step < parts))
             def _():
-                piece = all_wide_ref.at[shard]
-                send(piece, piece, w_send.at[n, shard], w_recv.at[shard], beside(step)).wait_send()
+                send(
+                    wide_ref, wide_ref, w_send.at[n, shard], w_recv.at[shard], beside(step)
+                ).wait_send()
 
     for shard in range(parts):
         for chunk in range(CHUNKS):
@@ -790,12 +866,12 @@
             jax.ShapeDtypeStruct((parts, *tokens.shape), tokens.dtype),
             jax.ShapeDtypeStruct((3, 2 * columns * wq.shape[1], wq.shape[2]), wq.dtype),
             jax.ShapeDtypeStruct((2 * columns, parts, *small.shape), small.dtype),
-            jax.ShapeDtypeStruct((parts, *wide.shape), wide.dtype),
+            jax.ShapeDtypeStruct((parts - 1, *wide.shape), wide.dtype),
         ],
         in_specs=[anywhere] * 4,
         out_specs=[anywhere] * 4,
         scratch_shapes=[
-            dma((4,)), dma((2, CHUNKS)), dma((2, parts, CHUNKS)), dma((parts, CHUNKS)),
+            dma((3,)), dma((2, CHUNKS)), dma((2, parts, CHUNKS)), dma((parts, CHUNKS)),
             dma((parts, CHUNKS)), dma((parts, CHUNKS)),
             dma((parts,)), dma((parts,)), dma((2, columns)), dma((2, columns)), dma((columns,)),
             dma((columns,)), dma((2, parts)), dma((parts,)), dma((2,)), dma((2,)),
@@ -1407,7 +1483,7 @@
 
 
 def feed_kernel(
-    shape, ff_local, x_ref, c_ref, attn_ref, norm_ref, proj_ref, up_ref, down_ref,
+    shape, ff_local, x_ref, c_ref, attn_ref, norm_ref, own_proj, other_proj, own_up, own_down, other_up, other_down,
     block_ref, middle_ref, given_ref, wide_ref, sums_ref,
     middle, total, second, a_second, a_turned, c_turned, own, other, taken, first_in,
     out_sems, keep_sems, proj_sems, *sems,
@@ -1422,14 +1498,20 @@
     slot = lax.rem(step, 2)
     adder = Adder(side, taken, first_in, sems)
     halves = own.shape[2:5]
+    _, _, zh, zl = place()
+    z = zh * shape["zl"] + zl
+
+    def part_at(distance):
+        return lax.rem(z + distance, parts)
+
+    def proj_at(distance):
+        return own_proj[...] if distance == 0 else other_proj[distance - 1]
 
     def keep(index, axis):
         for step in range(side):
             for which in range(2):
-                start = index // per * wide + which * ff_local + index % per * chunk
-                if not isinstance(index, int):
-                    start = lax.div(index, per) * wide + which * ff_local + lax.rem(index, per) * chunk
-                    start = pl.multiple_of(start, 128)
+                start = part_at(lax.div(index, per)) * wide + which * ff_local + lax.rem(index, per) * chunk
+                start = pl.multiple_of(start, 128)
                 yield pltpu.make_async_copy(
                     adder.owned(index, axis, step).at[which], wide_ref.at[step, :, pl.ds(start, chunk)],
                     keep_sems.at[index, step, which],
@@ -1456,8 +1538,8 @@
             pl.semaphore_signal(barrier, inc=1, device_id=peer, device_id_type=MESH)
         core = lax.axis_index("core")
         mixed = x_ref[...].astype(F32)
-        for part in range(parts):
-            mixed = mixed + dot(attn_ref[part].T, proj_ref[part], 1, 1)
+        for distance in range(parts):
+            mixed = mixed + dot(attn_ref[part_at(distance)].T, proj_at(distance), 1, 1)
         middle[...] = mixed
         value, _ = normed_of(mixed)
         a_second[...] = (value * norm_ref[0:1, :] + norm_ref[1:2, :]).astype(BF)
@@ -1471,7 +1553,9 @@
     def _():
         adder.swap(other.at[slot], step - 2).wait_send()
 
-    up, down = up_ref[0], down_ref[0]
+    mine = step < per
+    up = jnp.where(mine, own_up[...], other_up[0])
+    down = jnp.where(mine, own_down[...], other_down[0])
     pre = dot(a_second[...], up, 1, 0)
     grad_hidden = dot(c_ref[...], down, 1, 0)
     normal = 0.5 * (1.0 + lax.erf(pre * 2.0**-0.5))
@@ -1525,9 +1609,9 @@
             put(free, which, jnp.concatenate(grads, axis=1))
         adder.swap(other.at[free], steps).start()
         adder.add_first(last - 1, keep)
-        for part in range(parts):
-            rows = pl.ds(part * heads_cols, heads_cols)
-            c_turned[rows, :] = dot(low, proj_ref[part], 1, 0).T.astype(BF)
+        for distance in range(parts):
+            rows = pl.ds(pl.multiple_of(part_at(distance) * heads_cols, heads_cols), heads_cols)
+            c_turned[rows, :] = dot(low, proj_at(distance), 1, 0).T.astype(BF)
         out_given = pltpu.make_async_copy(c_turned, given_ref, out_sems.at[2])
         out_given.start()
         adder.add_core(own.at[free], other.at[free], steps)
@@ -1544,19 +1628,18 @@
 def column_segments(parts, ff_local, heads_cols):
     chunk = min(512, ff_local)
     per = ff_local // chunk
-    wide = 2 * ff_local + heads_cols
     segments = [
-        (part * wide + which * ff_local + n * chunk, chunk, 1 - (part * per + n) % 2)
-        for part in range(parts)
+        (distance, which * ff_local + n * chunk, chunk, 1 - (distance * per + n) % 2)
+        for distance in range(parts)
         for which in range(2)
         for n in range(per)
     ]
     return segments + [
-        (part * wide + 2 * ff_local, heads_cols, 1 - parts * per % 2) for part in range(parts)
+        (distance, 2 * ff_local, heads_cols, 1 - parts * per % 2) for distance in range(parts)
     ]
 
 
-def feed_forward(shape, tokens, cotangent, attn_rows, norm, shared, ff_local):
+def feed_forward(shape, tokens, cotangent, attn_rows, norm, shared_own, shared_others, ff_local):
     rows, width = tokens.shape
     parts, heads_cols = attn_rows.shape[:2]
     chunk = min(512, ff_local)
@@ -1578,9 +1661,19 @@
             once((rows, width), 0, 0),
             once((parts, heads_cols, rows), 0, 0, 0),
             once((2, width), 0, 0),
-            once((parts, width, heads_cols), 0, 0, 2 * ff_local // heads_cols),
-            pl.BlockSpec((1, width, chunk), lambda s: (s // per, 0, s % per)),
-            pl.BlockSpec((1, width, chunk), lambda s: (s // per, 0, per + s % per)),
+            once((width, heads_cols), 0, 2 * ff_local // heads_cols),
+            once((parts - 1, width, heads_cols), 0, 0, 2 * ff_local // heads_cols),
+            *[
+                pl.BlockSpec((width, chunk), lambda s, at=at: (0, at + jnp.minimum(s, per - 1)))
+                for at in (0, per)
+            ],
+            *[
+                pl.BlockSpec(
+                    (1, width, chunk),
+                    lambda s, at=at: (jnp.maximum(s - per, 0) // per, 0, at + jnp.maximum(s - per, 0) % per),
+                )
+                for at in (0, per)
+            ],
         ],
         out_specs=[anywhere] * 4 + [pl.BlockSpec((2, width), lambda s: (0, 0))],
         out_shape=[
@@ -1613,7 +1706,7 @@
             vmem_limit_bytes=62 * 2**20, collective_id=5, has_side_effects=True
         ),
         name="feed_forward",
-    )(tokens, cotangent, attn_rows, norm, shared, shared, shared)
+    )(tokens, cotangent, attn_rows, norm, shared_own, shared_others, *[shared_own] * 2, *[shared_others] * 2)
 
 
 def norm_parts(values):
@@ -1651,6 +1744,7 @@
     ff_local, heads_cols = w_up.shape[1], w_proj.shape[0]
     local = jnp.concatenate([w_up, w_down.T, w_proj.T], axis=1).astype(BF)
 
+    shared_own = lax.all_gather(local, DP, axis=0, tiled=True)
     n_bias, n_gain = rel_bias.shape[0], ln_gain.shape[1]
     n_small = n_bias + 4 * n_gain
 
@@ -1662,7 +1756,7 @@
     group_rows, w_heads, small, wide = gather(
         shape, tokens, w_qkv.astype(BF), small_weights, local
     )
-    shared = lax.all_gather(wide, DP, axis=1, tiled=True)
+    shared_others = lax.all_gather(wide, DP, axis=1, tiled=True)
     small = small.reshape(devices, LANES)
 
     def columns_of(start):
@@ -1694,7 +1788,7 @@
     attn_rows = attn_rows.reshape(parts, heads * DH, rows)
     norm_two = jnp.stack([gains[1], shifts[1]])
     block_out, grad_middle, grad_attn, wide_grad, sums_two = feed_forward(
-        shape, tokens, cotangent, attn_rows, norm_two, shared, ff_local
+        shape, tokens, cotangent, attn_rows, norm_two, shared_own, shared_others, ff_local
     )
     gain_two, shift_two = sums_two[0], sums_two[1]
     given = grad_attn.reshape(parts, heads, DH, rows)
@@ -1704,17 +1798,9 @@
     )
     grad_heads = grad_heads.reshape(3, heads * DH, tok)
 
-    first = lax.dot_general(
-        grad_heads, w_heads, (((0, 1), (0, 2)), ((), ())), preferred_element_type=F32
-    ).astype(BF)
-    grad_qkv = jnp.einsum("td,cet->cde", a_first, grad_heads, preferred_element_type=F32)
-    head_sums = jnp.sum(grad_heads.astype(F32), axis=2)
-    wide_heads = w_heads.astype(F32)
-    shift_one = jnp.sum(wide_heads * head_sums[:, None, :], axis=(0, 2))
-    gain_one = (
-        jnp.sum(wide_heads * grad_qkv, axis=(0, 2)) - shifts[0] * shift_one
-    ) / gains[0]
-    grad_qkv = grad_qkv.astype(BF)
+    first, grad_qkv, head_sums, column_sums = project_back(a_first, grad_heads, w_heads)
+    shift_one = jnp.sum(w_heads.astype(F32) * head_sums.reshape(3, 1, heads * DH), axis=(0, 2))
+    gain_one = (jnp.sum(column_sums, axis=1) - shifts[0] * shift_one) / gains[0]
 
     bias_grad = lax.dot_general(
         one_hot, grad_pattern[:, 0, :tok], (((1,), (1,)), ((), ())),

time: 576 us -> 547 us (0.950)
  matrix products: 15 us -> 0.63 us
  other arithmetic: 13.9 us -> 7.93 us
  local copies, waits for them, and re-layouts: 17.6 us -> 11.7 us
    pallas_call x0 -> x1, Pallas kernels: none -> 16.9 us  [project_back(): pl.pallas_call(project_back_kernel, grid=(tok // BLK,), in_specs=[pl.Bloc...]
    dot_general x2 -> x0, matrix products: 14.4 us -> none  [the longest x1 7.27 us: per_device(): jnp.einsum('td,cet->cde', a_first, grad_heads, preferred_element_type=F32)]
    pallas_call x1, Pallas kernels: 78.4 us -> 70 us  [attend(): pl.pallas_call(functools.partial(attend_kernel, shape), grid=(heads,), in...]
    unnamed x78 -> x82, local copies, waits for them, and re-layouts: 13.2 us -> 8.5 us
  transfers between devices with their start and end apart: 2 -> 3, of which waited for: 1 -> 0; matrix products, arithmetic and copies ran while one was open for 1% -> 1% of each run, Pallas kernels for 16% -> 34%
where the time goes in v4:
time: 547 us; the launch traced here: 540 us
  Pallas kernels  505 us (92%)
  between operations  15.1 us (3%)
  local copies, waits for them, and re-layouts  11.7 us (2%)
  other arithmetic  7.93 us (1%)
    pallas_call x1, Pallas kernels, gather(): pl.pallas_call(functools.partial(gather_kernel, shape), out_shape=[jax.Sh...  102 us
    pallas_call x1, Pallas kernels, attend_back(): pl.pallas_call(functools.partial(attend_back_kernel, shape, segments), gr...  92.7 us
    pallas_call x1, Pallas kernels, feed_forward(): pl.pallas_call(functools.partial(feed_kernel, shape, ff_local), grid=(ste...  87.3 us
    pallas_call x1, Pallas kernels, attend(): pl.pallas_call(functools.partial(attend_kernel, shape), grid=(heads,), in...  70 us
    pallas_call x1, Pallas kernels, sums(): pl.pallas_call(functools.partial(sums_kernel, shape, n_bias, n_gain), out...  64.1 us
    pallas_call x1, Pallas kernels, finish_rows(): pl.pallas_call(functools.partial(rows_kernel, shape), out_shape=jax.Shape...  43.3 us
    pallas_call x1, Pallas kernels, project_back(): pl.pallas_call(project_back_kernel, grid=(tok // BLK,), in_specs=[pl.Bloc...  16.9 us
    pallas_call x1, Pallas kernels, project(): pl.pallas_call(project_kernel, grid=(tok // BLK,), in_specs=[pl.BlockSpec...  12.7 us
  transfers between devices with their start and end apart: 3, of which 0 were waited for; matrix products, arithmetic and copies ran while one was open for 1% of the time, Pallas kernels for 34%

profile of v4, /device:TPU:8, one launch (start us, length us, event | category | flops | bytes accessed | tf_op | source)
XLA Modules:
  0.0 540.4 jit_solution(15708550536486205432)
XLA Ops:
  7.3 1.2 copy.55
  8.5 1.1 convert.11
  9.7 0.1 copy.56
  9.8 0.9 pad_maximum_fusion.wide_ref
  10.7 0.1 reshape.122
  10.9 0.7 convert_element_type.12.wq_ref
  11.6 0.6 select_maximum_fusion.4
  12.2 102.4 %gather.1 = (bf16[4,768,1024]{2,1,0:T(8,128)(2,1)}, bf16[3,1024,256]{2,1,0:T(8,128)(2,1)}, f32[8,4,1,256]{3,2,1,0:T(1,128)}, bf16[3,128,2304]{2,1,0:T(8,128)(2,1)}) custom-call(bf16[768,1024]{1,0:T(8,128)(2,1)} %x_ref.3, bf16[3,128,256]{2,1,0:T(8,128)(2,1)} %convert_element_type.12.wq_ref, f32[1,256]{1,0:T(1,128)} %bitcast.32, ...), custom_call_target="tpu_custom_call" | custom-call | tf_op jit(solution)/shard_map/gather/pallas_call | solution.py:863
  114.8 0.6 copy-done.26
  115.4 0.1 reduce
  115.6 0.1 reshape.126
  115.7 0.1 reshape.127
  115.7 0.2 slice_reduce_fusion
  116.1 0.3 convolution_multiply_fusion
  116.5 0.7 broadcast_in_dim.25.pattern_ref
  117.3 0.1 reshape.134
  117.5 0.1 reshape.136
  117.7 0.6 pad_maximum_fusion.1.norm_ref
  118.3 12.7 %project.1 = (bf16[3072,1024]{1,0:T(8,128)(2,1)}, bf16[3,256,3072]{2,1,0:T(8,128)(2,1)}) custom-call(bf16[3072,1024]{1,0:T(8,128)(2,1)} %bitcast.44, f32[2,1024]{1,0:T(2,128)} %pad_maximum_fusion.1.norm_ref, bf16[3,1024,256]{2,1,0:T(8,128)(2,1)} %get-tuple-element.84.w_ref), custom_call_target="tpu_custom_call" | custom-call | tf_op jit(solution)/shard_map/project/pallas_call | solution.py:50
  131.2 0.6 pad_maximum_fusion.2.norm_ref
  131.8 0.5 broadcast_select_fusion
  132.3 70.0 %attend.1 = (bf16[4,64,3072]{2,1,0:T(8,128)(2,1)}, bf16[4,4,64,768]{3,2,1,0:T(8,128)(2,1)}, f32[4,1,3072]{2,1,0:T(1,128)}) custom-call(s32[1]{0:T(128)} %bitcast.56, f32[4,1,3584]{2,1,0:T(1,128)} %broadcast_in_dim.25.pattern_ref, bf16[768,3072]{1,0:T(8,128)(2,1)} %bitcast.38, bf16[768,3072]{1,0:T(8,128)(2,1)} %bitcast.39, bf16[768,3072]{1,0:T(8,128)(2,1)} %bitcast.40), custom_call_target="tpu_custom_call" | custom-call | tf_op jit(solution)/shard_map/attend/pallas_call | solution.py:260
  202.4 87.3 %feed_forward.1 = (bf16[768,1024]{1,0:T(8,128)(2,1)}, f32[768,1024]{1,0:T(8,128)}, bf16[1024,768]{1,0:T(8,128)(2,1)}, bf16[2,128,9216]{2,1,0:T(8,128)(2,1)}, f32[2,1024]{1,0:T(2,128)}) custom-call(bf16[768,1024]{1,0:T(8,128)(2,1)} %x_ref.3, bf16[768,1024]{1,0:T(8,128)(2,1)} %c_ref.1, bf16[4,256,768]{2,1,0:T(8,128)(2,1)} %bitcast.47, ...), custom_call_target="tpu_custom_call" | custom-call | tf_op jit(solution)/shard_map/feed_forward/pallas_call | solution.py:1656
  289.7 92.7 %attend_back.1 = (bf16[3,4,64,3072]{3,2,1,0:T(8,128)(2,1)}, bf16[4,128,2304]{2,1,0:T(8,128)(2,1)}, f32[4,1,3584]{2,1,0:T(1,128)}) custom-call(s32[1]{0:T(128)} %bitcast.57, f32[4,1,3584]{2,1,0:T(1,128)} %broadcast_in_dim.25.pattern_ref, bf16[768,3072]{1,0:T(8,128)(2,1)} %bitcast.41, bf16[768,3072]{1,0:T(8,128)(2,1)} %bitcast.42, bf16[768,3072]{1,0:T(8,128)(2,1)} %bitcast.43, ...), custom_call_target="tpu_custom_call" | custom-call | tf_op jit(solution)/shard_map/attend_back/pallas_call | solution.py:452
  382.4 16.9 %project_back.1 = (bf16[3072,1024]{1,0:T(8,128)(2,1)}, bf16[3,1024,256]{2,1,0:T(8,128)(2,1)}, f32[3,256,1]{2,1,0:T(8,128)}, f32[1024,3]{1,0:T(8,128)}) custom-call(bf16[3072,1024]{1,0:T(8,128)(2,1)} %get-tuple-element.89.a_ref, bf16[3,256,3072]{2,1,0:T(8,128)(2,1)} %bitcast.45, bf16[3,1024,256]{2,1,0:T(8,128)(2,1)} %get-tuple-element.84.w_ref), custom_call_target="tpu_custom_call" | custom-call | tf_op jit(solution)/shard_map/project_back/pallas_call | solution.py:101
  399.4 1.2 reduce.5
  400.6 0.4 multiply_reduce_fusion
  401.0 0.1 reduce_sum.25
  401.1 0.2 reduce_sum.22
  401.3 0.1 reduce_sum.23
  401.6 0.1 reshape.132
  401.8 0.1 reshape.133
  401.9 0.3 fusion
  402.2 0.6 dynamic_update_slice.3
  402.8 0.7 maximum_maximum_fusion.small_ref
  403.6 64.1 %sums.1 = (bf16[2,768,1024]{2,1,0:T(8,128)(2,1)}, bf16[4,768,512]{2,1,0:T(8,128)(2,1)}, f32[3,128,256]{2,1,0:T(8,128)}, f32[128,2304]{1,0:T(8,128)}, f32[32,256]{1,0:T(8,128)}, /*index=5*/f32[1,128]{1,0:T(1,128)}) custom-call(bf16[3072,1024]{1,0:T(8,128)(2,1)} %get-tuple-element.95.first_ref, bf16[3,1024,256]{2,1,0:T(8,128)(2,1)} %get-tuple-element.96.grad_qkv_ref, ...), custom_call_target="tpu_custom_call" | custom-call | tf_op jit(solution)/shard_map/sums/pallas_call | solution.py:1214
  467.9 1.0 copy-done.11
  468.8 0.8 copy-done.14
  469.6 0.7 copy-done.16
  470.3 4.3 moments.1
  474.6 0.5 copy-done.19
  475.1 9.7 %reduce_row.1.update_ref = f32[1,128]{1,0:T(1,128)} custom-call(f32[1,128]{1,0:T(1,128)} %copy-done.19), custom_call_target="tpu_custom_call" | custom-call | tf_op jit(solution)/shard_map/reduce_row/pallas_call | solution.py:1258
  484.9 43.3 %finish_rows.1 = bf16[768,1024]{1,0:T(8,128)(2,1)} custom-call(bf16[4,768,512]{2,1,0:T(8,128)(2,1)} %get-tuple-element.108.added_ref, bf16[2,768,1024]{2,1,0:T(8,128)(2,1)} %get-tuple-element.109.early_ref, bf16[768,1024]{1,0:T(8,128)(2,1)} %x_ref.3, f32[768,1024]{1,0:T(8,128)} %get-tuple-element.110.middle_ref, f32[1,1024]{1,0:T(1,128)} %copy-done.25), custom_call_target="tpu_custom_call" | custom-call | tf_op jit(solution)/shard_map/finish_rows/pallas_call | solution.py:1183
  528.2 1.4 weights.1
  529.6 0.4 copy-done.22
  530.0 1.1 copy.70
  531.1 0.8 copy-done.21
  532.0 1.1 copy.71
  (102 shorter events, 1.6 us)
Async XLA Ops:
  7.2 2.5 copy-start.4
  7.2 195.1 %all-gather.3.cloned.1.call-start = ((), (), s32[]{:S(2)}) async-start(), calls=%async_computation | async-start | bytes 5308416 | tf_op jit(solution)/shard_map/all_gather | solution.py:1747
  8.5 2.2 copy-start.33
  8.5 2.3 copy-start.34
  8.5 2.4 copy-start.2
  8.5 3.1 copy-start.28
  10.6 191.7 %all-gather.5.cloned.1.call-start = ((), (), s32[]{:S(2)}) async-start(), calls=%async_computation.1 | async-start | bytes 15925248 | tf_op jit(solution)/shard_map/all_gather | solution.py:1759
  12.2 102.5 %copy-start.31 = (s32[1,2]{1,0:T(1,128)S(1)}, s32[1,2]{1,0:T(1,128)}, u32[]{:S(2)}) copy-start(s32[1,2]{1,0:T(1,128)} %param.27) | copy-start | bytes 28
  114.6 0.8 copy-start.26
  114.6 1.5 copy-start.32
  114.6 2.7 copy-start.35
  114.6 2.7 copy-start.36
  114.7 2.8 copy-start.37
  114.7 2.9 copy-start.38
  114.7 17.1 %collective-permute-start = (s32[1,2]{1,0:T(1,128)S(1)}, s32[1,2]{1,0:T(1,128)S(1)}, u32[]{:S(2)}, u32[]{:S(2)}) collective-permute-start(s32[1,2]{1,0:T(1,128)S(1)} %copy-done.31), channel_id=1, source_target_pairs={{0,4},{4,0},{1,5},{5,1},{2,6},{6,2},{3,7},{7,3},{8,12},{12,8},{9,1... | collective-permute-start | bytes 32 | tf_op jit(solution)/shard_map/ppermute | solution.py:1768
  116.0 15.0 %copy-start.25 = (f32[1,1024]{1,0:T(1,128)}, f32[1,1024]{1,0:T(1,128)S(1)}, u32[]{:S(2)}) copy-start(f32[1,1024]{1,0:T(1,128)S(1)} %slice.52.gain_ref) | copy-start | bytes 12292
  118.3 12.7 %copy-start.29 = (f32[16]{0:T(128)S(1)}, f32[16]{0:T(128)}, u32[]{:S(2)}) copy-start(f32[16]{0:T(128)} %param.40) | copy-start | bytes 196
  118.3 12.8 %copy-start.30 = (f32[16]{0:T(128)S(1)}, f32[16]{0:T(128)}, u32[]{:S(2)}) copy-start(f32[16]{0:T(128)} %param.47) | copy-start | bytes 196
  382.4 18.2 %copy-start.20 = (bf16[3,1024,256]{2,1,0:T(8,128)(2,1)S(1)}, bf16[3,1024,256]{2,1,0:T(8,128)(2,1)}, u32[]{:S(2)}) copy-start(bf16[3,1024,256]{2,1,0:T(8,128)(2,1)} %get-tuple-element.84.w_ref) | copy-start | bytes 4718596
  399.3 1.7 copy-start.23
  399.3 2.0 copy-start.27
  399.4 2.5 copy-start.24
  403.5 64.2 %copy-start = (f32[1024,128]{1,0:T(8,128)S(1)}, f32[1024,128]{1,0:T(8,128)}, u32[]{:S(2)}) copy-start(f32[1024,128]{1,0:T(8,128)} %wd.3) | copy-start | bytes 1572868
  403.5 64.2 %copy-start.1 = (f32[128,1024]{1,0:T(8,128)S(1)}, f32[128,1024]{1,0:T(8,128)}, u32[]{:S(2)}) copy-start(f32[128,1024]{1,0:T(8,128)} %wu.3) | copy-start | bytes 1572868
  403.5 64.2 %copy-start.3 = (f32[3,128,256]{2,1,0:T(8,128)S(1)}, f32[3,128,256]{2,1,0:T(8,128)}, u32[]{:S(2)}) copy-start(f32[3,128,256]{2,1,0:T(8,128)} %wq.3) | copy-start | bytes 1179652
  403.5 64.2 %copy-start.5 = (f32[256,128]{1,0:T(8,128)S(1)}, f32[256,128]{1,0:T(8,128)}, u32[]{:S(2)}) copy-start(f32[256,128]{1,0:T(8,128)} %wp.3) | copy-start | bytes 393220
  403.5 64.2 %copy-start.6 = (f32[128,1024]{1,0:T(8,128)S(1)}, f32[128,1024]{1,0:T(8,128)}, u32[]{:S(2)}) copy-start(f32[128,1024]{1,0:T(8,128)} %mu.1) | copy-start | bytes 1572868
  403.6 64.2 %copy-start.7 = (f32[1024,128]{1,0:T(8,128)S(1)}, f32[1024,128]{1,0:T(8,128)}, u32[]{:S(2)}) copy-start(f32[1024,128]{1,0:T(8,128)} %md.1) | copy-start | bytes 1572868
  403.6 64.2 %copy-start.8 = (f32[128,1024]{1,0:T(8,128)S(1)}, f32[128,1024]{1,0:T(8,128)}, u32[]{:S(2)}) copy-start(f32[128,1024]{1,0:T(8,128)} %su.1) | copy-start | bytes 1572868
  403.6 64.2 %copy-start.9 = (f32[3,128,256]{2,1,0:T(8,128)S(1)}, f32[3,128,256]{2,1,0:T(8,128)}, u32[]{:S(2)}) copy-start(f32[3,128,256]{2,1,0:T(8,128)} %mq.1) | copy-start | bytes 1179652
  403.6 64.2 %copy-start.10 = (f32[3,128,256]{2,1,0:T(8,128)S(1)}, f32[3,128,256]{2,1,0:T(8,128)}, u32[]{:S(2)}) copy-start(f32[3,128,256]{2,1,0:T(8,128)} %sq.1) | copy-start | bytes 1179652
  403.6 64.2 %copy-start.12 = (f32[256,128]{1,0:T(8,128)S(1)}, f32[256,128]{1,0:T(8,128)}, u32[]{:S(2)}) copy-start(f32[256,128]{1,0:T(8,128)} %mp.1) | copy-start | bytes 393220
  403.6 64.2 %copy-start.13 = (f32[256,128]{1,0:T(8,128)S(1)}, f32[256,128]{1,0:T(8,128)}, u32[]{:S(2)}) copy-start(f32[256,128]{1,0:T(8,128)} %sp.1) | copy-start | bytes 393220
  403.6 64.2 %copy-start.15 = (f32[256]{0:T(256)S(1)}, f32[256]{0:T(256)}, u32[]{:S(2)}) copy-start(f32[256]{0:T(256)} %select_maximum_fusion.4) | copy-start | bytes 3076
  467.8 1.0 copy-start.11
  468.8 0.8 copy-start.14
  469.6 0.7 copy-start.16
  474.6 0.5 copy-start.19
  484.9 43.3 %copy-start.17 = (f32[1,128]{1,0:T(1,128)S(1)}, f32[1,128]{1,0:T(1,128)}, u32[]{:S(2)}) copy-start(f32[1,128]{1,0:T(1,128)} %get-tuple-element.103.totals_ref) | copy-start | bytes 1540
  484.9 43.3 %copy-start.18 = (f32[1,128]{1,0:T(1,128)S(1)}, f32[1,128]{1,0:T(1,128)}, u32[]{:S(2)}) copy-start(f32[1,128]{1,0:T(1,128)} %reduce_row.1.update_ref) | copy-start | bytes 1540
  528.2 1.8 copy-start.22
  530.0 2.0 copy-start.21
Sparse Core Ops, SparseCore 0:
  10.8 40.0 all-gather.2
  114.8 84.6 all-gather.4

commit v5 on v4

--- a/solution.py
+++ b/solution.py
@@ -67,61 +67,6 @@
         compiler_params=pltpu.CompilerParams(vmem_limit_bytes=62 * 2**20),
         name="project",
     )(rows, norm, weights)
-
-
-def project_back_kernel(a_ref, grads_ref, w_ref, first_ref, grad_ref, sums_ref, low_ref, total, turned):
-    step = pl.program_id(0)
-
-    @pl.when(step == 0)
-    def _():
-        total[...] = jnp.zeros_like(total)
-        sums_ref[...] = jnp.zeros_like(sums_ref)
-        for c in range(3):
-            turned[c] = w_ref[c].T
-
-    first = jnp.zeros(first_ref.shape, F32)
-    for c in range(3):
-        grads = grads_ref[c]
-        first = first + dot(grads.T, turned[c], 1, 0)
-        total[c] += dot(grads, a_ref[...], 1, 0)
-        sums_ref[c] += jnp.sum(grads.astype(F32), axis=1, keepdims=True)
-    first_ref[...] = first.astype(BF)
-
-    @pl.when(step == pl.num_programs(0) - 1)
-    def _():
-        for c in range(3):
-            grad = total[c].T
-            grad_ref[c] = grad.astype(BF)
-            low_ref[:, c : c + 1] = jnp.sum(grad * w_ref[c].astype(F32), axis=1, keepdims=True)
-
-
-def project_back(a_first, grads, weights):
-    tok, width = a_first.shape
-    cols = grads.shape[1]
-    return pl.pallas_call(
-        project_back_kernel,
-        grid=(tok // BLK,),
-        in_specs=[
-            pl.BlockSpec((BLK, width), lambda s: (s, 0)),
-            pl.BlockSpec((3, cols, BLK), lambda s: (0, 0, s)),
-            pl.BlockSpec((3, width, cols), lambda s: (0, 0, 0)),
-        ],
-        out_specs=[
-            pl.BlockSpec((BLK, width), lambda s: (s, 0)),
-            pl.BlockSpec((3, width, cols), lambda s: (0, 0, 0)),
-            pl.BlockSpec((3, cols, 1), lambda s: (0, 0, 0)),
-            pl.BlockSpec((width, 3), lambda s: (0, 0)),
-        ],
-        out_shape=[
-            jax.ShapeDtypeStruct((tok, width), BF),
-            jax.ShapeDtypeStruct((3, width, cols), BF),
-            jax.ShapeDtypeStruct((3, cols, 1), F32),
-            jax.ShapeDtypeStruct((width, 3), F32),
-        ],
-        scratch_shapes=[pltpu.VMEM((3, cols, width), F32), pltpu.VMEM((3, cols, width), BF)],
-        compiler_params=pltpu.CompilerParams(vmem_limit_bytes=62 * 2**20),
-        name="project_back",
-    )(a_first, grads, weights)
 
 
 def make_slab(pattern, slab):
@@ -971,9 +916,9 @@
 
 def sums_kernel(
     shape, n_bias, n_gain,
-    first_ref, grad_qkv_ref, small_ref, parts_ref, wq_ref, wp_ref, wu_ref, wd_ref, ws_ref,
+    a_ref, heads_ref, w_ref, norm_ref, small_ref, parts_ref, wq_ref, wp_ref, wu_ref, wd_ref, ws_ref,
     rows_ref, added_ref, sum_ref, wide_ref, small_sum_ref, totals_ref,
-    taken, added, plane, both, pieces, small_column, small_plane, row_column, row_plane,
+    first, total, turned, grad_qkv, small_all_ref, taken, added, plane, both, pieces, small_column, small_plane, row_column, row_plane,
     t_send, t_recv, o_send, o_recv, p_send, p_recv, q_send, q_recv, local_sems, small_sems, row_sems,
 ):
     me = place()
@@ -994,7 +939,7 @@
         return pl.ds(pl.multiple_of(which * half, half), half)
 
     def to_sibling(shard):
-        part = first_ref.at[pl.ds(pl.multiple_of(shard * rows, rows), rows), columns_at(1 - core)]
+        part = first.at[shard, :, columns_at(1 - core)]
         return send(part, taken.at[shard], t_send.at[shard], t_recv.at[shard], sibling)
 
     def to_owner():
@@ -1006,11 +951,29 @@
     def add_rows(index):
         shard = shard_at(index)
         to_sibling(shard).wait_recv()
-        here = first_ref[pl.ds(pl.multiple_of(shard * rows, rows), rows), columns_at(core)]
+        here = first[shard, :, columns_at(core)]
         added[shard] = (here.astype(F32) + taken[shard].astype(F32)).astype(BF)
 
-    def plane_part(column):
-        return grad_qkv_ref.at[:, pl.ds(pl.multiple_of(column * 2 * depth, 2 * depth), 2 * depth), :]
+    def plane_part(c, column):
+        return grad_qkv.at[c, pl.ds(pl.multiple_of(column * 2 * depth, 2 * depth), 2 * depth), :]
+
+    def plane_copies(c):
+        for step, there, device in plane_peers(shape, me):
+            yield send(
+                plane_part(c, there), plane.at[xy, c], p_send.at[c, step], p_recv.at[c, xy], device
+            )
+
+    def keep_part(c):
+        return pltpu.make_async_copy(plane_part(c, xy), plane.at[xy, c], local_sems.at[3 + c])
+
+    def back_of_shard(index):
+        shard = shard_at(index)
+        here = pl.ds(pl.multiple_of(shard * rows, rows), rows)
+        part_sum = jnp.zeros((rows, 2 * half), F32)
+        for c in range(3):
+            part_sum = part_sum + dot(heads_ref[c, :, here].T, turned[c], 1, 0)
+        first[shard] = part_sum.astype(BF)
+        to_sibling(shard).start()
 
     def target(c):
         return (xy, c, lax.div(head_block, places), lax.rem(head_block, places))
@@ -1022,16 +985,35 @@
         return both.at[:, c * depth : (c + 1) * depth, :]
 
     greet(shape)
-    to_sibling(shard_at(0)).start()
-    small_all.start(0, small_ref[...])
-    keep_part = pltpu.make_async_copy(plane_part(xy), plane.at[xy], local_sems.at[1])
-    keep_part.start()
-    for step, there, device in plane_peers(shape, me):
-        send(plane_part(there), plane.at[xy], p_send.at[step], p_recv.at[xy], device).start()
-    for index in range(1, parts):
-        to_sibling(shard_at(index)).start()
+    for c in range(3):
+        turned[c] = w_ref[c].T
+    back_of_shard(0)
+    back_of_shard(1)
     add_rows(0)
     to_owner().start()
+
+    shift_one = jnp.zeros((1, 2 * half), F32)
+    gain_one = jnp.zeros((1, 2 * half), F32)
+    for c in range(3):
+        total[...] = jnp.zeros_like(total)
+        for n in range(parts):
+            here = slice(n * rows, (n + 1) * rows)
+            total[...] += dot(heads_ref[c, :, here], a_ref[here, :], 1, 0)
+        grad_qkv[c] = total[...].T.astype(BF)
+        keep_part(c).start()
+        for copy in plane_copies(c):
+            copy.start()
+        wide_turned = turned[c].astype(F32)
+        head_sums = jnp.sum(heads_ref[c].astype(F32), axis=1, keepdims=True)
+        shift_one = shift_one + jnp.sum(wide_turned * head_sums, axis=0, keepdims=True)
+        gain_one = gain_one + jnp.sum(wide_turned * total[...], axis=0, keepdims=True)
+    gain_one = (gain_one - norm_ref[1:2, :] * shift_one) / norm_ref[0:1, :]
+    lines = [
+        vector[:, n : n + LANES] for vector in (gain_one, shift_one) for n in range(0, 2 * half, LANES)
+    ]
+    small_all.start(0, jnp.concatenate([small_ref[...], *lines], axis=0))
+    for index in range(2, parts):
+        back_of_shard(index)
 
     def square(values):
         wide = values.astype(F32)
@@ -1049,14 +1031,15 @@
     values += lane_sums(ws_ref[...] * ws_ref[...], ranges)
     small_all.start(1, small_all.finish(0))
 
-    keep_part.wait()
-    for step, there, device in plane_peers(shape, me):
-        send(plane_part(there), plane.at[there], p_send.at[step], p_recv.at[there], device).wait_recv()
     for c in range(3):
-        total = plane[0, c].astype(F32)
+        keep_part(c).wait()
+        for step, there, device in plane_peers(shape, me):
+            here = plane.at[there, c]
+            send(here, here, p_send.at[c, step], p_recv.at[c, there], device).wait_recv()
+        column_sum = plane[0, c].astype(F32)
         for n in range(1, columns):
-            total = total + plane[n, c].astype(F32)
-        both[c] = total.astype(BF)
+            column_sum = column_sum + plane[n, c].astype(F32)
+        both[c] = column_sum.astype(BF)
     for c in range(2):
 
         @pl.when(is_same(target(c), me))
@@ -1070,8 +1053,7 @@
     for index in range(1, parts):
         add_rows(index)
     keep_added.start()
-    small = small_all.finish(1)
-    small_sum_ref[...] = small
+    small_all_ref[...] = small_all.finish(1)
     for n in range(2):
 
         @pl.when(is_same(target(n), me))
@@ -1088,19 +1070,37 @@
 
     squares = []
     for c in range(3):
-        total = pieces[0, c].astype(F32) + pieces[1, c].astype(F32)
-        sum_ref[c] = total
-        squares.append(square(total))
+        piece_sum = pieces[0, c].astype(F32) + pieces[1, c].astype(F32)
+        sum_ref[c] = piece_sum
+        squares.append(square(piece_sum))
     row_all.start(0, row_of(squares + values))
     row_all.start(1, row_all.finish(0))
     row = row_all.finish(1)
     lane = lax.broadcasted_iota(jnp.int32, (1, 128), 1)
-    for n, value in enumerate(lane_sums(small * small, ranges)):
+    devices = small_ref.shape[0]
+    count = 2 * half // LANES
+    small = small_all_ref[0:devices, :]
+    small_squares = lane_sums(small * small, ranges)
+    for vector, spot in ((0, 1), (1, 3)):
+        line = small_all_ref[devices + vector * count : devices + (vector + 1) * count, :]
+        small_squares[spot] = jnp.sum(line * line)
+    for n, value in enumerate(small_squares):
         row = jnp.where(lane == 17 + n, value, row)
     totals_ref[...] = row
-
-    for step, there, device in plane_peers(shape, me):
-        send(plane_part(there), plane.at[xy], p_send.at[step], p_recv.at[xy], device).wait_send()
+    number = ((xy * 2 + core) * 2 + zh) * places + zl
+    mine = small_all_ref[pl.ds(number, 1), :]
+    column = lax.broadcasted_iota(jnp.int32, (1, LANES), 1)
+    for vector, spot in ((0, 1), (1, 3)):
+        low, high = ranges[spot]
+        at = number * n_gain
+        line = small_all_ref[pl.ds(devices + vector * count + lax.div(at, LANES), 1), :]
+        line = pltpu.roll(line, lax.rem(low + LANES - lax.rem(at, LANES), LANES), 1)
+        mine = jnp.where((column >= low) & (column < high), line, mine)
+    small_sum_ref[...] = mine
+
+    for c in range(3):
+        for copy in plane_copies(c):
+            copy.wait_send()
     for shard in range(parts):
         to_sibling(shard).wait_send()
     keep_added.wait()
@@ -1201,12 +1201,13 @@
     return wide_ref[:, :ff], wide_ref[:, ff : 2 * ff], wide_ref[:, 2 * ff : 2 * ff + heads]
 
 
-def sums(shape, n_bias, n_gain, first, grad_qkv, small, wide, weights):
+def sums(shape, n_bias, n_gain, a_first, grad_heads, w_heads, norm, small, wide, weights):
     places, columns = shape["zl"], shape["xy"]
     members, parts = 4 * places, 2 * places
-    rows, width = first.shape[0] // parts, first.shape[1]
-    depth = grad_qkv.shape[1] // (2 * columns)
-    heads_cols = grad_qkv.shape[2]
+    rows, width = a_first.shape[0] // parts, a_first.shape[1]
+    depth = width // (2 * columns)
+    heads_cols = w_heads.shape[2]
+    lines = (small.shape[0] + 2 * width // LANES, LANES)
     vmem = pl.BlockSpec(memory_space=pltpu.VMEM)
     anywhere = pl.BlockSpec(memory_space=pl.ANY)
     dma = pltpu.SemaphoreType.DMA
@@ -1218,30 +1219,35 @@
             jax.ShapeDtypeStruct((parts, rows, width // 2), BF),
             jax.ShapeDtypeStruct((3, depth, heads_cols), F32),
             jax.ShapeDtypeStruct(wide.shape[1:], F32),
-            jax.ShapeDtypeStruct(small.shape, F32),
+            jax.ShapeDtypeStruct((1, LANES), F32),
             jax.ShapeDtypeStruct((1, 128), F32),
         ],
-        in_specs=[vmem, anywhere] + [vmem] * 7,
+        in_specs=[vmem] * 11,
         out_specs=[anywhere] * 2 + [vmem] * 4,
         scratch_shapes=[
+            pltpu.VMEM((parts, rows, width), BF),
+            pltpu.VMEM((heads_cols, width), F32),
+            pltpu.VMEM((3, heads_cols, width), BF),
+            pltpu.VMEM((3, width, heads_cols), BF),
+            pltpu.VMEM(lines, F32),
             pltpu.VMEM((parts, rows, width // 2), BF),
             pltpu.VMEM((parts, rows, width // 2), BF),
             pltpu.VMEM((columns, 3, 2 * depth, heads_cols), BF),
             pltpu.VMEM((3, 2 * depth, heads_cols), BF),
             pltpu.VMEM((2, 3, depth, heads_cols), BF),
-            pltpu.VMEM((members, *small.shape), F32),
-            pltpu.VMEM((columns, *small.shape), F32),
+            pltpu.VMEM((members, *lines), F32),
+            pltpu.VMEM((columns, *lines), F32),
             pltpu.VMEM((members, 1, 128), F32),
             pltpu.VMEM((columns, 1, 128), F32),
             dma((parts,)), dma((parts,)), dma((parts,)), dma((places, 2)),
-            dma((columns,)), dma((columns,)), dma((2,)), dma((2,)), dma((3,)),
+            dma((3, columns)), dma((3, columns)), dma((2,)), dma((2,)), dma((6,)),
             dma((4, slots)), dma((4, slots)),
         ],
         compiler_params=pltpu.CompilerParams(
-            collective_id=3, has_side_effects=True, vmem_limit_bytes=56 * 2**20
+            collective_id=3, has_side_effects=True, vmem_limit_bytes=50 * 2**20
         ),
         name="sums",
-    )(first, grad_qkv, small, wide, *weights)
+    )(a_first, grad_heads, w_heads, norm, small, wide, *weights)
 
 
 def reduce_kernel(shape, row_ref, total_ref, row_column, row_plane, row_sems):
@@ -1271,7 +1277,7 @@
 
 
 def moments_kernel(
-    n_bias, n_gain, spot_ref, totals_ref, small_ref,
+    n_bias, n_gain, totals_ref, small_ref,
     gq, wide, wq, wp, wu, wd, ws, mq, mp, mu, md, ms, sq, sp, su, sd, ss,
     nmq, nmp, nmu, nmd, nmb, nmg, nmt, nsq, nsp, nsu, nsd, nsb, nsg, nst, uq, up, uu, ud, us, row_ref,
 ):
@@ -1303,9 +1309,7 @@
         nm[...], ns[...], update = step(grad.T if turned else grad, w[...], m[...], s[...])
         u[...] = update
         values.append(jnp.sum(update * update))
-    spot = spot_ref[0]
-    grad = small_ref[pl.ds(spot, 1), :]
-    new_mean, new_square, update = step(grad, ws[...], ms[...], ss[...])
+    new_mean, new_square, update = step(small_ref[...], ws[...], ms[...], ss[...])
     us[...] = update
     ranges = small_ranges(n_bias, n_gain)
     values += lane_sums(update * update, ranges)
@@ -1352,7 +1356,7 @@
     return [jax.ShapeDtypeStruct(array.shape, F32) for array in arrays]
 
 
-def optimizer(shape, n_bias, n_gain, spot, totals, small, grads, weights, means, squares, small_like):
+def optimizer(shape, n_bias, n_gain, totals, small, grads, weights, means, squares, small_like):
     vmem = pl.BlockSpec(memory_space=pltpu.VMEM)
     big = list(weights[:4])
     results = shapes_of(big) + shapes_of(small_like)
@@ -1361,11 +1365,11 @@
     out = pl.pallas_call(
         functools.partial(moments_kernel, n_bias, n_gain),
         out_shape=results * 2 + shapes_of(weights) + [row],
-        in_specs=[pl.BlockSpec(memory_space=pltpu.SMEM)] + [vmem] * 19,
+        in_specs=[vmem] * 19,
         out_specs=[vmem] * 20,
         compiler_params=params,
         name="moments",
-    )(spot, totals, small, *grads, *weights, *means, *squares)
+    )(totals, small, *grads, *weights, *means, *squares)
     new_means, new_squares, updates, row_here = out[:7], out[7:14], out[14:19], out[19]
     updates_total = reduce_row(shape, row_here)
     out = pl.pallas_call(
@@ -1738,7 +1742,6 @@
     heads = w_qkv.shape[2] // DH
     tok = rows * parts
     xy, core, zh, zl = place()
-    me = ((xy * 2 + core) * 2 + zh) * places + zl
     head_block = zl * 2 + core
 
     ff_local, heads_cols = w_up.shape[1], w_proj.shape[0]
@@ -1768,9 +1771,8 @@
     other_len = lax.ppermute(item_len, "core", [(0, 1), (1, 0)])
     split = jnp.where(zh == core, item_len, other_len)[0, 0:1]
 
-    a_first, qkv = project(
-        group_rows.reshape(tok, width), jnp.stack([gains[0], shifts[0]]), w_heads
-    )
+    norm_one = jnp.stack([gains[0], shifts[0]])
+    a_first, qkv = project(group_rows.reshape(tok, width), norm_one, w_heads)
     qkv = qkv.reshape(3 * heads * DH, tok)
 
     table = lax.dynamic_slice_in_dim(
@@ -1798,10 +1800,6 @@
     )
     grad_heads = grad_heads.reshape(3, heads * DH, tok)
 
-    first, grad_qkv, head_sums, column_sums = project_back(a_first, grad_heads, w_heads)
-    shift_one = jnp.sum(w_heads.astype(F32) * head_sums.reshape(3, 1, heads * DH), axis=(0, 2))
-    gain_one = (jnp.sum(column_sums, axis=1) - shifts[0] * shift_one) / gains[0]
-
     bias_grad = lax.dot_general(
         one_hot, grad_pattern[:, 0, :tok], (((1,), (1,)), ((), ())),
         precision=HIGHEST, preferred_element_type=F32,
@@ -1816,19 +1814,19 @@
     small_grad = jnp.concatenate(
         [
             table_grad.reshape(devices, n_bias),
-            by_device(gain_one, gain_two),
-            by_device(shift_one, shift_two),
+            by_device(jnp.zeros_like(gain_two), gain_two),
+            by_device(jnp.zeros_like(shift_two), shift_two),
             jnp.zeros((devices, LANES - n_small), F32),
         ],
         axis=1,
     )
     weights = (w_qkv, w_proj, w_up, w_down, small_weights)
     early_rows, added, sum_qkv, wide_sum, small_sum, totals = sums(
-        shape, n_bias, n_gain, first, grad_qkv, small_grad, wide_parts, weights
+        shape, n_bias, n_gain, a_first, grad_heads, w_heads, norm_one, small_grad, wide_parts, weights
     )
     small_like = [rel_bias[None, :], ln_gain, ln_shift]
     updates_total, grad_norm, param_norms, *results = optimizer(
-        shape, n_bias, n_gain, me[None].astype(jnp.int32), totals, small_sum,
+        shape, n_bias, n_gain, totals, small_sum,
         (sum_qkv, wide_sum), weights,
         (mean_qkv, mean_proj, mean_up, mean_down, pack(mean_bias, mean_gain, mean_shift)),
         (square_qkv, square_proj, square_up, square_down, pack(square_bias, square_gain, square_shift)),

time: 547 us -> 536 us (0.980)
  Pallas kernels: 505 us -> 496 us
    pallas_call x1 -> x0, Pallas kernels: 16.9 us -> none  [project_back(): pl.pallas_call(project_back_kernel, grid=(tok // BLK,), in_specs=[pl.Bloc...]
    pallas_call x1, Pallas kernels: 64.1 us -> 71.4 us  [sums(): pl.pallas_call(functools.partial(sums_kernel, shape, n_bias, n_gain), out...]
  transfers between devices with their start and end apart: 3 -> 3, of which waited for: 0 -> 0; matrix products, arithmetic and copies ran while one was open for 1% -> 1% of each run, Pallas kernels for 34% -> 35%
where the time goes in v5:
time: 536 us; the launch traced here: 529 us
  Pallas kernels  496 us (93%)
  between operations  14.9 us (3%)
  local copies, waits for them, and re-layouts  11.5 us (2%)
  other arithmetic  5.38 us (1%)
    pallas_call x1, Pallas kernels, gather(): pl.pallas_call(functools.partial(gather_kernel, shape), out_shape=[jax.Sh...  102 us
    pallas_call x1, Pallas kernels, attend_back(): pl.pallas_call(functools.partial(attend_back_kernel, shape, segments), gr...  93 us
    pallas_call x1, Pallas kernels, feed_forward(): pl.pallas_call(functools.partial(feed_kernel, shape, ff_local), grid=(ste...  87.6 us
    pallas_call x1, Pallas kernels, sums(): pl.pallas_call(functools.partial(sums_kernel, shape, n_bias, n_gain), out...  71.4 us
    pallas_call x1, Pallas kernels, attend(): pl.pallas_call(functools.partial(attend_kernel, shape), grid=(heads,), in...  70 us
    pallas_call x1, Pallas kernels, finish_rows(): pl.pallas_call(functools.partial(rows_kernel, shape), out_shape=jax.Shape...  43.7 us
    pallas_call x1, Pallas kernels, project(): pl.pallas_call(project_kernel, grid=(tok // BLK,), in_specs=[pl.BlockSpec...  12.7 us
  transfers between devices with their start and end apart: 3, of which 0 were waited for; matrix products, arithmetic and copies ran while one was open for 1% of the time, Pallas kernels for 35%

profile of v5, /device:TPU:8, one launch (start us, length us, event | category | flops | bytes accessed | tf_op | source)
XLA Modules:
  0.0 529.0 jit_solution(13076015759604829354)
XLA Ops:
  7.3 1.2 copy.55
  8.5 1.1 convert.11
  9.7 0.1 copy.56
  9.8 0.9 pad_maximum_fusion.wide_ref
  10.7 0.1 reshape.111
  10.8 0.1 reshape.112
  10.9 0.7 convert_element_type.9.wq_ref
  11.6 0.6 select_maximum_fusion.4
  12.2 102.4 %gather.1 = (bf16[4,768,1024]{2,1,0:T(8,128)(2,1)}, bf16[3,1024,256]{2,1,0:T(8,128)(2,1)}, f32[8,4,1,256]{3,2,1,0:T(1,128)}, bf16[3,128,2304]{2,1,0:T(8,128)(2,1)}) custom-call(bf16[768,1024]{1,0:T(8,128)(2,1)} %x_ref.3, bf16[3,128,256]{2,1,0:T(8,128)(2,1)} %convert_element_type.9.wq_ref, f32[1,256]{1,0:T(1,128)} %bitcast.31, ...), custom_call_target="tpu_custom_call" | custom-call | tf_op jit(solution)/shard_map/gather/pallas_call | solution.py:808
  114.8 0.6 copy-done.21
  115.4 0.1 reduce
  115.6 0.1 reshape.115
  115.7 0.1 reshape.116
  115.7 0.2 slice_reduce_fusion
  115.9 0.1 slice.50.gain_ref
  116.1 0.3 convolution_multiply_fusion
  116.5 0.7 broadcast_in_dim.22.pattern_ref
  117.3 0.1 reshape.125
  117.4 0.1 reshape.126
  117.5 0.1 reshape.127
  117.5 0.1 reshape.128
  117.7 0.6 pad_maximum_fusion.1.norm_ref
  118.3 12.7 %project.1 = (bf16[3072,1024]{1,0:T(8,128)(2,1)}, bf16[3,256,3072]{2,1,0:T(8,128)(2,1)}) custom-call(bf16[3072,1024]{1,0:T(8,128)(2,1)} %bitcast.43, f32[2,1024]{1,0:T(2,128)} %pad_maximum_fusion.1.norm_ref, bf16[3,1024,256]{2,1,0:T(8,128)(2,1)} %get-tuple-element.80.w_ref), custom_call_target="tpu_custom_call" | custom-call | tf_op jit(solution)/shard_map/project/pallas_call | solution.py:50
  131.2 0.6 pad_maximum_fusion.2.norm_ref
  131.8 0.5 broadcast_select_fusion
  132.3 70.0 %attend.1 = (bf16[4,64,3072]{2,1,0:T(8,128)(2,1)}, bf16[4,4,64,768]{3,2,1,0:T(8,128)(2,1)}, f32[4,1,3072]{2,1,0:T(1,128)}) custom-call(s32[1]{0:T(128)} %bitcast.53, f32[4,1,3584]{2,1,0:T(1,128)} %broadcast_in_dim.22.pattern_ref, bf16[768,3072]{1,0:T(8,128)(2,1)} %bitcast.37, bf16[768,3072]{1,0:T(8,128)(2,1)} %bitcast.38, bf16[768,3072]{1,0:T(8,128)(2,1)} %bitcast.39), custom_call_target="tpu_custom_call" | custom-call | tf_op jit(solution)/shard_map/attend/pallas_call | solution.py:205
  202.4 87.6 %feed_forward.1 = (bf16[768,1024]{1,0:T(8,128)(2,1)}, f32[768,1024]{1,0:T(8,128)}, bf16[1024,768]{1,0:T(8,128)(2,1)}, bf16[2,128,9216]{2,1,0:T(8,128)(2,1)}, f32[2,1024]{1,0:T(2,128)}) custom-call(bf16[768,1024]{1,0:T(8,128)(2,1)} %x_ref.3, bf16[768,1024]{1,0:T(8,128)(2,1)} %c_ref.1, bf16[4,256,768]{2,1,0:T(8,128)(2,1)} %bitcast.46, ...), custom_call_target="tpu_custom_call" | custom-call | tf_op jit(solution)/shard_map/feed_forward/pallas_call | solution.py:1660
  290.0 93.0 %attend_back.1 = (bf16[3,4,64,3072]{3,2,1,0:T(8,128)(2,1)}, bf16[4,128,2304]{2,1,0:T(8,128)(2,1)}, f32[4,1,3584]{2,1,0:T(1,128)}) custom-call(s32[1]{0:T(128)} %bitcast.54, f32[4,1,3584]{2,1,0:T(1,128)} %broadcast_in_dim.22.pattern_ref, bf16[768,3072]{1,0:T(8,128)(2,1)} %bitcast.40, bf16[768,3072]{1,0:T(8,128)(2,1)} %bitcast.41, bf16[768,3072]{1,0:T(8,128)(2,1)} %bitcast.42, ...), custom_call_target="tpu_custom_call" | custom-call | tf_op jit(solution)/shard_map/attend_back/pallas_call | solution.py:397
  383.0 0.8 slice.58
  383.8 0.3 fusion
  384.2 0.1 reshape.121
  384.3 0.1 reshape.122
  384.4 0.1 reshape.123
  384.5 0.1 reshape.124
  384.6 0.5 dynamic_update_slice.3
  385.1 0.1 maximum_maximum_fusion.small_ref
  385.3 71.4 %sums.1 = (bf16[2,768,1024]{2,1,0:T(8,128)(2,1)}, bf16[4,768,512]{2,1,0:T(8,128)(2,1)}, f32[3,128,256]{2,1,0:T(8,128)S(1)}, f32[128,2304]{1,0:T(8,128)S(1)}, f32[1,256]{1,0:T(1,128)S(1)}, /*index=5*/f32[1,128]{1,0:T(1,128)S(1)}) custom-call(bf16[3072,1024]{1,0:T(8,128)(2,1)} %get-tuple-element.85.a_ref, bf16[3,256,3072]{2,1,0:T(8,128)(2,1)} %bitcast.44, ...), custom_call_target="tpu_custom_call" | custom-call | tf_op jit(solution)/shard_map/sums/pallas_call | solution.py:1215
  456.7 1.0 copy-done.4
  457.8 4.4 moments.1
  462.2 0.6 copy-done.12
  462.8 0.5 copy-done.17
  463.3 9.8 %reduce_row.1.update_ref = f32[1,128]{1,0:T(1,128)} custom-call(f32[1,128]{1,0:T(1,128)} %copy-done.17), custom_call_target="tpu_custom_call" | custom-call | tf_op jit(solution)/shard_map/reduce_row/pallas_call | solution.py:1264
  473.2 43.7 %finish_rows.1 = bf16[768,1024]{1,0:T(8,128)(2,1)} custom-call(bf16[4,768,512]{2,1,0:T(8,128)(2,1)} %get-tuple-element.100.added_ref, bf16[2,768,1024]{2,1,0:T(8,128)(2,1)} %get-tuple-element.101.early_ref, bf16[768,1024]{1,0:T(8,128)(2,1)} %x_ref.3, f32[768,1024]{1,0:T(8,128)} %get-tuple-element.102.middle_ref, f32[1,1024]{1,0:T(1,128)} %copy-done.20), custom_call_target="tpu_custom_call" | custom-call | tf_op jit(solution)/shard_map/finish_rows/pallas_call | solution.py:1183
  517.0 1.4 weights.1
  518.4 0.4 copy-done.19
  518.8 1.1 copy.74
  520.0 0.8 copy-done.18
  520.8 1.1 copy.75
  (87 shorter events, 1.1 us)
Async XLA Ops:
  7.2 2.4 copy-start.3
  7.2 195.1 %all-gather.3.cloned.1.call-start = ((), (), s32[]{:S(2)}) async-start(), calls=%async_computation | async-start | bytes 5308416 | tf_op jit(solution)/shard_map/all_gather | solution.py:1750
  8.5 2.2 copy-start.28
  8.5 2.3 copy-start.29
  8.5 2.4 copy-start.2
  8.5 3.1 copy-start.23
  10.6 191.7 %all-gather.5.cloned.1.call-start = ((), (), s32[]{:S(2)}) async-start(), calls=%async_computation.1 | async-start | bytes 15925248 | tf_op jit(solution)/shard_map/all_gather | solution.py:1762
  12.2 102.5 %copy-start.26 = (s32[1,2]{1,0:T(1,128)S(1)}, s32[1,2]{1,0:T(1,128)}, u32[]{:S(2)}) copy-start(s32[1,2]{1,0:T(1,128)} %param.27) | copy-start | bytes 28
  114.6 0.8 copy-start.21
  114.6 1.5 copy-start.27
  114.6 2.7 copy-start.30
  114.6 2.7 copy-start.31
  114.6 2.8 copy-start.32
  114.7 2.9 copy-start.33
  114.7 17.1 %collective-permute-start = (s32[1,2]{1,0:T(1,128)S(1)}, s32[1,2]{1,0:T(1,128)S(1)}, u32[]{:S(2)}, u32[]{:S(2)}) collective-permute-start(s32[1,2]{1,0:T(1,128)S(1)} %copy-done.26), channel_id=1, source_target_pairs={{0,4},{4,0},{1,5},{5,1},{2,6},{6,2},{3,7},{7,3},{8,12},{12,8},{9,1... | collective-permute-start | bytes 32 | tf_op jit(solution)/shard_map/ppermute | solution.py:1771
  116.0 15.0 %copy-start.20 = (f32[1,1024]{1,0:T(1,128)}, f32[1,1024]{1,0:T(1,128)S(1)}, u32[]{:S(2)}) copy-start(f32[1,1024]{1,0:T(1,128)S(1)} %slice.50.gain_ref) | copy-start | bytes 12292
  118.3 12.7 %copy-start.24 = (f32[16]{0:T(128)S(1)}, f32[16]{0:T(128)}, u32[]{:S(2)}) copy-start(f32[16]{0:T(128)} %param.40) | copy-start | bytes 196
  118.3 12.8 %copy-start.25 = (f32[16]{0:T(128)S(1)}, f32[16]{0:T(128)}, u32[]{:S(2)}) copy-start(f32[16]{0:T(128)} %param.47) | copy-start | bytes 196
  290.0 94.1 %copy-start.22 = (f32[2,1024]{1,0:T(2,128)S(1)}, f32[2,1024]{1,0:T(2,128)}, u32[]{:S(2)}) copy-start(f32[2,1024]{1,0:T(2,128)} %get-tuple-element.92) | copy-start | bytes 24580
  290.0 95.2 %copy-start = (f32[1024,128]{1,0:T(8,128)S(1)}, f32[1024,128]{1,0:T(8,128)}, u32[]{:S(2)}) copy-start(f32[1024,128]{1,0:T(8,128)} %wd.3) | copy-start | bytes 1572868
  290.0 95.2 %copy-start.1 = (f32[128,1024]{1,0:T(8,128)S(1)}, f32[128,1024]{1,0:T(8,128)}, u32[]{:S(2)}) copy-start(f32[128,1024]{1,0:T(8,128)} %wu.3) | copy-start | bytes 1572868
  290.0 95.2 %copy-start.14 = (f32[2,1024]{1,0:T(2,128)S(1)}, f32[2,1024]{1,0:T(2,128)}, u32[]{:S(2)}) copy-start(f32[2,1024]{1,0:T(2,128)} %pad_maximum_fusion.1.norm_ref) | copy-start | bytes 24580
  290.0 95.2 %copy-start.15 = (f32[256]{0:T(256)S(1)}, f32[256]{0:T(256)}, u32[]{:S(2)}) copy-start(f32[256]{0:T(256)} %select_maximum_fusion.4) | copy-start | bytes 3076
  385.2 72.5 %copy-start.5 = (f32[128,1024]{1,0:T(8,128)S(1)}, f32[128,1024]{1,0:T(8,128)}, u32[]{:S(2)}) copy-start(f32[128,1024]{1,0:T(8,128)} %mu.1) | copy-start | bytes 1572868
  385.3 72.5 %copy-start.6 = (f32[1024,128]{1,0:T(8,128)S(1)}, f32[1024,128]{1,0:T(8,128)}, u32[]{:S(2)}) copy-start(f32[1024,128]{1,0:T(8,128)} %md.1) | copy-start | bytes 1572868
  385.3 72.5 %copy-start.7 = (f32[128,1024]{1,0:T(8,128)S(1)}, f32[128,1024]{1,0:T(8,128)}, u32[]{:S(2)}) copy-start(f32[128,1024]{1,0:T(8,128)} %su.1) | copy-start | bytes 1572868
  385.3 72.4 %copy-start.8 = (f32[3,128,256]{2,1,0:T(8,128)S(1)}, f32[3,128,256]{2,1,0:T(8,128)}, u32[]{:S(2)}) copy-start(f32[3,128,256]{2,1,0:T(8,128)} %mq.1) | copy-start | bytes 1179652
  385.3 72.4 %copy-start.9 = (f32[3,128,256]{2,1,0:T(8,128)S(1)}, f32[3,128,256]{2,1,0:T(8,128)}, u32[]{:S(2)}) copy-start(f32[3,128,256]{2,1,0:T(8,128)} %sq.1) | copy-start | bytes 1179652
  385.3 72.4 %copy-start.10 = (f32[256,128]{1,0:T(8,128)S(1)}, f32[256,128]{1,0:T(8,128)}, u32[]{:S(2)}) copy-start(f32[256,128]{1,0:T(8,128)} %mp.1) | copy-start | bytes 393220
  385.3 72.4 %copy-start.11 = (f32[256,128]{1,0:T(8,128)S(1)}, f32[256,128]{1,0:T(8,128)}, u32[]{:S(2)}) copy-start(f32[256,128]{1,0:T(8,128)} %sp.1) | copy-start | bytes 393220
  456.7 1.0 copy-start.4
  462.2 0.7 copy-start.12
  462.8 0.5 copy-start.17
  473.2 43.8 %copy-start.13 = (f32[256,128]{1,0:T(8,128)S(1)}, f32[256,128]{1,0:T(8,128)}, u32[]{:S(2)}) copy-start(f32[256,128]{1,0:T(8,128)} %copy-done.12) | copy-start | bytes 393220
  473.2 43.8 %copy-start.16 = (f32[1,128]{1,0:T(1,128)S(1)}, f32[1,128]{1,0:T(1,128)}, u32[]{:S(2)}) copy-start(f32[1,128]{1,0:T(1,128)} %reduce_row.1.update_ref) | copy-start | bytes 1540
  517.0 1.8 copy-start.19
  518.8 2.0 copy-start.18
Sparse Core Ops, SparseCore 0:
  10.8 40.0 all-gather.2
  114.8 84.5 all-gather.4

commit v6 on v5

--- a/solution.py
+++ b/solution.py
@@ -1029,7 +1029,6 @@
     values += [square(ref[...]) for ref in (wp_ref, wu_ref, wd_ref)]
     ranges = small_ranges(n_bias, n_gain)
     values += lane_sums(ws_ref[...] * ws_ref[...], ranges)
-    small_all.start(1, small_all.finish(0))
 
     for c in range(3):
         keep_part(c).wait()
@@ -1050,6 +1049,7 @@
         def _():
             send(part(c), pieces.at[zh], q_send.at[c], q_recv.at[zh], target(c)).start()
 
+    small_all.start(1, small_all.finish(0))
     for index in range(1, parts):
         add_rows(index)
     keep_added.start()

time: 536 us -> 534 us (level)
  no operation moved by 1% of the time
where the time goes in v6:
time: 534 us; the launch traced here: 527 us
  Pallas kernels  495 us (93%)
  between operations  14.9 us (3%)
  local copies, waits for them, and re-layouts  11.5 us (2%)
  other arithmetic  5.38 us (1%)
    pallas_call x1, Pallas kernels, gather(): pl.pallas_call(functools.partial(gather_kernel, shape), out_shape=[jax.Sh...  102 us
    pallas_call x1, Pallas kernels, attend_back(): pl.pallas_call(functools.partial(attend_back_kernel, shape, segments), gr...  93 us
    pallas_call x1, Pallas kernels, feed_forward(): pl.pallas_call(functools.partial(feed_kernel, shape, ff_local), grid=(ste...  87.6 us
    pallas_call x1, Pallas kernels, sums(): pl.pallas_call(functools.partial(sums_kernel, shape, n_bias, n_gain), out...  70 us
    pallas_call x1, Pallas kernels, attend(): pl.pallas_call(functools.partial(attend_kernel, shape), grid=(heads,), in...  70 us
    pallas_call x1, Pallas kernels, finish_rows(): pl.pallas_call(functools.partial(rows_kernel, shape), out_shape=jax.Shape...  43.3 us
    pallas_call x1, Pallas kernels, project(): pl.pallas_call(project_kernel, grid=(tok // BLK,), in_specs=[pl.BlockSpec...  12.7 us
  transfers between devices with their start and end apart: 3, of which 0 were waited for; matrix products, arithmetic and copies ran while one was open for 1% of the time, Pallas kernels for 35%

profile of v6, /device:TPU:8, one launch (start us, length us, event | category | flops | bytes accessed | tf_op | source)
XLA Modules:
  0.0 527.3 jit_solution(5903896693266470180)
XLA Ops:
  7.3 1.2 copy.55
  8.5 1.1 convert.11
  9.7 0.1 copy.56
  9.8 0.9 pad_maximum_fusion.wide_ref
  10.7 0.1 reshape.111
  10.8 0.1 reshape.112
  10.9 0.7 convert_element_type.9.wq_ref
  11.6 0.6 select_maximum_fusion.4
  12.2 102.4 %gather.1 = (bf16[4,768,1024]{2,1,0:T(8,128)(2,1)}, bf16[3,1024,256]{2,1,0:T(8,128)(2,1)}, f32[8,4,1,256]{3,2,1,0:T(1,128)}, bf16[3,128,2304]{2,1,0:T(8,128)(2,1)}) custom-call(bf16[768,1024]{1,0:T(8,128)(2,1)} %x_ref.3, bf16[3,128,256]{2,1,0:T(8,128)(2,1)} %convert_element_type.9.wq_ref, f32[1,256]{1,0:T(1,128)} %bitcast.31, ...), custom_call_target="tpu_custom_call" | custom-call | tf_op jit(solution)/shard_map/gather/pallas_call | solution.py:808
  114.8 0.6 copy-done.21
  115.4 0.1 reduce
  115.6 0.1 reshape.115
  115.7 0.1 reshape.116
  115.7 0.2 slice_reduce_fusion
  115.9 0.1 slice.50.gain_ref
  116.1 0.3 convolution_multiply_fusion
  116.5 0.7 broadcast_in_dim.22.pattern_ref
  117.3 0.1 reshape.125
  117.4 0.1 reshape.126
  117.5 0.1 reshape.127
  117.5 0.1 reshape.128
  117.7 0.6 pad_maximum_fusion.1.norm_ref
  118.3 12.7 %project.1 = (bf16[3072,1024]{1,0:T(8,128)(2,1)}, bf16[3,256,3072]{2,1,0:T(8,128)(2,1)}) custom-call(bf16[3072,1024]{1,0:T(8,128)(2,1)} %bitcast.43, f32[2,1024]{1,0:T(2,128)} %pad_maximum_fusion.1.norm_ref, bf16[3,1024,256]{2,1,0:T(8,128)(2,1)} %get-tuple-element.80.w_ref), custom_call_target="tpu_custom_call" | custom-call | tf_op jit(solution)/shard_map/project/pallas_call | solution.py:50
  131.2 0.6 pad_maximum_fusion.2.norm_ref
  131.8 0.5 broadcast_select_fusion
  132.3 70.0 %attend.1 = (bf16[4,64,3072]{2,1,0:T(8,128)(2,1)}, bf16[4,4,64,768]{3,2,1,0:T(8,128)(2,1)}, f32[4,1,3072]{2,1,0:T(1,128)}) custom-call(s32[1]{0:T(128)} %bitcast.53, f32[4,1,3584]{2,1,0:T(1,128)} %broadcast_in_dim.22.pattern_ref, bf16[768,3072]{1,0:T(8,128)(2,1)} %bitcast.37, bf16[768,3072]{1,0:T(8,128)(2,1)} %bitcast.38, bf16[768,3072]{1,0:T(8,128)(2,1)} %bitcast.39), custom_call_target="tpu_custom_call" | custom-call | tf_op jit(solution)/shard_map/attend/pallas_call | solution.py:205
  202.4 87.6 %feed_forward.1 = (bf16[768,1024]{1,0:T(8,128)(2,1)}, f32[768,1024]{1,0:T(8,128)}, bf16[1024,768]{1,0:T(8,128)(2,1)}, bf16[2,128,9216]{2,1,0:T(8,128)(2,1)}, f32[2,1024]{1,0:T(2,128)}) custom-call(bf16[768,1024]{1,0:T(8,128)(2,1)} %x_ref.3, bf16[768,1024]{1,0:T(8,128)(2,1)} %c_ref.1, bf16[4,256,768]{2,1,0:T(8,128)(2,1)} %bitcast.46, ...), custom_call_target="tpu_custom_call" | custom-call | tf_op jit(solution)/shard_map/feed_forward/pallas_call | solution.py:1660
  290.0 93.0 %attend_back.1 = (bf16[3,4,64,3072]{3,2,1,0:T(8,128)(2,1)}, bf16[4,128,2304]{2,1,0:T(8,128)(2,1)}, f32[4,1,3584]{2,1,0:T(1,128)}) custom-call(s32[1]{0:T(128)} %bitcast.54, f32[4,1,3584]{2,1,0:T(1,128)} %broadcast_in_dim.22.pattern_ref, bf16[768,3072]{1,0:T(8,128)(2,1)} %bitcast.40, bf16[768,3072]{1,0:T(8,128)(2,1)} %bitcast.41, bf16[768,3072]{1,0:T(8,128)(2,1)} %bitcast.42, ...), custom_call_target="tpu_custom_call" | custom-call | tf_op jit(solution)/shard_map/attend_back/pallas_call | solution.py:397
  383.0 0.8 slice.58
  383.8 0.3 fusion
  384.2 0.1 reshape.121
  384.3 0.1 reshape.122
  384.4 0.1 reshape.123
  384.5 0.1 reshape.124
  384.6 0.5 dynamic_update_slice.3
  385.1 0.1 maximum_maximum_fusion.small_ref
  385.3 70.0 %sums.1 = (bf16[2,768,1024]{2,1,0:T(8,128)(2,1)}, bf16[4,768,512]{2,1,0:T(8,128)(2,1)}, f32[3,128,256]{2,1,0:T(8,128)S(1)}, f32[128,2304]{1,0:T(8,128)S(1)}, f32[1,256]{1,0:T(1,128)S(1)}, /*index=5*/f32[1,128]{1,0:T(1,128)S(1)}) custom-call(bf16[3072,1024]{1,0:T(8,128)(2,1)} %get-tuple-element.85.a_ref, bf16[3,256,3072]{2,1,0:T(8,128)(2,1)} %bitcast.44, ...), custom_call_target="tpu_custom_call" | custom-call | tf_op jit(solution)/shard_map/sums/pallas_call | solution.py:1215
  455.4 1.0 copy-done.4
  456.4 4.4 moments.1
  460.9 0.6 copy-done.12
  461.5 0.5 copy-done.17
  462.0 9.8 %reduce_row.1.update_ref = f32[1,128]{1,0:T(1,128)} custom-call(f32[1,128]{1,0:T(1,128)} %copy-done.17), custom_call_target="tpu_custom_call" | custom-call | tf_op jit(solution)/shard_map/reduce_row/pallas_call | solution.py:1264
  471.9 43.3 %finish_rows.1 = bf16[768,1024]{1,0:T(8,128)(2,1)} custom-call(bf16[4,768,512]{2,1,0:T(8,128)(2,1)} %get-tuple-element.100.added_ref, bf16[2,768,1024]{2,1,0:T(8,128)(2,1)} %get-tuple-element.101.early_ref, bf16[768,1024]{1,0:T(8,128)(2,1)} %x_ref.3, f32[768,1024]{1,0:T(8,128)} %get-tuple-element.102.middle_ref, f32[1,1024]{1,0:T(1,128)} %copy-done.20), custom_call_target="tpu_custom_call" | custom-call | tf_op jit(solution)/shard_map/finish_rows/pallas_call | solution.py:1183
  515.2 1.4 weights.1
  516.6 0.4 copy-done.19
  517.1 1.1 copy.74
  518.2 0.8 copy-done.18
  519.0 1.1 copy.75
  (87 shorter events, 1.1 us)
Async XLA Ops:
  7.2 2.4 copy-start.3
  7.2 195.1 %all-gather.3.cloned.1.call-start = ((), (), s32[]{:S(2)}) async-start(), calls=%async_computation | async-start | bytes 5308416 | tf_op jit(solution)/shard_map/all_gather | solution.py:1750
  8.5 2.2 copy-start.28
  8.5 2.3 copy-start.29
  8.5 2.4 copy-start.2
  8.5 3.1 copy-start.23
  10.6 191.7 %all-gather.5.cloned.1.call-start = ((), (), s32[]{:S(2)}) async-start(), calls=%async_computation.1 | async-start | bytes 15925248 | tf_op jit(solution)/shard_map/all_gather | solution.py:1762
  12.2 102.5 %copy-start.26 = (s32[1,2]{1,0:T(1,128)S(1)}, s32[1,2]{1,0:T(1,128)}, u32[]{:S(2)}) copy-start(s32[1,2]{1,0:T(1,128)} %param.27) | copy-start | bytes 28
  114.6 0.8 copy-start.21
  114.6 1.5 copy-start.27
  114.6 2.7 copy-start.30
  114.6 2.7 copy-start.31
  114.6 2.8 copy-start.32
  114.7 2.9 copy-start.33
  114.7 17.1 %collective-permute-start = (s32[1,2]{1,0:T(1,128)S(1)}, s32[1,2]{1,0:T(1,128)S(1)}, u32[]{:S(2)}, u32[]{:S(2)}) collective-permute-start(s32[1,2]{1,0:T(1,128)S(1)} %copy-done.26), channel_id=1, source_target_pairs={{0,4},{4,0},{1,5},{5,1},{2,6},{6,2},{3,7},{7,3},{8,12},{12,8},{9,1... | collective-permute-start | bytes 32 | tf_op jit(solution)/shard_map/ppermute | solution.py:1771
  116.0 15.0 %copy-start.20 = (f32[1,1024]{1,0:T(1,128)}, f32[1,1024]{1,0:T(1,128)S(1)}, u32[]{:S(2)}) copy-start(f32[1,1024]{1,0:T(1,128)S(1)} %slice.50.gain_ref) | copy-start | bytes 12292
  118.3 12.7 %copy-start.24 = (f32[16]{0:T(128)S(1)}, f32[16]{0:T(128)}, u32[]{:S(2)}) copy-start(f32[16]{0:T(128)} %param.40) | copy-start | bytes 196
  118.3 12.8 %copy-start.25 = (f32[16]{0:T(128)S(1)}, f32[16]{0:T(128)}, u32[]{:S(2)}) copy-start(f32[16]{0:T(128)} %param.47) | copy-start | bytes 196
  290.0 94.1 %copy-start.22 = (f32[2,1024]{1,0:T(2,128)S(1)}, f32[2,1024]{1,0:T(2,128)}, u32[]{:S(2)}) copy-start(f32[2,1024]{1,0:T(2,128)} %get-tuple-element.92) | copy-start | bytes 24580
  290.0 95.2 %copy-start = (f32[1024,128]{1,0:T(8,128)S(1)}, f32[1024,128]{1,0:T(8,128)}, u32[]{:S(2)}) copy-start(f32[1024,128]{1,0:T(8,128)} %wd.3) | copy-start | bytes 1572868
  290.0 95.2 %copy-start.1 = (f32[128,1024]{1,0:T(8,128)S(1)}, f32[128,1024]{1,0:T(8,128)}, u32[]{:S(2)}) copy-start(f32[128,1024]{1,0:T(8,128)} %wu.3) | copy-start | bytes 1572868
  290.0 95.2 %copy-start.14 = (f32[2,1024]{1,0:T(2,128)S(1)}, f32[2,1024]{1,0:T(2,128)}, u32[]{:S(2)}) copy-start(f32[2,1024]{1,0:T(2,128)} %pad_maximum_fusion.1.norm_ref) | copy-start | bytes 24580
  290.0 95.2 %copy-start.15 = (f32[256]{0:T(256)S(1)}, f32[256]{0:T(256)}, u32[]{:S(2)}) copy-start(f32[256]{0:T(256)} %select_maximum_fusion.4) | copy-start | bytes 3076
  385.2 71.1 %copy-start.5 = (f32[128,1024]{1,0:T(8,128)S(1)}, f32[128,1024]{1,0:T(8,128)}, u32[]{:S(2)}) copy-start(f32[128,1024]{1,0:T(8,128)} %mu.1) | copy-start | bytes 1572868
  385.3 71.1 %copy-start.6 = (f32[1024,128]{1,0:T(8,128)S(1)}, f32[1024,128]{1,0:T(8,128)}, u32[]{:S(2)}) copy-start(f32[1024,128]{1,0:T(8,128)} %md.1) | copy-start | bytes 1572868
  385.3 71.1 %copy-start.7 = (f32[128,1024]{1,0:T(8,128)S(1)}, f32[128,1024]{1,0:T(8,128)}, u32[]{:S(2)}) copy-start(f32[128,1024]{1,0:T(8,128)} %su.1) | copy-start | bytes 1572868
  385.3 71.1 %copy-start.8 = (f32[3,128,256]{2,1,0:T(8,128)S(1)}, f32[3,128,256]{2,1,0:T(8,128)}, u32[]{:S(2)}) copy-start(f32[3,128,256]{2,1,0:T(8,128)} %mq.1) | copy-start | bytes 1179652
  385.3 71.1 %copy-start.9 = (f32[3,128,256]{2,1,0:T(8,128)S(1)}, f32[3,128,256]{2,1,0:T(8,128)}, u32[]{:S(2)}) copy-start(f32[3,128,256]{2,1,0:T(8,128)} %sq.1) | copy-start | bytes 1179652
  385.3 71.1 %copy-start.10 = (f32[256,128]{1,0:T(8,128)S(1)}, f32[256,128]{1,0:T(8,128)}, u32[]{:S(2)}) copy-start(f32[256,128]{1,0:T(8,128)} %mp.1) | copy-start | bytes 393220
  385.3 71.1 %copy-start.11 = (f32[256,128]{1,0:T(8,128)S(1)}, f32[256,128]{1,0:T(8,128)}, u32[]{:S(2)}) copy-start(f32[256,128]{1,0:T(8,128)} %sp.1) | copy-start | bytes 393220
  455.4 1.0 copy-start.4
  460.9 0.7 copy-start.12
  461.5 0.5 copy-start.17
  471.9 43.3 %copy-start.13 = (f32[256,128]{1,0:T(8,128)S(1)}, f32[256,128]{1,0:T(8,128)}, u32[]{:S(2)}) copy-start(f32[256,128]{1,0:T(8,128)} %copy-done.12) | copy-start | bytes 393220
  471.9 43.3 %copy-start.16 = (f32[1,128]{1,0:T(1,128)S(1)}, f32[1,128]{1,0:T(1,128)}, u32[]{:S(2)}) copy-start(f32[1,128]{1,0:T(1,128)} %reduce_row.1.update_ref) | copy-start | bytes 1540
  515.2 1.8 copy-start.19
  517.1 2.0 copy-start.18
Sparse Core Ops, SparseCore 0:
  10.8 40.0 all-gather.2
  114.8 84.5 all-gather.4
